TPU v7x, 128 devices: a whole 4x4x4 slice. The times are simulated.
128 devices in a mesh: slab: 8 (over y, core), patch: 16 (over x, z).
Axes of the slice: x: 4, y: 4, z: 4, core: 2. Of those that a mesh axis runs over, the one named last changes fastest.
Arguments:
- coarse: float32 [5, 128, 128, 128], P(None, 'slab', 'patch'), may hold values from -1.2 to 7.7, as said below
- fine: float32 [5, 256, 32, 1024], P(None, ('slab', 'patch')), may hold values from -1.2 to 7.7, as said below
- columns: int32 [32, 2], replicated, may hold values from 0 to 5, as said below
- patch_ids: int32 [8, 32], P('slab'), may hold values from 0 to 31, each once within a row
Outputs:
- coarse_out: float32 [5, 128, 128, 128], P(None, 'slab', 'patch')
- fine_out: float32 [5, 256, 32, 1024], P(None, ('slab', 'patch'))
Inputs may be any that keep to these rules, and one draw needn't show every extreme that they name: `coarse`: conserved variables of states with density and pressure between 0.5 and 2 and velocity components between -0.6 and 1.4. `fine`: conserved variables of states with density and pressure between 0.5 and 2 and velocity components between -0.6 and 1.4. `columns`: 32 distinct pairs (gy, gz) with gy below 6 and gz below 6. `patch_ids`: each row is a permutation of the 32 patch numbers of a slab.
All inputs are finite; a program needn't handle non-finite values.
Results may differ from a plain program's by a relative error of at most 0.00005.
Values sent between devices are 32-bit elements; how exact they have to be, the bound alone decides.
A program may use at most 320 MiB of HBM per device.

v0:
```python
import jax
import jax.numpy as jnp
from jax import lax
from jax.sharding import Mesh
from jax.sharding import PartitionSpec as P

P_SIZE = 32
LX = 1
GY = 6
GZ = 6
PYZ = 32
H = 16
NZC = 128
PATCH = ("patch_0", "patch_1")
SLAB_PATCH = ("slab", "patch_0", "patch_1")


heat_ratio = 1.4
fine_rate = 0.1
coarse_rate = 0.05
highest = lax.Precision.HIGHEST


def padded_2(block, sides, width):
    for axis, dim in sides:
        count = lax.axis_size(axis)
        forward = [(i, i + 1) for i in range(count - 1)]
        backward = [(target, source) for source, target in forward]
        low = lax.ppermute(
            lax.slice_in_dim(block, block.shape[dim] - width, None, axis=dim), axis, forward
        )
        high = lax.ppermute(lax.slice_in_dim(block, 0, width, axis=dim), axis, backward)
        block = jnp.concatenate([low, block, high], axis=dim)
    return block


def sent_together(arrays, axis, dim, along):
    widths = [a.shape[along] for a in arrays]
    both = jnp.concatenate(arrays, axis=along)
    result = lax.psum_scatter(both, axis, scatter_dimension=dim, tiled=True)
    return tuple(jnp.split(result, [sum(widths[:k]) for k in range(1, len(widths))], axis=along))


def scatter_axes(shard, axes, dim):
    for axis in axes:
        shard = lax.psum_scatter(shard, axis, scatter_dimension=dim, tiled=True)
    return shard


def extended(shard, sides, width):
    edges = {}
    for axis, dim in sides:
        size, length = (lax.axis_size(axis), shard.shape[dim])
        up = [(i, (i + 1) % size) for i in range(size - 1)]
        last = lax.slice_in_dim(shard, length - width, length, axis=dim)
        initial = lax.slice_in_dim(shard, 0, width, axis=dim)
        edges[dim] = (
            lax.ppermute(last, axis, up),
            lax.ppermute(initial, axis, [(b, a) for a, b in up]),
        )
    done = []
    for _, dim in sides:
        low, high = edges[dim]
        around = [(width, width) if d in done else (0, 0) for d in range(shard.ndim)]
        shard = jnp.concatenate([jnp.pad(low, around), shard, jnp.pad(high, around)], axis=dim)
        done.append(dim)
    return shard


def euler_flux(fields, normal_axis):
    density = fields[0]
    momentum = fields[1:4]
    energy = fields[4]
    velocity = momentum / density
    pressure = (heat_ratio - 1.0) * (energy - 0.5 * jnp.sum(momentum * velocity, axis=0))
    normal_speed = velocity[normal_axis]
    components = [
        momentum[normal_axis],
        momentum[0] * normal_speed,
        momentum[1] * normal_speed,
        momentum[2] * normal_speed,
        (energy + pressure) * normal_speed,
    ]
    components[1 + normal_axis] = components[1 + normal_axis] + pressure
    signal = jnp.abs(normal_speed) + jnp.sqrt(heat_ratio * pressure / density)
    return (jnp.stack(components), signal)


def rusanov(left_side, right_side, normal_axis):
    left_flux, left_signal = euler_flux(left_side, normal_axis)
    right_flux, right_signal = euler_flux(right_side, normal_axis)
    return 0.5 * (left_flux + right_flux) - 0.5 * jnp.maximum(left_signal, right_signal) * (
        right_side - left_side
    )


def advance(fields, ghosts):
    x_low, x_high, z_low, z_high, y_low, y_high = ghosts
    patch_count = fields.shape[1]
    side_cells = fields.shape[2]
    lane_count = side_cells * side_cells
    cube_view = fields.reshape(5, patch_count, side_cells, side_cells, side_cells)
    along_x = jnp.concatenate(
        [
            x_low.reshape(5, patch_count, 1, lane_count),
            fields,
            x_high.reshape(5, patch_count, 1, lane_count),
        ],
        axis=2,
    )
    flux_x = rusanov(along_x[:, :, :-1], along_x[:, :, 1:], 0)
    lane_index = jnp.arange(lane_count, dtype=jnp.int32)
    y_place = lane_index % side_cells
    z_place = lane_index // side_cells
    z_beyond = jnp.where(
        z_place == side_cells - 1,
        jnp.tile(z_high, (1, 1, 1, side_cells)),
        jnp.roll(fields, -side_cells, axis=3),
    )
    z_upper_flux = rusanov(fields, z_beyond, 2)
    z_edge = rusanov(z_low, cube_view[:, :, :, 0], 2)
    z_lower_flux = jnp.where(
        z_place == 0,
        jnp.tile(z_edge, (1, 1, 1, side_cells)),
        jnp.roll(z_upper_flux, side_cells, axis=3),
    )
    y_beyond = jnp.where(
        y_place == side_cells - 1,
        jnp.repeat(y_high, side_cells, axis=3),
        jnp.roll(fields, -1, axis=3),
    )
    y_upper_flux = rusanov(fields, y_beyond, 1)
    y_edge = rusanov(y_low, cube_view[..., 0], 1)
    y_lower_flux = jnp.where(
        y_place == 0, jnp.repeat(y_edge, side_cells, axis=3), jnp.roll(y_upper_flux, 1, axis=3)
    )
    change = (
        flux_x[:, :, 1:]
        - flux_x[:, :, :-1]
        + (z_upper_flux - z_lower_flux)
        + (y_upper_flux - y_lower_flux)
    )
    updated = fields - fine_rate * change
    y_top = y_upper_flux.reshape(5, patch_count, side_cells, side_cells, side_cells)[
        ..., side_cells - 1
    ]
    z_top = z_upper_flux[..., (side_cells - 1) * side_cells :]
    return (updated, (y_edge, y_top, z_edge, z_top))


def pair_mean(face_cells):
    extents = face_cells.shape
    return face_cells.reshape(extents[0], extents[1], extents[2] // 2, 2, extents[3] // 2, 2).mean(
        axis=(3, 5)
    )


def cell_mean(fields):
    extents = fields.shape
    return fields.reshape(
        extents[0], extents[1], extents[2] // 2, 2, extents[3] // 2, 2, extents[4] // 2, 2
    ).mean(axis=(3, 5, 7))


def upsample(face_cells):
    return jnp.repeat(jnp.repeat(face_cells, 2, axis=-2), 2, axis=-1)


def onehot(indices, extent):
    return (indices[:, None] == jnp.arange(extent, dtype=jnp.int32)[None, :]).astype(jnp.float32)


def neighbours(columns, step_y, step_z):
    matches = (columns[None, :, 0] == columns[:, None, 0] + step_y) & (
        columns[None, :, 1] == columns[:, None, 1] + step_z
    )
    present = jnp.any(matches, axis=1)
    partner = jnp.sum(
        jnp.where(matches, jnp.arange(columns.shape[0], dtype=jnp.int32)[None, :], 0), axis=1
    )
    return (present, partner)


def block_targets(column_y, column_z):
    grid_width = GY + 2
    return (
        (column_z + 1) * grid_width + column_y + 1,
        (column_z + 1) * grid_width + column_y,
        (column_z + 1) * grid_width + column_y + 2,
        column_z * grid_width + column_y + 1,
        (column_z + 2) * grid_width + column_y + 1,
    )


def cover_mask(columns):
    centre = block_targets(columns[:, 0], columns[:, 1])[0]
    occupied = jnp.sum(onehot(centre, (GZ + 2) * (GY + 2)), axis=0)
    return jnp.repeat(jnp.repeat(occupied.reshape(GZ + 2, GY + 2), H, axis=0), H, axis=1)


def block_form(slab):
    layer_depth = slab.shape[1] // H
    shaped = slab.reshape(5, layer_depth, H, GZ + 2, H, GY + 2, H).transpose(0, 1, 2, 4, 6, 3, 5)
    return shaped.reshape(5, layer_depth, H, H, H, (GZ + 2) * (GY + 2))


def slab_form(blocks):
    layer_depth = blocks.shape[1]
    shaped = blocks.reshape(5, layer_depth, H, H, H, GZ + 2, GY + 2).transpose(0, 1, 2, 5, 3, 6, 4)
    return shaped.reshape(5, layer_depth * H, (GZ + 2) * H, (GY + 2) * H)


def slot_order(numbers):
    slot_range = jnp.arange(numbers.shape[0], dtype=jnp.int32)
    found = jnp.sum(
        jnp.where(numbers[:, None] == slot_range[None, :], slot_range[:, None], 0), axis=0
    )
    return jnp.clip(found, 0, numbers.shape[0] - 1)


def coarse_faces(slab, layer_index, column_y, column_z):
    blocks = block_form(slab)
    layer_pick = onehot(layer_index, LX)
    centre, below_y, above_y, below_z, above_z = block_targets(column_y, column_z)
    nblocks = blocks.shape[-1]

    def select(portion, target):
        return jnp.einsum(
            "nl,nb,vlxzb->vnxz", layer_pick, onehot(target, nblocks), portion, precision=highest
        )

    return (
        select(blocks[:, :, :, :, H - 1], below_y),
        select(blocks[:, :, :, :, 0], above_y),
        select(blocks[:, :, :, H - 1], below_z),
        select(blocks[:, :, :, 0], above_z),
    )


def coarse_terms(averaged, face_terms, layer_index, column_y, column_z):
    layer_pick = onehot(layer_index, LX)
    centre, below_y, above_y, below_z, above_z = block_targets(column_y, column_z)
    nblocks = (GZ + 2) * (GY + 2)
    first_row = (jnp.arange(H) == 0).astype(jnp.float32)
    last_row = (jnp.arange(H) == H - 1).astype(jnp.float32)

    def spread(values, target):
        return jnp.einsum(
            "nl,nb,vnxz->vlxzb", layer_pick, onehot(target, nblocks), values, precision=highest
        )

    y_lower, y_upper, z_lower, z_upper = face_terms
    totals = jnp.einsum(
        "nl,nb,vnxzy->vlxzyb", layer_pick, onehot(centre, nblocks), averaged, precision=highest
    )
    totals = totals + spread(y_lower, below_y)[:, :, :, :, None, :] * last_row[:, None]
    totals = totals + spread(y_upper, above_y)[:, :, :, :, None, :] * first_row[:, None]
    totals = totals + spread(z_lower, below_z)[:, :, :, None, :, :] * last_row[:, None, None]
    totals = totals + spread(z_upper, above_z)[:, :, :, None, :, :] * first_row[:, None, None]
    return slab_form(totals)


def local(coarse, fine, columns, patch_ids):
    own_count = fine.shape[1]
    row_count = coarse.shape[2]
    patch_rank = lax.axis_index(PATCH)
    slab_rank = lax.axis_index("slab")
    slab_total = lax.axis_size("slab")
    numbers = patch_ids[0]
    own_numbers = lax.dynamic_slice_in_dim(numbers, patch_rank * own_count, own_count)
    inverse = slot_order(numbers)
    cube_fields = fine.reshape(5, own_count, P_SIZE, P_SIZE, P_SIZE)
    own_faces = jnp.stack(
        [
            cube_fields[:, :, 0],
            cube_fields[:, :, P_SIZE - 1],
            cube_fields[:, :, :, 0],
            cube_fields[:, :, :, P_SIZE - 1],
            cube_fields[..., 0],
            cube_fields[..., P_SIZE - 1],
        ]
    )
    slab_faces = lax.all_gather(own_faces, PATCH, axis=2, tiled=True)
    slab_faces = jnp.take(slab_faces, inverse, axis=2)
    edge_faces = jnp.stack([slab_faces[0, :, :PYZ], slab_faces[1, :, -PYZ:]])
    rim_faces = padded_2(edge_faces, (("slab", 0),), 1)
    lower_rim = rim_faces[0]
    upper_rim = rim_faces[3]
    lower_source = jnp.where(slab_rank == 0, slab_faces[0, :, :PYZ], lower_rim)
    upper_source = jnp.where(slab_rank == slab_total - 1, slab_faces[1, :, -PYZ:], upper_rim)
    x_lower_table = jnp.concatenate([lower_source, slab_faces[1, :, :-PYZ]], axis=1)
    x_upper_table = jnp.concatenate([slab_faces[0, :, PYZ:], upper_source], axis=1)
    layer_index = own_numbers // PYZ
    column_index = own_numbers % PYZ
    column_y = columns[column_index, 0]
    column_z = columns[column_index, 1]
    all_layers = numbers // PYZ
    all_y = columns[numbers % PYZ, 0]
    all_z = columns[numbers % PYZ, 1]
    padded = jnp.zeros((5, coarse.shape[1], NZC, coarse.shape[3]), jnp.float32)
    padded = lax.dynamic_update_slice_in_dim(padded, coarse, patch_rank * row_count, 2)
    partial_faces = coarse_faces(padded, all_layers, all_y, all_z)
    injected = sent_together(
        (partial_faces[0], partial_faces[1], partial_faces[2], partial_faces[3]), PATCH, 1, 0
    )

    def blend_faces(face_id, step_y, step_z, coarse_face):
        present, partner = neighbours(columns, step_y, step_z)
        target = layer_index * PYZ + partner[column_index]
        neighbour_face = jnp.take(slab_faces[face_id], target, axis=1)
        keep_mask = present[column_index][None, :, None, None]
        return jnp.where(keep_mask, neighbour_face, upsample(coarse_face))

    ghosts = (
        jnp.take(x_lower_table, own_numbers, axis=1),
        jnp.take(x_upper_table, own_numbers, axis=1),
        blend_faces(3, 0, -1, injected[2]),
        blend_faces(2, 0, 1, injected[3]),
        blend_faces(5, -1, 0, injected[0]),
        blend_faces(4, 1, 0, injected[1]),
    )
    updated, boundary = advance(fine, ghosts)

    def absent_mask(step_y, step_z):
        gaps = 1.0 - neighbours(columns, step_y, step_z)[0].astype(jnp.float32)
        return gaps[column_index][None, :, None, None]

    y_lower = -coarse_rate * pair_mean(boundary[0]) * absent_mask(-1, 0)
    y_upper = coarse_rate * pair_mean(boundary[1]) * absent_mask(1, 0)
    z_lower = -coarse_rate * pair_mean(boundary[2]) * absent_mask(0, -1)
    z_upper = coarse_rate * pair_mean(boundary[3]) * absent_mask(0, 1)
    averaged = cell_mean(updated.reshape(5, own_count, P_SIZE, P_SIZE, P_SIZE))
    placed = coarse_terms(
        averaged, (y_lower, y_upper, z_lower, z_upper), layer_index, column_y, column_z
    )
    contrib = scatter_axes(placed, PATCH, 2)
    margin_cells = extended(coarse, (("slab", 1), (PATCH, 2)), 1)
    before_x = jnp.where(slab_rank == 0, coarse[:, :1], margin_cells[:, :1, 1:-1])
    after_x = jnp.where(slab_rank == slab_total - 1, coarse[:, -1:], margin_cells[:, -1:, 1:-1])
    along_x = jnp.concatenate([before_x, coarse, after_x], axis=1)
    before_z = jnp.where(patch_rank == 0, coarse[:, :, :1], margin_cells[:, 1:-1, :1])
    after_z = jnp.where(
        patch_rank == lax.axis_size(PATCH) - 1, coarse[:, :, -1:], margin_cells[:, 1:-1, -1:]
    )
    along_z = jnp.concatenate([before_z, coarse, after_z], axis=2)
    along_y = jnp.concatenate([coarse[..., :1], coarse, coarse[..., -1:]], axis=3)
    covered = cover_mask(columns)
    own_cover = lax.dynamic_slice_in_dim(covered, patch_rank * row_count, row_count, 0)
    cover_z = lax.dynamic_slice_in_dim(
        jnp.pad(covered, ((1, 1), (0, 0))), patch_rank * row_count, row_count + 2, 0
    )
    cover_y = jnp.pad(own_cover, ((0, 0), (1, 1)))
    flux_x = rusanov(along_x[:, :-1], along_x[:, 1:], 0) * (1.0 - own_cover)
    flux_z = rusanov(along_z[:, :, :-1], along_z[:, :, 1:], 2) * (
        (1.0 - cover_z[:-1]) * (1.0 - cover_z[1:])
    )
    flux_y = rusanov(along_y[..., :-1], along_y[..., 1:], 1) * (
        (1.0 - cover_y[:, :-1]) * (1.0 - cover_y[:, 1:])
    )
    change = (
        flux_x[:, 1:]
        - flux_x[:, :-1]
        + (flux_z[:, :, 1:] - flux_z[:, :, :-1])
        + (flux_y[..., 1:] - flux_y[..., :-1])
    )
    provisional = coarse - coarse_rate * change
    coarse_out = jnp.where(own_cover > 0, contrib, provisional + contrib)
    return (coarse_out, updated)


def solution(mesh):
    finer = Mesh(mesh.devices.reshape(mesh.shape["slab"], 4, 4), ("slab", "patch_0", "patch_1"))
    return jax.shard_map(
        local,
        mesh=finer,
        in_specs=(
            P(None, "slab", PATCH, None),
            P(None, SLAB_PATCH, None, None),
            P(),
            P("slab", None),
        ),
        out_specs=(P(None, "slab", PATCH, None), P(None, SLAB_PATCH, None, None)),
        check_vma=False,
    )
```

profile of v0, /device:TPU:2, one launch (start us, length us, event | category | flops | bytes accessed | tf_op | source)
XLA Modules:
  0.0 714.3 jit_solution(11980178886842121223)
XLA Ops:
  15.0 9.7 %fusion.235 = (f32[5,2,32,32,1]{4,3,2,1,0:T(8,128)}, f32[5,2,32,32,1]{4,3,2,1,0:T(8,128)}) fusion(f32[5,2,32,32,32]{4,3,2,1,0:T(8,128)} %reshape.745), kind=kLoop, calls=%fused_computation.662 | loop fusion | bytes 163840 | tf_op jit(solution)/shard_map/slice | solution.py:280
  37.2 24.0 %reshape.748 = f32[5,1,16,8,16,8,16]{6,5,4,3,2,0,1:T(8,128)} reshape(f32[5,16,128,128]{3,2,1,0:T(8,128)} %constant_dynamic-update-slice_fusion.58) | data formatting | bytes 10485760 | tf_op jit(solution)/shard_map/reshape | solution.py:203
  61.2 29.7 %copy_bitcast_fusion = f32[5,1,16,16,16,64]{4,5,3,2,0,1:T(8,128)} fusion(f32[5,1,16,8,16,8,16]{6,5,4,3,2,0,1:T(8,128)} %reshape.748), kind=kLoop, calls=%fused_computation.23 | loop fusion | bytes 10485760 | tf_op jit(solution)/shard_map/reshape | solution.py:204
  92.5 57.1 %fusion.232 = (f32[5,1,16,16,1,64]{4,5,3,2,0,1:T(8,128)}, f32[5,1,16,16,1,64]{4,5,3,2,0,1:T(8,128)}) fusion(f32[5,1,16,16,16,64]{4,5,3,2,0,1:T(8,128)} %copy_bitcast_fusion), kind=kLoop, calls=%fused_computation.659 | loop fusion | bytes 1310720 | tf_op jit(solution)/shard_map/slice | solution.py:233
  149.6 22.6 %copy.492 = f32[5,1,16,16,1,64]{5,3,2,0,4,1:T(8,128)S(1)} copy(f32[5,1,16,16,1,64]{4,5,3,2,0,1:T(8,128)} %get-tuple-element.59) | data formatting | bytes 655360
  172.3 22.9 %copy.491 = f32[5,1,16,16,1,64]{5,3,2,0,4,1:T(8,128)S(1)} copy(f32[5,1,16,16,1,64]{4,5,3,2,0,1:T(8,128)} %get-tuple-element.58) | data formatting | bytes 655360
  196.6 6.0 fusion.16
  202.6 6.0 fusion.15
  264.3 13.6 %gather_fusion.2 = f32[32,6,5,32,32]{4,3,2,1,0:T(8,128)} fusion(f32[6,5,32,32,32]{4,3,1,2,0:T(8,128)} %all-gather.2.cloned.1.call-done, s32[1024]{0:T(1024)S(1)} %pad_clamp_fusion.6), kind=kCustom, calls=%fused_computation.8 | custom fusion | bytes 7864448 | tf_op jit(solution)/shard_map/jit(_take)/gather | solution.py:284
  277.9 6.9 copy_bitcast_fusion.1
  306.8 11.8 %select_bitcast_fusion.1 = (f32[5,32,32,32]{3,2,1,0:T(8,128)}, f32[5,32,32,32]{3,2,1,0:T(8,128)}, f32[5,32,32,32]{3,2,1,0:T(8,128)}, f32[5,32,32,32]{3,2,1,0:T(8...) fusion(f32[1,5,32,32,32]{4,3,2,1,0:T(8,128)} %collective-permute-done, pred[]{:T(512)S(6)} %eq.190, ...), kind=kLoop, calls=%fused_computation.47 | loop fusion | flops 327680 | bytes 9175042 | tf_op jit(solution)/shard_map/jit(_where)/select_n | solution.py:289
  374.6 6.3 slice.908
  380.9 14.6 %copy.510 = f32[5,2,32,32,1]{0,3,2,1,4:T(8,128)} copy(f32[5,2,32,32,1]{4,3,2,1,0:T(8,128)} %slice.908) | data formatting | bytes 81920
  416.4 5.6 tile.21
  439.1 16.8 %copy.454 = f32[5,2,32,1024]{0,3,2,1:T(8,128)} copy(f32[5,2,32,1024]{3,2,1,0:T(8,128)S(1)} %fusion.11) | data formatting | bytes 2621440 | tf_op jit(solution)/shard_map/sub | solution.py:143
  455.9 25.7 %reduce_sum.253 = f32[5,2,16,16,16]{0,4,3,2,1:T(8,128)} reduce(f32[5,2,16,2,16,2,16,2]{0,7,6,5,4,3,2,1:T(2,128)} %bitcast.654, f32[]{:T(128)} %constant.196.clone.1), dimensions={3,5,7}, to_apply=%region_20.22 | reduce | flops 286720 | bytes 1474564 | tf_op jit(solution)/shard_map/reduce_sum | solution.py:162
  481.6 5.7 copy.455
  493.7 23.0 %fusion.2 = f32[5,1,16,16,16,64]{5,4,3,2,0,1:T(8,128)} fusion(f32[16]{0:T(128)S(1)} %copy-done.53, f32[5,16,16,64]{3,2,1,0:T(8,128)S(1)} %convolution_bitcast_fusion, f32[16]{0:T(128)S(1)} %copy-done.54, f32[5,16,16,64]{3,2,1,0:T(8,128)S(1)} %convolution_bitcast_fusion.1, f32[5,16,16,64]{3,2,1,0:T(8,128)S(1)} %convolution_bitcast_fusion.2, ...), kind=kOutput, calls=%fused_computation.28 | convolution fusion | flops 41943296 | bytes 6717584 | tf_op jit(solution)/shard_map/nl,nb,vnxzy->vlxzyb/dot_general | solution.py:253
  516.7 24.4 %copy.469 = f32[5,1,16,16,16,64]{4,5,3,2,0,1:T(8,128)} copy(f32[5,1,16,16,16,64]{5,4,3,2,0,1:T(8,128)} %fusion.2) | data formatting | bytes 10485760 | tf_op jit(solution)/shard_map/add | solution.py:259
  541.1 29.1 %copy.470 = f32[5,1,16,8,16,8,16]{6,5,4,3,2,0,1:T(8,128)} copy(f32[5,1,16,8,16,8,16]{6,5,3,4,2,0,1:T(8,128)} %bitcast.653) | data formatting | bytes 10485760 | tf_op jit(solution)/shard_map/transpose | solution.py:209
  570.1 26.8 %reshape.769 = f32[5,16,128,128]{3,2,1,0:T(8,128)} reshape(f32[5,1,16,8,16,8,16]{6,5,4,3,2,0,1:T(8,128)} %copy.470) | data formatting | bytes 10485760 | tf_op jit(solution)/shard_map/reshape | solution.py:210
  607.3 24.4 %collective-permute-start.2 = (f32[5,1,8,128]{3,2,1,0:T(8,128)S(1)}, f32[5,1,8,128]{3,2,1,0:T(8,128)S(1)}, u32[]{:S(2)}, u32[]{:S(2)}) collective-permute-start(f32[5,1,8,128]{3,2,1,0:T(8,128)S(1)} %get-tuple-element.135), channel_id=1, source_target_pairs={{0,16},{16,32},{32,48},{48,64},{64,80},{80,96},{96,112},{1,17},{17... | collective-permute-start | bytes 61448 | tf_op jit(solution)/shard_map/ppermute | solution.py:58
  635.4 41.9 %reduce-scatter.6.cloned.1.call-done = f32[5,16,32,128]{3,2,1,0:T(8,128)} async-done(((f32[5,16,128,128]{3,2,1,0:T(8,128)}), f32[5,16,32,128]{3,2,1,0:T(8,128)}) %reduce-scatter.6.cloned.1.call-update) | async-done | bytes 1310736 | tf_op jit(solution)/shard_map/reduce_scatter | solution.py:46
  678.5 26.9 %reduce-scatter.8.cloned.1.call-done = f32[5,16,8,128]{3,2,1,0:T(8,128)} async-done(((f32[5,16,32,128]{3,2,1,0:T(8,128)}), f32[5,16,8,128]{3,2,1,0:T(8,128)}) %reduce-scatter.8.cloned.1.call-update) | async-done | bytes 327696 | tf_op jit(solution)/shard_map/reduce_scatter | solution.py:46
  (381 shorter events, 217.2 us)
Async XLA Ops:
  7.2 257.1 %all-gather.2.cloned.1.call-start = ((), (), s32[]{:S(2)}) async-start(), calls=%async_computation.3 | async-start | bytes 16711680 | tf_op jit(solution)/shard_map/all_gather | solution.py:283
  15.0 17.3 %copy-start.20 = (f32[5,2,32,1,32]{4,3,2,1,0:T(1,128)}, f32[5,2,32,1,32]{4,3,2,1,0:T(1,128)S(1)}, u32[]{:S(2)}) copy-start(f32[5,2,32,1,32]{4,3,2,1,0:T(1,128)S(1)} %get-tuple-element.81) | copy-start | bytes 122884
  33.3 269.0 %reduce-scatter.4.cloned.1.call-start = ((), (), s32[]{:S(2)}) async-start(), calls=%async_computation.4 | async-start | bytes 4456448 | tf_op jit(solution)/shard_map/reduce_scatter | solution.py:40
  61.2 29.7 %copy-start.37 = (s32[1,32]{1,0:T(1,128)S(1)}, s32[1,32]{1,0:T(1,128)}, u32[]{:S(2)}) copy-start(s32[1,32]{1,0:T(1,128)} %param.9) | copy-start | bytes 388
  61.2 29.7 %copy-start = (s32[32,2]{0,1:T(2,128)S(1)}, s32[32,2]{0,1:T(2,128)}, u32[]{:S(2)}) copy-start(s32[32,2]{0,1:T(2,128)} %param.8) | copy-start | bytes 772
  213.9 463.4 %reduce-scatter.6.cloned.1.call-start = ((), (), s32[]{:S(2)}) async-start(), calls=%async_computation.5 | async-start | bytes 6553600 | tf_op jit(solution)/shard_map/reduce_scatter | solution.py:46
  243.2 5.8 copy-start.40
  264.3 13.6 %copy-start.49 = (pred[32]{0:T(512)(128)(4,1)S(1)}, pred[32]{0:T(512)(128)(4,1)}, u32[]{:S(2)}) copy-start(pred[32]{0:T(512)(128)(4,1)} %compare_and_fusion.9) | copy-start | bytes 100
  284.8 7.0 copy-start.5
  291.8 14.9 %collective-permute-start = (f32[1,5,32,32,32]{4,3,2,1,0:T(8,128)}, f32[1,5,32,32,32]{4,3,2,1,0:T(8,128)}, u32[]{:S(2)}, u32[]{:S(2)}) collective-permute-start(f32[1,5,32,32,32]{4,3,2,1,0:T(8,128)} %get-tuple-element.66), channel_id=1, source_target_pairs={{0,16},{16,32},{32,48},{48,64},{64,80},{80,96},{96,112},{1,17},{17... | collective-permute-start | bytes 1966088 | tf_op jit(solution)/shard_map/ppermute | solution.py:29
  294.8 12.0 %collective-permute-start.1 = (f32[1,5,32,32,32]{4,3,2,1,0:T(8,128)}, f32[1,5,32,32,32]{4,3,2,1,0:T(8,128)}, u32[]{:S(2)}, u32[]{:S(2)}) collective-permute-start(f32[1,5,32,32,32]{4,3,2,1,0:T(8,128)} %get-tuple-element.67), channel_id=1, source_target_pairs={{16,0},{32,16},{48,32},{64,48},{80,64},{96,80},{112,96},{17,1},{33... | collective-permute-start | bytes 1966088 | tf_op jit(solution)/shard_map/ppermute | solution.py:32
  306.7 14.4 %copy-start.34 = (f32[5,2,32,32]{3,2,0,1:T(8,128)S(1)}, f32[5,2,32,32]{3,2,0,1:T(8,128)}, u32[]{:S(2)}) copy-start(f32[5,2,32,32]{3,2,0,1:T(8,128)} %constant_dynamic-update-slice_fusion.15) | copy-start | bytes 122884
  344.7 5.5 slice-start.1
  344.7 5.5 copy-start.12
  397.6 9.9 %copy-start.42 = (pred[2]{0:T(512)(128)(4,1)S(1)}, pred[2]{0:T(512)(128)(4,1)}, u32[]{:S(2)}) copy-start(pred[2]{0:T(512)(128)(4,1)} %get-tuple-element.31) | copy-start | bytes 10
  439.1 16.8 %copy-start.10 = (f32[5,2,32,1024]{3,2,1,0:T(8,128)}, f32[5,2,32,1024]{3,2,1,0:T(8,128)S(1)}, u32[]{:S(2)}) copy-start(f32[5,2,32,1024]{3,2,1,0:T(8,128)S(1)} %fusion.11) | copy-start | bytes 3932164
  488.4 5.3 copy-start.53
  488.4 5.3 copy-start.54
  596.9 36.0 %copy-start.50 = (s32[32]{0:T(128)S(1)}, s32[32]{0:T(128)}, u32[]{:S(2)}) copy-start(s32[32]{0:T(128)} %get-tuple-element.175) | copy-start | bytes 388
  596.9 108.5 %reduce-scatter.8.cloned.1.call-start = ((), (), s32[]{:S(2)}) async-start(), calls=%async_computation.6 | async-start | bytes 1638400 | tf_op jit(solution)/shard_map/reduce_scatter | solution.py:46
  597.9 79.6 %collective-permute-start.4 = (f32[5,16,1,128]{3,2,1,0:T(1,128)S(1)}, f32[5,16,1,128]{3,2,1,0:T(1,128)S(1)}, u32[]{:S(2)}, u32[]{:S(2)}) collective-permute-start(f32[5,16,1,128]{3,2,1,0:T(1,128)S(1)} %get-tuple-element.145), channel_id=1, source_target_pairs={{0,1},{1,2},{2,3},{3,4},{4,5},{5,6},{6,7},{7,8},{8,9},{9,10},{10,1... | collective-permute-start | bytes 122888 | tf_op jit(solution)/shard_map/ppermute | solution.py:58
  602.6 74.9 %collective-permute-start.5 = (f32[5,16,1,128]{3,2,1,0:T(1,128)S(1)}, f32[5,16,1,128]{3,2,1,0:T(1,128)S(1)}, u32[]{:S(2)}, u32[]{:S(2)}) collective-permute-start(f32[5,16,1,128]{3,2,1,0:T(1,128)S(1)} %get-tuple-element.146), channel_id=1, source_target_pairs={{1,0},{2,1},{3,2},{4,3},{5,4},{6,5},{7,6},{8,7},{9,8},{10,9},{11,1... | collective-permute-start | bytes 122888 | tf_op jit(solution)/shard_map/ppermute | solution.py:59
  607.3 27.9 %collective-permute-start.2 = (f32[5,1,8,128]{3,2,1,0:T(8,128)S(1)}, f32[5,1,8,128]{3,2,1,0:T(8,128)S(1)}, u32[]{:S(2)}, u32[]{:S(2)}) collective-permute-start(f32[5,1,8,128]{3,2,1,0:T(8,128)S(1)} %get-tuple-element.135), channel_id=1, source_target_pairs={{0,16},{16,32},{32,48},{48,64},{64,80},{80,96},{96,112},{1,17},{17... | collective-permute-start | bytes 61448 | tf_op jit(solution)/shard_map/ppermute | solution.py:58
  631.6 3.5 collective-permute-start.3
  (43 other events, 112.5 us)
Sparse Core Ops, SparseCore 0:
  33.5 108.4 all-gather.1
  214.0 81.0 reduce-scatter.3
  597.0 80.1 reduce-scatter.5
  679.7 25.6 reduce-scatter.7
where the time goes:
time: 725 us; the launch traced here: 714 us
  local copies, waits for them, and re-layouts  454 us (63%)
  other arithmetic  95.2 us (13%)
  waiting for transfers between devices  68.8 us (9%)
  matrix products  41.5 us (6%)
  starting transfers between devices  39.4 us (5%)
  between operations  15.8 us (2%)
    unnamed x129, local copies, waits for them, and re-layouts  90.3 us
    reduce_scatter x2, waiting for transfers between devices, scatter_axes(): shard = lax.psum_scatter(shard, axis, scatter_dimension=dim, tiled=True)  68.8 us
    slice x1, local copies, waits for them, and re-layouts, coarse_faces(): blocks[:, :, :, :, H - 1]  57.1 us
    reshape x1, local copies, waits for them, and re-layouts, block_form(): return shaped.reshape(5, layer_depth, H, H, H, (GZ + 2) * (GY + 2))  29.7 us
    ppermute x2, starting transfers between devices, extended(): lax.ppermute(last, axis, up)  29.1 us
    transpose x1, local copies, waits for them, and re-layouts, slab_form(): blocks.reshape(5, layer_depth, H, H, H, GZ + 2, GY + 2)  29.1 us
    reshape x1, local copies, waits for them, and re-layouts, slab_form(): return shaped.reshape(5, layer_depth * H, (GZ + 2) * H, (GY + 2) * H)  26.8 us
    reduce_sum x1, other arithmetic, cell_mean(): return fields.reshape(extents[0], extents[1], extents[2] // 2, 2, extents...  25.7 us
  transfers between devices with their start and end apart: 10, of which 2 were waited for; matrix products, arithmetic and copies ran while one was open for 38% of the time, Pallas kernels for 0%

commit v1 on v0

v1 whole, which is shorter than its diff:
```python
import jax
import jax.numpy as jnp
from jax import lax
from jax.experimental import pallas as pl
from jax.experimental.pallas import tpu as pltpu
from jax.sharding import PartitionSpec as P

F32 = jnp.float32
BF16 = jnp.bfloat16
I32 = jnp.int32
MESH = pl.DeviceIdType.MESH
NS = 8
NP = 16
GOFF = 16


def iota(shape, dim):
    return lax.broadcasted_iota(I32, shape, dim)


def dot3(x, m):
    hi = x.astype(BF16)
    r = x - hi.astype(F32)
    mid = r.astype(BF16)
    lo = (r - mid.astype(F32)).astype(BF16)
    d = lambda a: jnp.dot(a, m, preferred_element_type=F32)
    return d(hi) + (d(mid) + d(lo))


def ones_where(c):
    return jnp.where(c, 1.0, 0.0).astype(BF16)


def state(q):
    r = 1.0 / q[0]
    p = 0.4 * (q[4] - 0.5 * ((q[1] * q[1] + q[2] * q[2] + q[3] * q[3]) * r))
    c = jnp.sqrt(1.4 * p * r)
    return r, p, c


def flux(q, s, d):
    r, p, c = s
    u = q[1 + d] * r
    f = [q[1 + d], q[1] * u, q[2] * u, q[3] * u, (q[4] + p) * u]
    f[1 + d] = f[1 + d] + p
    return f, jnp.abs(u) + c


def rusanov(ql, fl, al, qr, fr, ar):
    a = 0.5 * jnp.maximum(al, ar)
    return [0.5 * (fl[v] + fr[v]) - a * (qr[v] - ql[v]) for v in range(5)]


def pack_kernel(fine, coarse, ids, cols, yzp, xf, cp, rz, cx, tab, grid, ct):
    rank = lax.axis_index("patch")
    half = lax.rem(rank, 2)
    for i in range(96):
        grid[0, i] = jnp.int32(-1)

    def place(s, _):
        n = ids[0, s]
        gy = cols[n, 0]
        gz = cols[n, 1]
        tab[8, s] = gy
        tab[9, s] = gz
        grid[0, gy + 8 * gz + GOFF] = s
        return 0

    lax.fori_loop(0, 32, place, 0)

    def look(s, _):
        code = tab[8, s] + 8 * tab[9, s] + GOFF
        for g, step in enumerate((-1, 1, -8, 8)):
            q = grid[0, code + step]
            t = jnp.maximum(q, 0)
            tab[g, s] = (t >> 3) * 2 + (t & 1)
            tab[4 + g, s] = jnp.where(q < 0, -1, (t >> 1) & 3)
        return 0

    lax.fori_loop(0, 32, look, 0)
    k = iota((1024, 128), 0)
    c = iota((1024, 128), 1)
    g = c // 32
    i = lax.rem(c, 32)
    want = jnp.where(g == 0, 32 * i + 31, jnp.where(g == 1, 32 * i, jnp.where(g == 2, 992 + i, i)))
    sel = ones_where(k == want)
    for v in range(5):
        for p in range(2):
            yzp[p, v] = dot3(fine[v, p], sel)
    for d, row in ((0, 0), (1, 31)):
        for p in range(2):
            for v in range(5):
                for j in range(8):
                    xf[d, p * 5 + v, j : j + 1, :] = fine[v, p, row : row + 1, 128 * j : 128 * j + 128]
        sub = iota((8, 128), 0)
        tag = jnp.where(sub == 0, ids[0, 2 * rank], ids[0, 2 * rank + 1])
        xf[d, 10] = tag.astype(F32)
    for v in range(5):
        for z in range(8):
            ct[z, 16 * v : 16 * v + 16, :] = coarse[v, :, z, :]
    y = iota((128, 128), 0)
    k = iota((128, 128), 1) // 8
    plane = jnp.where(k < 6, 16 * (k + 1) - 1, jnp.where(k < 12, 16 * (k - 4), -1))
    sel = ones_where(y == plane)
    lane8 = lax.rem(iota((80, 128), 1), 8)
    acc = jnp.zeros((80, 128), F32)
    for z in range(8):
        acc = jnp.where(lane8 == z, dot3(ct[z], sel), acc)
    first = ct[0]
    last = ct[7]
    own = jnp.where(half == 0, first, last)
    for v in range(5):
        cut = slice(16 * v, 16 * v + 16)
        cp[v, 0] = acc[cut]
        cp[v, 1] = own[cut]
        rz[0, v] = first[cut]
        rz[1, v] = last[cut]
        cx[0, v] = coarse[v, 0]
        cx[1, v] = coarse[v, 15]


def ghost_kernel(yzp, xf, cp, cx, tab, ids, oyz, ox, oc, ocx, gx, bx, cz, syz, sx, sc, ss, rs, ls):
    s = lax.axis_index("slab")
    me = lax.axis_index("patch")
    x = me // 4
    z = lax.rem(me, 4)
    up = lax.rem(s + 1, NS)
    down = lax.rem(s + NS - 1, NS)
    xp = [lax.rem(x + d, 4) for d in range(4)]
    zp = [lax.rem(z + d, 4) for d in range(4)]
    barrier = pltpu.get_barrier_semaphore()
    for d in range(1, 4):
        pl.semaphore_signal(barrier, inc=1, device_id=(s, xp[d] * 4 + z), device_id_type=MESH)
        pl.semaphore_signal(barrier, inc=1, device_id=(s, x * 4 + zp[d]), device_id_type=MESH)
    for d in range(4):
        pl.semaphore_signal(barrier, inc=1, device_id=(up, x * 4 + zp[d]), device_id_type=MESH)
        pl.semaphore_signal(barrier, inc=1, device_id=(down, x * 4 + zp[d]), device_id_type=MESH)
    pl.semaphore_wait(barrier, 14)

    def send(k, src, dst, dev):
        c = pltpu.make_async_remote_copy(
            src_ref=src, dst_ref=dst, send_sem=ss.at[k], recv_sem=rs.at[k],
            device_id=dev, device_id_type=MESH,
        )
        c.start()
        return c

    one = []
    k = 0
    for d in range(1, 4):
        one.append(send(k, yzp, gx.at[pl.ds(2 * x, 2)], (s, xp[d] * 4 + z)))
        k += 1
    for d in range(4):
        one.append(send(k, xf.at[0], bx.at[1, z], (down, x * 4 + zp[d])))
        one.append(send(k + 1, xf.at[1], bx.at[0, z], (up, x * 4 + zp[d])))
        k += 2
    for d in range(1, 4):
        one.append(send(k, cp, cz.at[z], (s, x * 4 + zp[d])))
        k += 1
    one.append(send(k, cx.at[0], ocx.at[1], (down, me)))
    one.append(send(k + 1, cx.at[1], ocx.at[0], (up, me)))
    k += 2
    l0 = pltpu.make_async_copy(yzp, gx.at[pl.ds(2 * x, 2)], ls.at[0])
    l1 = pltpu.make_async_copy(cp, cz.at[z], ls.at[1])
    l0.start()
    l1.start()
    l0.wait()
    l1.wait()
    for c in one:
        c.wait()
    two = []
    lane = iota((5, 32, 128), 2) // 32
    for d in (1, 2, 3, 0):
        for p in range(2):
            slot = 2 * (x * 4 + zp[d]) + p
            got = [gx[tab[g, slot]] for g in range(4)]
            val = jnp.where(lane == 0, got[0], jnp.where(lane == 1, got[1], jnp.where(lane == 2, got[2], got[3])))
            if d:
                syz[d - 1, p] = val
            else:
                oyz[z, p] = val
        if d:
            two.append(send(k, syz.at[d - 1], oyz.at[z], (s, x * 4 + zp[d])))
            k += 1
    lane = iota((80, 128), 1)
    for d in (1, 2, 3, 0):
        for p in range(2):
            slot = 2 * (xp[d] * 4 + z) + p
            n = ids[0, slot].astype(F32)
            for way in range(2):
                acc = jnp.zeros((5, 8, 128), F32)
                for j in range(4):
                    for t in range(2):
                        hit = bx[way, j, 10, t : t + 1, :] == n
                        acc = jnp.where(hit[None], bx[way, j, 5 * t : 5 * t + 5], acc)
                if d:
                    sx[d - 1, p, way] = acc
                else:
                    ox[x, p, way] = acc
            gy = tab[8, slot]
            gz = tab[9, slot]
            a = 2 * ((gz + 1) & 1)
            b = 2 * (gz & 1)
            y0 = cz[a, :, 0].reshape(80, 128)
            y1 = cz[a + 1, :, 0].reshape(80, 128)
            z0 = cz[b + 1, :, 1].reshape(80, 128)
            z1 = cz[b, :, 1].reshape(80, 128)
            r0 = pltpu.roll(y0, (128 - 8 * gy) & 127, 1)
            r1 = pltpu.roll(y1, (136 - 8 * gy) & 127, 1)
            r2 = pltpu.roll(z0, (176 - 16 * gy) & 127, 1)
            r3 = pltpu.roll(z1, (192 - 16 * gy) & 127, 1)
            val = jnp.where(lane < 64, jnp.where((lane & 8) == 0, r0, r1), jnp.where(lane < 80, r2, r3))
            val = val.reshape(5, 16, 128)
            if d:
                sc[d - 1, p] = val
            else:
                oc[x, p] = val
        if d:
            two.append(send(k, sx.at[d - 1], ox.at[x], (s, xp[d] * 4 + z)))
            two.append(send(k + 1, sc.at[d - 1], oc.at[x], (s, xp[d] * 4 + z)))
            k += 2
    for c in two:
        c.wait()


def fine_kernel(fine, oyz, ox, oc, tab, out, av, ext, ghost, chg, fy, fz, xs, tmp):
    s = lax.axis_index("slab")
    me = lax.axis_index("patch")
    lane = iota((80, 128), 1)
    src = iota((128, 128), 0)
    dst = iota((128, 128), 1)
    g = dst // 32
    i = lax.rem(dst, 32) // 2
    base = jnp.where(g == 0, 0, jnp.where(g == 1, 48, jnp.where(g == 2, 64, 80)))
    spread = ones_where(src == base + i)
    src = iota((128, 1024), 0)
    dst = iota((128, 1024), 1)
    g = src // 32
    expand = ones_where(
        ((g == 0) & (dst == 32 * lax.rem(src, 32))) | ((g == 1) & (dst == 32 * lax.rem(src, 32) + 31))
    )
    src = iota((1024, 256), 0)
    dst = iota((1024, 256), 1)
    pair = ones_where((src // 64 == dst // 16) & (lax.rem(src, 32) // 2 == lax.rem(dst, 16)))
    src = iota((1024, 128), 0)
    dst = iota((1024, 128), 1)
    zz = (dst // 32) * 8 + lax.rem(dst, 8)
    side = lax.rem(dst, 32) // 8
    ypair = ones_where(
        (dst < 64) & (src // 64 == zz)
        & (((side == 0) & (lax.rem(src, 32) == 0)) | ((side == 1) & (lax.rem(src, 32) == 31)))
    )
    src = iota((128, 128), 0)
    dst = iota((128, 128), 1)
    zpair = ones_where(
        ((dst >= 48) & (dst < 64) & (src // 2 == dst - 48))
        | ((dst >= 16) & (dst < 32) & (src >= 96) & ((src - 96) // 2 == dst - 16))
    )
    l1 = iota((1, 128), 1)
    low = (lax.rem(l1, 32) < 8) | ((l1 >= 48) & (l1 < 64))
    coef = jnp.where(low, -0.05, 0.05).astype(F32)
    lg = iota((5, 32, 128), 2) // 32

    for p in range(2):
        slot = 2 * me + p
        gz = tab[9, slot]
        cy = oc[(gz + 1) >> 1, p].reshape(80, 128)
        cl = oc[gz >> 1, p].reshape(80, 128)
        ch = oc[(gz + 2) >> 1, p].reshape(80, 128)
        cg = jnp.where(lane < 64, cy, jnp.where(lane < 80, cl, ch))
        tmp[0:80, 0:128] = dot3(cg, spread)
        for v in range(5):
            for r in range(16):
                ghost[v, 2 * r : 2 * r + 2, :] = jnp.broadcast_to(tmp[16 * v + r : 16 * v + r + 1, 0:128], (2, 128))
        val = ghost[...]
        for g in range(4):
            q = tab[4 + g, slot]
            near = oyz[jnp.maximum(q, 0), p]
            val = jnp.where((lg == g) & (q >= 0), near, val)
        ghost[...] = val
        for way in range(2):
            edge = (s == 0) if way == 0 else (s == NS - 1)
            xs[...] = (ox[0, p, way] + ox[1, p, way]) + (ox[2, p, way] + ox[3, p, way])
            row = 7 if way == 0 else 40
            mine = 0 if way == 0 else 31
            for v in range(5):
                for j in range(8):
                    cut = slice(128 * j, 128 * j + 128)
                    ext[v, row : row + 1, cut] = jnp.where(edge, fine[v, p, mine : mine + 1, cut], xs[v, j : j + 1, :])
        for v in range(5):
            ext[v, 8:40, :] = fine[v, p]

        def along_x(j, _):
            cut = pl.ds(pl.multiple_of(128 * j, 128), 128)
            q = [ext[v, :, cut] for v in range(5)]
            f, a = flux(q, state(q), 0)
            nxt = lambda t: pltpu.roll(t, 47, 0)
            up = rusanov(q, f, a, [nxt(t) for t in q], [nxt(t) for t in f], nxt(a))
            for v in range(5):
                chg[v, :, cut] = (up[v] - pltpu.roll(up[v], 1, 0))[8:40]
            return 0

        lax.fori_loop(0, 8, along_x, 0)

        def rows(c, _):
            cut = pl.ds(pl.multiple_of(8 * c, 8), 8)
            q = [fine[v, p, cut, :] for v in range(5)]
            gh = [ghost[v, cut, :] for v in range(5)]
            gr = [pltpu.roll(t, 32, 1) for t in gh]
            qe = [jnp.concatenate([gr[v], q[v], gr[v]], axis=1) for v in range(5)]
            f, a = flux(qe, state(qe), 2)
            nxt = lambda t: pltpu.roll(t, 1280 - 32, 1)
            up = rusanov(qe, f, a, [nxt(t) for t in qe], [nxt(t) for t in f], nxt(a))
            lo = [pltpu.roll(t, 32, 1) for t in up]
            l8 = iota((8, 128), 1)
            for v in range(5):
                fz[v, cut, :] = jnp.where(l8 < 32, lo[v][:, 128:256], up[v][:, 1024:1152])
            change = [chg[v, cut, :] + (up[v] - lo[v])[:, 128:1152] for v in range(5)]
            eg = [dot3(t, expand) for t in gh]
            y = iota((8, 1024), 1) & 31
            qr = [jnp.where(y == 31, eg[v], pltpu.roll(q[v], 1023, 1)) for v in range(5)]
            ql = [jnp.where(y == 0, eg[v], pltpu.roll(q[v], 1, 1)) for v in range(5)]
            f, a = flux(q, state(q), 1)
            fr, ar = flux(qr, state(qr), 1)
            fl, al = flux(ql, state(ql), 1)
            up = rusanov(q, f, a, qr, fr, ar)
            lo = rusanov(ql, fl, al, q, f, a)
            for v in range(5):
                fy[v, cut, :] = jnp.where(y == 0, lo[v], up[v])
                out[v, p, cut, :] = q[v] - 0.1 * (change[v] + (up[v] - lo[v]))
            return 0

        lax.fori_loop(0, 4, rows, 0)
        l16 = iota((16, 128), 1) // 32
        for v in range(5):
            m = dot3(out[v, p], pair) * 0.125
            for h in range(2):
                tmp[0:32, 0:128] = m[:, 128 * h : 128 * h + 128]
                av[h, p, v] = tmp[pl.ds(0, 16, 2), :] + tmp[pl.ds(1, 16, 2), :]
            m = (dot3(fy[v], ypair) + dot3(fz[v], zpair)) * (0.25 * coef)
            tmp[0:32, 0:128] = m
            m = tmp[pl.ds(0, 16, 2), :] + tmp[pl.ds(1, 16, 2), :]
            t = 5 if v < 4 else 6
            gv = v % 4
            for h in range(2):
                r = pltpu.roll(m, (32 * gv - 32 * h) % 128, 1) if (32 * gv - 32 * h) % 128 else m
                if gv == 0:
                    av[h, p, t] = r
                else:
                    av[h, p, t] = jnp.where(l16 == gv, r, av[h, p, t])


def owner_kernel(av, rz, rb, oz, ss, rs, ls):
    s = lax.axis_index("slab")
    me = lax.axis_index("patch")
    peer = [lax.rem(me + d, NP) for d in range(NP)]
    barrier = pltpu.get_barrier_semaphore()
    for d in range(1, NP):
        pl.semaphore_signal(barrier, inc=1, device_id=(s, peer[d]), device_id_type=MESH)
    pl.semaphore_wait(barrier, NP - 1)
    own = pltpu.make_async_copy(av.at[lax.rem(me, 2)], rb.at[me], ls)
    own.start()
    copies = []

    def send(k, src, dst, to):
        c = pltpu.make_async_remote_copy(
            src_ref=src, dst_ref=dst, send_sem=ss.at[k], recv_sem=rs.at[k],
            device_id=(s, to), device_id_type=MESH,
        )
        c.start()
        copies.append(c)

    for d in range(1, NP):
        send(d, av.at[lax.rem(peer[d], 2)], rb.at[me], peer[d])
    send(0, rz.at[1], oz.at[0], peer[1])
    send(NP, rz.at[0], oz.at[1], peer[NP - 1])
    own.wait()
    for c in copies:
        c.wait()


def coarse_kernel(coarse, rb, oz, ocx, grid, out, ext, blk, zbl, res, sems):
    s = lax.axis_index("slab")
    me = lax.axis_index("patch")
    r = me // 2
    h = lax.rem(me, 2)
    rz = jnp.where(h == 0, r - 2, r)
    have = []
    havez = []
    cps = []
    for gy in range(6):
        a = grid[0, gy + 8 * (r - 1) + GOFF]
        b = grid[0, gy + 8 * rz + GOFF]
        have.append(a >= 0)
        havez.append(b >= 0)
        a = jnp.maximum(a, 0)
        b = jnp.maximum(b, 0)
        cps.append(pltpu.make_async_copy(rb.at[a >> 1, a & 1], blk.at[gy], sems.at[gy]))
        cps.append(pltpu.make_async_copy(rb.at[b >> 1, b & 1, pl.ds(5, 2)], zbl.at[gy], sems.at[6 + gy]))
    for c in cps:
        c.start()
    lane = iota((16, 128), 1)
    blocks = lane // 16

    def cover(row):
        m = jnp.zeros((16, 128), F32)
        for gy in range(6):
            m = jnp.where((blocks == gy + 1) & (grid[0, gy + 8 * (row - 1) + GOFF] >= 0), 1.0, m)
        return m

    mid = cover(r)
    below = jnp.where(h == 0, cover(r - 1), mid)
    above = jnp.where(h == 1, cover(r + 1), mid)
    free = 1.0 - mid
    fup = free * (1.0 - pltpu.roll(mid, 127, 1))
    flo = free * (1.0 - pltpu.roll(mid, 1, 1))
    zlo = free * (1.0 - below)
    zhi = free * (1.0 - above)
    for v in range(5):
        for k in range(8):
            ext[v, k + 1, 8:24, :] = coarse[v, :, k, :]
            ext[v, k + 1, 7:8, :] = jnp.where(s == 0, coarse[v, 0, k : k + 1, :], ocx[0, v, k : k + 1, :])
            ext[v, k + 1, 24:25, :] = jnp.where(s == NS - 1, coarse[v, 15, k : k + 1, :], ocx[1, v, k : k + 1, :])
        ext[v, 0, 8:24, :] = jnp.where(me == 0, coarse[v, :, 0, :], oz[0, v])
        ext[v, 9, 8:24, :] = jnp.where(me == NP - 1, coarse[v, :, 7, :], oz[1, v])
    for k in range(8):
        q = [ext[v, k + 1] for v in range(5)]
        st = state(q)
        f, a = flux(q, st, 0)
        nxt = lambda t: pltpu.roll(t, 31, 0)
        up = rusanov(q, f, a, [nxt(t) for t in q], [nxt(t) for t in f], nxt(a))
        change = [((up[v] - pltpu.roll(up[v], 1, 0))[8:24]) * free for v in range(5)]
        q = [t[8:24] for t in q]
        st = tuple(t[8:24] for t in st)
        f, a = flux(q, st, 2)
        qn = [ext[v, k + 2, 8:24, :] for v in range(5)]
        fn, an = flux(qn, state(qn), 2)
        qb = [ext[v, k, 8:24, :] for v in range(5)]
        fb, ab = flux(qb, state(qb), 2)
        up = rusanov(q, f, a, qn, fn, an)
        lo = rusanov(qb, fb, ab, q, f, a)
        mu = zhi if k == 7 else free
        ml = zlo if k == 0 else free
        change = [change[v] + (up[v] * mu - lo[v] * ml) for v in range(5)]
        f, a = flux(q, st, 1)
        nxt = lambda t: jnp.where(lane == 127, t, pltpu.roll(t, 127, 1))
        prv = lambda t: jnp.where(lane == 0, t, pltpu.roll(t, 1, 1))
        up = rusanov(q, f, a, [nxt(t) for t in q], [nxt(t) for t in f], nxt(a))
        lo = rusanov([prv(t) for t in q], [prv(t) for t in f], prv(a), q, f, a)
        for v in range(5):
            res[v, k] = q[v] - 0.05 * (change[v] + (up[v] * fup - lo[v] * flo))
    for c in cps:
        c.wait()
    src = iota((128, 1024), 0)
    dst = iota((128, 1024), 1)
    y = lax.rem(dst, 128)
    side = lax.rem(src, 16) // 8
    want = jnp.where(side == 0, 16 * (src // 16 + 1) - 1, 16 * (src // 16 + 2))
    place = ones_where((src < 96) & (dst // 128 == lax.rem(src, 8)) & (y == want))
    for v in range(5):
        t = 5 if v < 4 else 6
        gv = v % 4
        w = jnp.zeros((16, 128), F32)
        zf = jnp.zeros((16, 128), F32)
        for gy in range(6):
            sh = (16 * gy - 32 * gv) % 128
            fr = blk[gy, t]
            zr = zbl[gy, t - 5]
            if sh:
                fr = pltpu.roll(fr, sh, 1)
                zr = pltpu.roll(zr, sh, 1)
            w = jnp.where((blocks == gy) & have[gy], fr, w)
            zf = jnp.where((blocks == gy + 1) & havez[gy], zr, zf)
        yf = dot3(w, place)
        for k in range(8):
            val = res[v, k] + yf[:, 128 * k : 128 * k + 128]
            if k == 0:
                val = val + jnp.where(h == 0, zf, 0.0)
            if k == 7:
                val = val + jnp.where(h == 1, zf, 0.0)
            for gy in range(6):
                sh = (16 * (gy + 1 - k)) % 128
                t = blk[gy, v]
                if sh:
                    t = pltpu.roll(t, sh, 1)
                val = jnp.where((blocks == gy + 1) & have[gy], t, val)
            out[v, :, k, :] = val


def vm():
    return pl.BlockSpec(memory_space=pltpu.VMEM)


def sm():
    return pl.BlockSpec(memory_space=pltpu.SMEM)


def hb():
    return pl.BlockSpec(memory_space=pl.ANY)


def sds(*shape, dtype=F32):
    return jax.ShapeDtypeStruct(shape, dtype)


LIMIT = 48 << 20


def local(coarse, fine, columns, patch_ids):
    yzp, xf, cp, rz, cx, tab, grid = pl.pallas_call(
        pack_kernel,
        out_shape=(
            sds(2, 5, 32, 128), sds(2, 11, 8, 128), sds(5, 2, 16, 128), sds(2, 5, 16, 128), sds(2, 5, 8, 128),
            sds(10, 32, dtype=I32), sds(1, 96, dtype=I32),
        ),
        in_specs=[vm(), vm(), sm(), sm()],
        out_specs=(vm(), vm(), vm(), vm(), vm(), sm(), sm()),
        scratch_shapes=[pltpu.VMEM((8, 80, 128), F32)],
        compiler_params=pltpu.CompilerParams(vmem_limit_bytes=LIMIT),
        name="pack",
    )(fine, coarse, patch_ids, columns)
    nsem = 25
    oyz, ox, oc, ocx = pl.pallas_call(
        ghost_kernel,
        out_shape=(sds(4, 2, 5, 32, 128), sds(4, 2, 2, 5, 8, 128), sds(4, 2, 5, 16, 128), sds(2, 5, 8, 128)),
        in_specs=[vm(), vm(), vm(), vm(), sm(), sm()],
        out_specs=(vm(), vm(), vm(), vm()),
        scratch_shapes=[
            pltpu.VMEM((8, 5, 32, 128), F32),
            pltpu.VMEM((2, 4, 11, 8, 128), F32),
            pltpu.VMEM((4, 5, 2, 16, 128), F32),
            pltpu.VMEM((3, 2, 5, 32, 128), F32),
            pltpu.VMEM((3, 2, 2, 5, 8, 128), F32),
            pltpu.VMEM((3, 2, 5, 16, 128), F32),
            pltpu.SemaphoreType.DMA((nsem,)),
            pltpu.SemaphoreType.DMA((nsem,)),
            pltpu.SemaphoreType.DMA((2,)),
        ],
        compiler_params=pltpu.CompilerParams(collective_id=0, has_side_effects=True, vmem_limit_bytes=LIMIT),
        name="ghosts",
    )(yzp, xf, cp, cx, tab, patch_ids)
    fine_out, av = pl.pallas_call(
        fine_kernel,
        out_shape=(sds(5, 2, 32, 1024), sds(2, 2, 7, 16, 128)),
        in_specs=[vm(), vm(), vm(), vm(), sm()],
        out_specs=(vm(), vm()),
        scratch_shapes=[
            pltpu.VMEM((5, 48, 1024), F32),
            pltpu.VMEM((5, 32, 128), F32),
            pltpu.VMEM((5, 32, 1024), F32),
            pltpu.VMEM((5, 32, 1024), F32),
            pltpu.VMEM((5, 32, 128), F32),
            pltpu.VMEM((5, 8, 128), F32),
            pltpu.VMEM((80, 128), F32),
        ],
        compiler_params=pltpu.CompilerParams(vmem_limit_bytes=LIMIT),
        name="fine_step",
    )(fine, oyz, ox, oc, tab)
    rb, oz = pl.pallas_call(
        owner_kernel,
        out_shape=(sds(16, 2, 7, 16, 128), sds(2, 5, 16, 128)),
        in_specs=[vm(), vm()],
        out_specs=(hb(), hb()),
        scratch_shapes=[
            pltpu.SemaphoreType.DMA((NP + 1,)),
            pltpu.SemaphoreType.DMA((NP + 1,)),
            pltpu.SemaphoreType.DMA,
        ],
        compiler_params=pltpu.CompilerParams(collective_id=1, has_side_effects=True, vmem_limit_bytes=LIMIT),
        name="owners",
    )(av, rz)
    coarse_out = pl.pallas_call(
        coarse_kernel,
        out_shape=sds(5, 16, 8, 128),
        in_specs=[vm(), hb(), vm(), vm(), sm()],
        out_specs=vm(),
        scratch_shapes=[
            pltpu.VMEM((5, 10, 32, 128), F32),
            pltpu.VMEM((6, 7, 16, 128), F32),
            pltpu.VMEM((6, 2, 16, 128), F32),
            pltpu.VMEM((5, 8, 16, 128), F32),
            pltpu.SemaphoreType.DMA((12,)),
        ],
        compiler_params=pltpu.CompilerParams(vmem_limit_bytes=LIMIT),
        name="coarse_step",
    )(coarse, rb, oz, ocx, grid)
    return coarse_out, fine_out


def solution(mesh):
    return jax.shard_map(
        local,
        mesh=mesh,
        in_specs=(
            P(None, "slab", "patch", None),
            P(None, ("slab", "patch"), None, None),
            P(),
            P("slab", None),
        ),
        out_specs=(P(None, "slab", "patch", None), P(None, ("slab", "patch"), None, None)),
        check_vma=False,
    )
```

time: 725 us -> 86.7 us (0.12)
  the two profiles are of different devices: /device:TPU:2 before, /device:TPU:10 now
where the time goes in v1:
time: 86.7 us; the launch traced here: 86.5 us
  Pallas kernels  82.1 us (95%)
  local copies, waits for them, and re-layouts  3.71 us (4%)
    pallas_call x1, Pallas kernels, local(): pl.pallas_call(owner_kernel, out_shape=(sds(16, 2, 7, 16, 128), sds(2, 5,...  37.5 us
    pallas_call x1, Pallas kernels, local(): pl.pallas_call(ghost_kernel, out_shape=(sds(4, 2, 5, 32, 128), sds(4, 2,...  25.6 us
    pallas_call x1, Pallas kernels, local(): pl.pallas_call(fine_kernel, out_shape=(sds(5, 2, 32, 1024), sds(2, 2, 7,...  11 us
    pallas_call x1, Pallas kernels, local(): pl.pallas_call(pack_kernel, out_shape=(sds(2, 5, 32, 128), sds(2, 11, 8,...  4.07 us
    pallas_call x1, Pallas kernels, local(): pl.pallas_call(coarse_kernel, out_shape=sds(5, 16, 8, 128), in_specs=[vm(...  4.02 us
    unnamed x11, local copies, waits for them, and re-layouts  3.71 us

profile of v1, /device:TPU:10, one launch (start us, length us, event | category | flops | bytes accessed | tf_op | source)
XLA Modules:
  0.0 86.5 jit_solution(11554810397015709842)
XLA Ops:
  0.6 0.8 copy.6.cols
  1.4 0.0 copy-start
  1.4 1.3 %copy-done = f32[5,2,32,1024]{3,2,1,0:T(8,128)S(1)} copy-done((f32[5,2,32,1024]{3,2,1,0:T(8,128)S(1)}, f32[5,2,32,1024]{3,2,1,0:T(8,128)}, u32[]{:S(2)}) %copy-start) | copy-done | bytes 1310744
  2.7 0.0 copy-start.2
  2.7 1.0 %copy-done.2 = f32[5,16,8,128]{3,2,1,0:T(8,128)S(1)} copy-done((f32[5,16,8,128]{3,2,1,0:T(8,128)S(1)}, f32[5,16,8,128]{3,2,1,0:T(8,128)}, u32[]{:S(2)}) %copy-start.2) | copy-done | bytes 327704
  3.7 0.0 copy-start.4
  3.7 0.7 copy-done.4
  4.3 0.0 copy-start.1
  4.3 4.1 %pack.1 = (f32[2,5,32,128]{3,2,1,0:T(8,128)S(1)}, f32[2,11,8,128]{3,2,1,0:T(8,128)S(1)}, f32[5,2,16,128]{3,2,1,0:T(8,128)S(1)}, f32[2,5,16,128]{3,2,1,0:T(8,128)...) custom-call(f32[5,2,32,1024]{3,2,1,0:T(8,128)S(1)} %copy-done, ...), custom_call_target="tpu_custom_call" | custom-call | tf_op jit(solution)/shard_map/pack/pallas_call | solution.py:510
  8.4 25.6 %ghosts.1 = (f32[4,2,5,32,128]{4,3,2,1,0:T(8,128)S(1)}, f32[4,2,2,5,8,128]{5,4,3,2,1,0:T(8,128)S(1)}, f32[4,2,5,16,128]{4,3,2,1,0:T(8,128)S(1)}, f32[2,5,8,128]{3,2,1,0:T(8,128)S(1)}) custom-call(f32[2,5,32,128]{3,2,1,0:T(8,128)S(1)} %get-tuple-element.17.yzp, f32[2,11,8,128]{3,2,1,0:T(8,128)S(1)} %get-tuple-element.18.xf, ...), custom_call_target="tpu_custom_call" | custom-call | tf_op jit(solution)/shard_map/ghosts/pallas_call | solution.py:523
  34.0 0.0 copy-done.1
  34.0 0.0 copy-start.3
  34.0 11.0 %fine_step.1 = (f32[5,2,32,1024]{3,2,1,0:T(8,128)}, f32[2,2,7,16,128]{4,3,2,1,0:T(8,128)S(1)}) custom-call(f32[5,2,32,1024]{3,2,1,0:T(8,128)S(1)} %copy-done.1, f32[4,2,5,32,128]{4,3,2,1,0:T(8,128)S(1)} %get-tuple-element.22.oyz, f32[4,2,2,5,8,128]{5,4,3,2,1,0:T(8,128)S(1)} %get-tuple-element.23.ox, f32[4,2,5,16,128]{4,3,2,1,0:T(8,128)S(1)} %get-tuple-element.24.oc, ...), custom_call_target="tpu_custom_call" | custom-call | tf_op jit(solution)/shard_map/fine_step/pallas_call | solution.py:542
  45.0 37.5 %owners.1 = (f32[16,2,7,16,128]{4,3,2,1,0:T(8,128)S(1)}, f32[2,5,16,128]{3,2,1,0:T(8,128)S(1)}) custom-call(f32[2,2,7,16,128]{4,3,2,1,0:T(8,128)S(1)} %get-tuple-element.25.av, f32[2,5,16,128]{3,2,1,0:T(8,128)S(1)} %get-tuple-element.26.rz), custom_call_target="tpu_custom_call" | custom-call | tf_op jit(solution)/shard_map/owners/pallas_call | solution.py:559
  82.5 0.0 copy-done.3
  82.5 4.0 %coarse_step.1 = f32[5,16,8,128]{3,2,1,0:T(8,128)} custom-call(f32[5,16,8,128]{3,2,1,0:T(8,128)S(1)} %copy-done.3, f32[16,2,7,16,128]{4,3,2,1,0:T(8,128)S(1)} %get-tuple-element.27.rb, f32[2,5,16,128]{3,2,1,0:T(8,128)S(1)} %get-tuple-element.28.oz, f32[2,5,8,128]{3,2,1,0:T(8,128)S(1)} %get-tuple-element.29.ocx, s32[1,96]{1,0:T(1,128)S(1)} %get-tuple-element.30.grid), custom_call_target="tpu_custom_call" | custom-call | tf_op jit(solution)/shard_map/coarse_step/pallas_call | solution.py:572
Async XLA Ops:
  1.4 1.3 %copy-start = (f32[5,2,32,1024]{3,2,1,0:T(8,128)S(1)}, f32[5,2,32,1024]{3,2,1,0:T(8,128)}, u32[]{:S(2)}) copy-start(f32[5,2,32,1024]{3,2,1,0:T(8,128)} %fine.3) | copy-start | bytes 3932164
  2.7 1.0 %copy-start.2 = (f32[5,16,8,128]{3,2,1,0:T(8,128)S(1)}, f32[5,16,8,128]{3,2,1,0:T(8,128)}, u32[]{:S(2)}) copy-start(f32[5,16,8,128]{3,2,1,0:T(8,128)} %coarse.3) | copy-start | bytes 983044
  3.7 0.7 copy-start.4
  4.3 29.6 %copy-start.1 = (f32[5,2,32,1024]{3,2,1,0:T(8,128)S(1)}, f32[5,2,32,1024]{3,2,1,0:T(8,128)}, u32[]{:S(2)}) copy-start(f32[5,2,32,1024]{3,2,1,0:T(8,128)} %fine.3) | copy-start | bytes 3932164
  34.0 48.5 %copy-start.3 = (f32[5,16,8,128]{3,2,1,0:T(8,128)S(1)}, f32[5,16,8,128]{3,2,1,0:T(8,128)}, u32[]{:S(2)}) copy-start(f32[5,16,8,128]{3,2,1,0:T(8,128)} %coarse.3) | copy-start | bytes 983044

commit v2 on v1

v2 whole, which is shorter than its diff:
```python
import jax
import jax.numpy as jnp
from jax import lax
from jax.experimental import pallas as pl
from jax.experimental.pallas import tpu as pltpu
from jax.sharding import PartitionSpec as P

F32 = jnp.float32
BF16 = jnp.bfloat16
I32 = jnp.int32
MESH = pl.DeviceIdType.MESH
NS = 8
NP = 16
GOFF = 16


def iota(shape, dim):
    return lax.broadcasted_iota(I32, shape, dim)


def dot3(x, m):
    hi = x.astype(BF16)
    r = x - hi.astype(F32)
    mid = r.astype(BF16)
    lo = (r - mid.astype(F32)).astype(BF16)
    d = lambda a: jnp.dot(a, m, preferred_element_type=F32)
    return d(hi) + (d(mid) + d(lo))


def moved(x, k):
    return pltpu.roll(x, k % 128, 1) if k % 128 else x


def ones_where(c):
    return jnp.where(c, 1.0, 0.0).astype(BF16)


def state(q):
    r = 1.0 / q[0]
    p = 0.4 * (q[4] - 0.5 * ((q[1] * q[1] + q[2] * q[2] + q[3] * q[3]) * r))
    c = jnp.sqrt(1.4 * p * r)
    return r, p, c


def flux(q, s, d):
    r, p, c = s
    u = q[1 + d] * r
    f = [q[1 + d], q[1] * u, q[2] * u, q[3] * u, (q[4] + p) * u]
    f[1 + d] = f[1 + d] + p
    return f, jnp.abs(u) + c


def rusanov(ql, fl, al, qr, fr, ar):
    a = 0.5 * jnp.maximum(al, ar)
    return [0.5 * (fl[v] + fr[v]) - a * (qr[v] - ql[v]) for v in range(5)]


def pack_kernel(fine, coarse, ids, cols, a1, x1, rz, cx, nbr, grid, ct, fr):
    rank = lax.axis_index("patch")
    half = lax.rem(rank, 2)
    for i in range(96):
        grid[0, i] = jnp.int32(-1)

    def place(s, _):
        n = ids[0, s]
        gy = cols[n, 0]
        gz = cols[n, 1]
        nbr[4, s] = gy
        nbr[5, s] = gz
        grid[0, gy + 8 * gz + GOFF] = s
        return 0

    lax.fori_loop(0, 32, place, 0)

    def look(s, _):
        code = nbr[4, s] + 8 * nbr[5, s] + GOFF
        for g, step in enumerate((-1, 1, -8, 8)):
            nbr[g, s] = grid[0, code + step]
        return 0

    lax.fori_loop(0, 32, look, 0)
    k = iota((1024, 128), 0)
    c = iota((1024, 128), 1)
    g = c // 32
    i = lax.rem(c, 32)
    want = jnp.where(g == 0, 32 * i + 31, jnp.where(g == 1, 32 * i, jnp.where(g == 2, 992 + i, i)))
    sel = ones_where(k == want)
    for v in range(5):
        for p in range(2):
            fr[...] = dot3(fine[v, p], sel)
            for xr in range(2):
                a1[:, p, 5 * xr + v, :] = fr[pl.ds(xr, 16, 2), :]
    lane = iota((5, 128), 1)
    n0 = ids[0, 2 * rank]
    n1 = ids[0, 2 * rank + 1]
    tag = jnp.where(iota((3, 128), 1) < 64, n0, n1).astype(F32)
    for d, row in ((0, 0), (1, 31)):
        for j in range(8):
            t0 = fine[:, 0, row, 128 * j : 128 * j + 128]
            t1 = fine[:, 1, row, 128 * j : 128 * j + 128]
            x1[d, 2 * j, 0:5, :] = jnp.where(lane < 64, t0, pltpu.roll(t1, 64, 1))
            x1[d, 2 * j + 1, 0:5, :] = jnp.where(lane < 64, pltpu.roll(t0, 64, 1), t1)
            x1[d, 2 * j, 5:8, :] = tag
            x1[d, 2 * j + 1, 5:8, :] = tag
    for v in range(5):
        for z in range(8):
            ct[z, 16 * v : 16 * v + 16, :] = coarse[v, :, z, :]
    y = iota((128, 128), 0)
    k = iota((128, 128), 1) // 8
    plane = jnp.where(k < 6, 16 * (k + 1) - 1, jnp.where(k < 12, 16 * (k - 4), -1))
    sel = ones_where(y == plane)
    lane8 = lax.rem(iota((80, 128), 1), 8)
    acc = jnp.zeros((80, 128), F32)
    for z in range(8):
        acc = jnp.where(lane8 == z, dot3(ct[z], sel), acc)
    first = ct[0]
    last = ct[7]
    own = jnp.where(half == 0, first, last)
    for v in range(5):
        cut = slice(16 * v, 16 * v + 16)
        a1[:, 0, 10 + v, :] = acc[cut]
        a1[:, 1, 10 + v, :] = own[cut]
        rz[0, v] = first[cut]
        rz[1, v] = last[cut]
        cx[0, v] = coarse[v, 0]
        cx[1, v] = coarse[v, 15]
    a1[:, 0, 15, :] = jnp.zeros((16, 128), F32)
    a1[:, 1, 15, :] = jnp.zeros((16, 128), F32)


def ghost_kernel(a1, x1, rz, cx, nbr, ids, og, oz, ocx, ba, bx, tb, dd, ss, rs, ls):
    s = lax.axis_index("slab")
    me = lax.axis_index("patch")
    up = lax.rem(s + 1, NS)
    down = lax.rem(s + NS - 1, NS)
    peer = [lax.rem(me + d, NP) for d in range(NP)]
    barrier = pltpu.get_barrier_semaphore()
    for d in range(NP):
        if d:
            pl.semaphore_signal(barrier, inc=1, device_id=(s, peer[d]), device_id_type=MESH)
        pl.semaphore_signal(barrier, inc=1, device_id=(up, peer[d]), device_id_type=MESH)
        pl.semaphore_signal(barrier, inc=1, device_id=(down, peer[d]), device_id_type=MESH)
    pl.semaphore_wait(barrier, 3 * NP - 1)
    one = []
    two = []
    count = [0]

    def send(to, src, dst, dev):
        k = count[0]
        count[0] += 1
        c = pltpu.make_async_remote_copy(
            src_ref=src, dst_ref=dst, send_sem=ss.at[k], recv_sem=rs.at[k],
            device_id=dev, device_id_type=MESH,
        )
        c.start()
        to.append(c)

    for d in range(NP):
        j = peer[d]
        if d:
            send(one, a1.at[j], ba.at[pl.ds(2 * me, 2)], (s, j))
        send(one, x1.at[0, j], bx.at[1, me], (down, j))
        send(one, x1.at[1, j], bx.at[0, me], (up, j))
    send(two, cx.at[0], ocx.at[1], (down, me))
    send(two, cx.at[1], ocx.at[0], (up, me))
    send(two, rz.at[1], oz.at[0], (s, peer[1]))
    send(two, rz.at[0], oz.at[1], (s, peer[NP - 1]))
    own = pltpu.make_async_copy(a1.at[me], ba.at[pl.ds(2 * me, 2)], ls)
    own.start()
    own.wait()
    src = iota((128, 128), 0)
    dst = iota((128, 128), 1)
    g = dst // 32
    i = lax.rem(dst, 32) // 2
    base = jnp.where(g == 0, 0, jnp.where(g == 1, 48, jnp.where(g == 2, 64, 80)))
    spread = ones_where(src == base + i)
    for c in one:
        c.wait()

    def tags(i, _):
        for way in range(2):
            t = bx[way, i]
            r = pltpu.roll(t, 64, 1)
            tb[way, 2 * i] = t
            tb[way, 2 * i + 1] = r
        return 0

    lax.fori_loop(0, NP, tags, 0)
    lane = iota((8, 128), 1)
    group = iota((10, 128), 1) // 32

    def select(j, _):
        nn = jnp.where(iota((1, 128), 1) < 64, ids[0, 2 * j], ids[0, 2 * j + 1]).astype(F32)
        for p in range(2):
            slot = 2 * j + p
            gy = nbr[4, slot]
            gz = nbr[5, slot]
            a = 4 * (gz + 1)
            y0 = ba[a, 8:16, :]
            y1 = ba[a + 2, 8:16, :]
            z0 = ba[4 * gz + 3, 8:16, :]
            z1 = ba[4 * gz + 9, 8:16, :]
            r0 = pltpu.roll(y0, (128 - 8 * gy) & 127, 1)
            r1 = pltpu.roll(y1, (136 - 8 * gy) & 127, 1)
            r2 = pltpu.roll(z0, (176 - 16 * gy) & 127, 1)
            r3 = pltpu.roll(z1, (192 - 16 * gy) & 127, 1)
            c = jnp.where(lane < 64, jnp.where((lane & 8) == 0, r0, r1), jnp.where(lane < 80, r2, r3))
            c = dot3(c, spread)[2:7]
            val = jnp.concatenate([c, c], axis=0)
            for g in range(4):
                q = nbr[g, slot]
                val = jnp.where((group == g) & (q >= 0), ba[jnp.maximum(q, 0), 0:10, :], val)
            dd[j, p, 0:10, :] = val
            way = p
            acc = jnp.zeros((5, 128), F32)
            for i in range(2 * NP):
                acc = jnp.where(tb[way, i, 5:6, :] == nn, tb[way, i, 0:5, :], acc)
            dd[j, p, 10:15, :] = acc
            dd[j, p, 15:16, :] = jnp.zeros((1, 128), F32)
        return 0

    lax.fori_loop(0, NP, select, 0)
    for d in range(1, NP):
        send(two, dd.at[peer[d]], og.at[me], (s, peer[d]))
    own = pltpu.make_async_copy(dd.at[me], og.at[me], ls)
    own.start()
    own.wait()
    for c in two:
        c.wait()


def fine_kernel(fine, og, out, av, ext, ghost, chg, fy, fz, tmp):
    s = lax.axis_index("slab")
    src = iota((128, 1024), 0)
    dst = iota((128, 1024), 1)
    g = src // 32
    expand = ones_where(
        ((g == 0) & (dst == 32 * lax.rem(src, 32))) | ((g == 1) & (dst == 32 * lax.rem(src, 32) + 31))
    )
    src = iota((1024, 256), 0)
    dst = iota((1024, 256), 1)
    zz = 8 * (dst // 128) + 7 - lax.rem(dst, 128) // 16
    pair = ones_where((src // 64 == zz) & (lax.rem(src, 32) // 2 == lax.rem(dst, 16)))
    src = iota((1024, 128), 0)
    dst = iota((1024, 128), 1)
    d64 = dst & 63
    isl = d64 < 8
    ish = (d64 >= 17) & (d64 < 25)
    zz = (dst // 64) * 8 + 7 - jnp.where(isl, d64, d64 - 17)
    ypair = ones_where(
        (src // 64 == zz) & ((isl & (lax.rem(src, 32) == 0)) | (ish & (lax.rem(src, 32) == 31)))
    )
    src = iota((128, 128), 0)
    dst = iota((128, 128), 1)
    zpair = ones_where(
        ((dst >= 64) & (dst < 80) & (src < 32) & (src // 2 == dst - 64))
        | ((dst < 16) & (src >= 96) & ((src - 96) // 2 == dst))
    )
    l1 = iota((1, 128), 1)
    ycoef = jnp.where((l1 & 63) < 8, -0.05, 0.05).astype(F32) * 0.25
    zcoef = jnp.where(l1 >= 64, -0.05, 0.05).astype(F32) * 0.25
    l5 = iota((5, 128), 1)

    for p in range(2):
        for m in range(16):
            for xr in range(2):
                for v in range(5):
                    ghost[v, 2 * m + xr : 2 * m + xr + 1, :] = og[m, p, 5 * xr + v : 5 * xr + v + 1, :]
        for way in range(2):
            edge = (s == 0) if way == 0 else (s == NS - 1)
            row = 7 if way == 0 else 40
            mine = 0 if way == 0 else 31
            for j in range(8):
                cut = slice(128 * j, 128 * j + 128)
                e = og[2 * j, way, 10:15, :]
                o = og[2 * j + 1, way, 10:15, :]
                if p == 0:
                    o = pltpu.roll(o, 64, 1)
                else:
                    e = pltpu.roll(e, 64, 1)
                ext[:, row, cut] = jnp.where(edge, fine[:, p, mine, cut], jnp.where(l5 < 64, e, o))
        for v in range(5):
            ext[v, 8:40, :] = fine[v, p]

        def along_x(j, _):
            cut = pl.ds(pl.multiple_of(128 * j, 128), 128)
            q = [ext[v, :, cut] for v in range(5)]
            f, a = flux(q, state(q), 0)
            nxt = lambda t: pltpu.roll(t, 47, 0)
            up = rusanov(q, f, a, [nxt(t) for t in q], [nxt(t) for t in f], nxt(a))
            for v in range(5):
                chg[v, :, cut] = (up[v] - pltpu.roll(up[v], 1, 0))[8:40]
            return 0

        lax.fori_loop(0, 8, along_x, 0)

        def rows(c, _):
            cut = pl.ds(pl.multiple_of(8 * c, 8), 8)
            q = [fine[v, p, cut, :] for v in range(5)]
            gh = [ghost[v, cut, :] for v in range(5)]
            gr = [pltpu.roll(t, 32, 1) for t in gh]
            qe = [jnp.concatenate([gr[v], q[v], gr[v]], axis=1) for v in range(5)]
            f, a = flux(qe, state(qe), 2)
            nxt = lambda t: pltpu.roll(t, 1280 - 32, 1)
            up = rusanov(qe, f, a, [nxt(t) for t in qe], [nxt(t) for t in f], nxt(a))
            lo = [pltpu.roll(t, 32, 1) for t in up]
            l8 = iota((8, 128), 1)
            for v in range(5):
                fz[v, cut, :] = jnp.where(l8 < 32, lo[v][:, 128:256], up[v][:, 1024:1152])
            change = [chg[v, cut, :] + (up[v] - lo[v])[:, 128:1152] for v in range(5)]
            eg = [dot3(t, expand) for t in gh]
            y = iota((8, 1024), 1) & 31
            qr = [jnp.where(y == 31, eg[v], pltpu.roll(q[v], 1023, 1)) for v in range(5)]
            ql = [jnp.where(y == 0, eg[v], pltpu.roll(q[v], 1, 1)) for v in range(5)]
            f, a = flux(q, state(q), 1)
            fr, ar = flux(qr, state(qr), 1)
            fl, al = flux(ql, state(ql), 1)
            up = rusanov(q, f, a, qr, fr, ar)
            lo = rusanov(ql, fl, al, q, f, a)
            for v in range(5):
                fy[v, cut, :] = jnp.where(y == 0, lo[v], up[v])
                out[v, p, cut, :] = q[v] - 0.1 * (change[v] + (up[v] - lo[v]))
            return 0

        lax.fori_loop(0, 4, rows, 0)
        l16 = iota((16, 128), 1)
        yr = [jnp.zeros((16, 128), F32)] * 2
        zr = [jnp.zeros((16, 128), F32)] * 2

        def halve(m):
            tmp[...] = m
            return tmp[pl.ds(0, 16, 2), :] + tmp[pl.ds(1, 16, 2), :]

        for v in range(5):
            m = dot3(out[v, p], pair) * 0.125
            ym = halve(dot3(fy[v], ypair) * ycoef)
            zm = halve(dot3(fz[v], zpair) * zcoef)
            for h in range(2):
                av[:, h, p, v, :] = halve(m[:, 128 * h : 128 * h + 128])
                yr[h] = jnp.where((l16 >= 25 * v) & (l16 < 25 * v + 25), moved(ym, 25 * v - 64 * h), yr[h])
                zr[h] = jnp.where(l16 // 16 == v, moved(zm, 16 * v - 64 * h), zr[h])
        for h in range(2):
            av[:, h, p, 5, :] = yr[h]
            av[:, h, p, 6, :] = zr[h]
            av[:, h, p, 7, :] = jnp.zeros((16, 128), F32)


def owner_kernel(av, grid, oe, bb, ee, ss, rs, ls):
    s = lax.axis_index("slab")
    me = lax.axis_index("patch")
    peer = [lax.rem(me + d, NP) for d in range(NP)]
    barrier = pltpu.get_barrier_semaphore()
    for d in range(1, NP):
        pl.semaphore_signal(barrier, inc=1, device_id=(s, peer[d]), device_id_type=MESH)
    pl.semaphore_wait(barrier, NP - 1)
    one = []
    two = []

    def send(to, k, src, dst, j):
        c = pltpu.make_async_remote_copy(
            src_ref=src, dst_ref=dst, send_sem=ss.at[k], recv_sem=rs.at[k],
            device_id=(s, j), device_id_type=MESH,
        )
        c.start()
        to.append(c)

    for d in range(1, NP):
        send(one, d - 1, av.at[peer[d]], bb.at[me], peer[d])
    own = pltpu.make_async_copy(av.at[me], bb.at[me], ls)
    own.start()
    own.wait()
    lane = iota((8, 128), 1)
    sub = iota((8, 128), 0)
    block = lane // 16
    for c in one:
        c.wait()

    def expand(j, _):
        h = lax.rem(j, 2)
        r = j // 2
        far = jnp.where(h == 0, r - 2, r)
        edge = jnp.where(h == 0, 0, 7)
        val = [jnp.zeros((8, 128), F32)] * 5
        add = [jnp.zeros((8, 128), F32)] * 5
        for gy in range(6):
            a = grid[0, gy + 8 * (r - 1) + GOFF]
            b = grid[0, gy + 8 * far + GOFF]
            a0 = jnp.maximum(a, 0)
            b0 = jnp.maximum(b, 0)
            t = bb[a0 // 2, h, a0 & 1]
            zt = bb[b0 // 2, h, b0 & 1, 6:7, :]
            ina = (block == gy + 1) & (a >= 0)
            inb = (block == gy + 1) & (sub == edge) & (b >= 0)
            iny = ((lane == 16 * gy + 15) | (lane == 16 * gy + 32)) & (a >= 0)
            yt = pltpu.roll(jnp.broadcast_to(t[5:6], (8, 128)), 0, 1, stride=1, stride_axis=0)
            zt = jnp.broadcast_to(zt, (8, 128))
            for v in range(5):
                w = jnp.broadcast_to(t[v : v + 1], (8, 128))
                w = moved(pltpu.roll(w, 0, 1, stride=16, stride_axis=0), 16 * gy + 32)
                val[v] = jnp.where(ina, w, val[v])
                w = moved(yt, 16 * gy + 8 - 25 * v)
                add[v] = jnp.where(iny, add[v] + w, add[v])
                w = moved(zt, 16 * gy + 16 - 16 * v)
                add[v] = jnp.where(inb, add[v] + w, add[v])
        covered = jnp.zeros((8, 128), F32)
        for gy in range(6):
            covered = jnp.where((block == gy + 1) & (grid[0, gy + 8 * (r - 1) + GOFF] >= 0), 1.0, covered)
        for v in range(5):
            ee[j, v] = jnp.where(covered > 0, val[v], add[v])
        return 0

    lax.fori_loop(0, NP, expand, 0)
    for d in range(1, NP):
        send(two, NP - 2 + d, ee.at[peer[d]], oe.at[me], peer[d])
    own = pltpu.make_async_copy(ee.at[me], oe.at[me], ls)
    own.start()
    own.wait()
    for c in two:
        c.wait()


def coarse_kernel(coarse, oe, oz, ocx, grid, out):
    s = lax.axis_index("slab")
    me = lax.axis_index("patch")
    r = me // 2
    h = lax.rem(me, 2)
    lane = iota((8, 128), 1)
    sub = iota((8, 128), 0)
    blocks = lane // 16

    def cover(row):
        m = jnp.zeros((8, 128), F32)
        for gy in range(6):
            m = jnp.where((blocks == gy + 1) & (grid[0, gy + 8 * (row - 1) + GOFF] >= 0), 1.0, m)
        return m

    mid = cover(r)
    below = jnp.where(h == 0, cover(r - 1), mid)
    above = jnp.where(h == 1, cover(r + 1), mid)
    free = 1.0 - mid
    fup = free * (1.0 - pltpu.roll(mid, 127, 1))
    flo = free * (1.0 - pltpu.roll(mid, 1, 1))
    zlo = free * (1.0 - jnp.where(sub == 0, below, mid))
    zhi = free * (1.0 - jnp.where(sub == 7, above, mid))

    def cells(x):
        q = [coarse[v, x] for v in range(5)]
        st = state(q)
        return q, st, flux(q, st, 0)

    def face(a, b):
        return rusanov(a[0], a[2][0], a[2][1], b[0], b[2][0], b[2][1])

    first = cells(0)
    q = [jnp.where(s == 0, coarse[v, 0], ocx[0, v]) for v in range(5)]
    st = state(q)
    lower = face((q, st, flux(q, st, 0)), first)
    here = first
    for x in range(16):
        if x < 15:
            there = cells(x + 1)
        else:
            q = [jnp.where(s == NS - 1, coarse[v, 15], ocx[1, v]) for v in range(5)]
            st = state(q)
            there = (q, st, flux(q, st, 0))
        upper = face(here, there)
        q, st, _ = here
        change = [(upper[v] - lower[v]) * free for v in range(5)]
        row = slice(x, x + 1)
        zn = [jnp.where(sub == 7, jnp.where(me == NP - 1, q[v], oz[1, v, row, :]), pltpu.roll(q[v], 7, 0)) for v in range(5)]
        zb = [jnp.where(sub == 0, jnp.where(me == 0, q[v], oz[0, v, row, :]), pltpu.roll(q[v], 1, 0)) for v in range(5)]
        f, a = flux(q, st, 2)
        fn, an = flux(zn, state(zn), 2)
        fb, ab = flux(zb, state(zb), 2)
        up = rusanov(q, f, a, zn, fn, an)
        lo = rusanov(zb, fb, ab, q, f, a)
        change = [change[v] + (up[v] * zhi - lo[v] * zlo) for v in range(5)]
        f, a = flux(q, st, 1)
        nxt = lambda t: jnp.where(lane == 127, t, pltpu.roll(t, 127, 1))
        prv = lambda t: jnp.where(lane == 0, t, pltpu.roll(t, 1, 1))
        up = rusanov(q, f, a, [nxt(t) for t in q], [nxt(t) for t in f], nxt(a))
        lo = rusanov([prv(t) for t in q], [prv(t) for t in f], prv(a), q, f, a)
        for v in range(5):
            prov = q[v] - 0.05 * (change[v] + (up[v] * fup - lo[v] * flo))
            e = oe[x, v]
            out[v, x] = jnp.where(mid > 0, e, prov + e)
        here = there
        lower = upper


def vm():
    return pl.BlockSpec(memory_space=pltpu.VMEM)


def sm():
    return pl.BlockSpec(memory_space=pltpu.SMEM)


def sds(*shape, dtype=F32):
    return jax.ShapeDtypeStruct(shape, dtype)


LIMIT = 48 << 20


def params(**k):
    return pltpu.CompilerParams(vmem_limit_bytes=LIMIT, **k)


def local(coarse, fine, columns, patch_ids):
    a1, x1, rz, cx, nbr, grid = pl.pallas_call(
        pack_kernel,
        out_shape=(
            sds(16, 2, 16, 128), sds(2, 16, 8, 128), sds(2, 5, 16, 128), sds(2, 5, 8, 128),
            sds(6, 32, dtype=I32), sds(1, 96, dtype=I32),
        ),
        in_specs=[vm(), vm(), sm(), sm()],
        out_specs=(vm(), vm(), vm(), vm(), sm(), sm()),
        scratch_shapes=[pltpu.VMEM((8, 80, 128), F32), pltpu.VMEM((32, 128), F32)],
        compiler_params=params(),
        name="pack",
    )(fine, coarse, patch_ids, columns)
    nsem = 3 * NP - 1 + 4 + NP - 1
    og, oz, ocx = pl.pallas_call(
        ghost_kernel,
        out_shape=(sds(16, 2, 16, 128), sds(2, 5, 16, 128), sds(2, 5, 8, 128)),
        in_specs=[vm(), vm(), vm(), vm(), sm(), sm()],
        out_specs=(vm(), vm(), vm()),
        scratch_shapes=[
            pltpu.VMEM((32, 16, 128), F32),
            pltpu.VMEM((2, 16, 8, 128), F32),
            pltpu.VMEM((2, 32, 8, 128), F32),
            pltpu.VMEM((16, 2, 16, 128), F32),
            pltpu.SemaphoreType.DMA((nsem,)),
            pltpu.SemaphoreType.DMA((nsem,)),
            pltpu.SemaphoreType.DMA,
        ],
        compiler_params=params(collective_id=0, has_side_effects=True),
        name="ghosts",
    )(a1, x1, rz, cx, nbr, patch_ids)
    fine_out, av = pl.pallas_call(
        fine_kernel,
        out_shape=(sds(5, 2, 32, 1024), sds(16, 2, 2, 8, 128)),
        in_specs=[vm(), vm()],
        out_specs=(vm(), vm()),
        scratch_shapes=[
            pltpu.VMEM((5, 48, 1024), F32),
            pltpu.VMEM((5, 32, 128), F32),
            pltpu.VMEM((5, 32, 1024), F32),
            pltpu.VMEM((5, 32, 1024), F32),
            pltpu.VMEM((5, 32, 128), F32),
            pltpu.VMEM((32, 128), F32),
        ],
        compiler_params=params(),
        name="fine_step",
    )(fine, og)
    oe = pl.pallas_call(
        owner_kernel,
        out_shape=sds(16, 5, 8, 128),
        in_specs=[vm(), sm()],
        out_specs=vm(),
        scratch_shapes=[
            pltpu.VMEM((16, 2, 2, 8, 128), F32),
            pltpu.VMEM((16, 5, 8, 128), F32),
            pltpu.SemaphoreType.DMA((2 * NP - 2,)),
            pltpu.SemaphoreType.DMA((2 * NP - 2,)),
            pltpu.SemaphoreType.DMA,
        ],
        compiler_params=params(collective_id=1, has_side_effects=True),
        name="owners",
    )(av, grid)
    coarse_out = pl.pallas_call(
        coarse_kernel,
        out_shape=sds(5, 16, 8, 128),
        in_specs=[vm(), vm(), vm(), vm(), sm()],
        out_specs=vm(),
        compiler_params=params(),
        name="coarse_step",
    )(coarse, oe, oz, ocx, grid)
    return coarse_out, fine_out


def solution(mesh):
    return jax.shard_map(
        local,
        mesh=mesh,
        in_specs=(
            P(None, "slab", "patch", None),
            P(None, ("slab", "patch"), None, None),
            P(),
            P("slab", None),
        ),
        out_specs=(P(None, "slab", "patch", None), P(None, ("slab", "patch"), None, None)),
        check_vma=False,
    )
```

time: 86.7 us -> 69.6 us (0.80)
  the two profiles are of different devices: /device:TPU:10 before, /device:TPU:0 now
where the time goes in v2:
time: 69.6 us; the launch traced here: 69.4 us
  Pallas kernels  65 us (93%)
  local copies, waits for them, and re-layouts  3.71 us (5%)
    pallas_call x1, Pallas kernels, local(): pl.pallas_call(ghost_kernel, out_shape=(sds(16, 2, 16, 128), sds(2, 5, 16...  29.4 us
    pallas_call x1, Pallas kernels, local(): pl.pallas_call(owner_kernel, out_shape=sds(16, 5, 8, 128), in_specs=[vm()...  19.4 us
    pallas_call x1, Pallas kernels, local(): pl.pallas_call(fine_kernel, out_shape=(sds(5, 2, 32, 1024), sds(16, 2, 2,...  10.2 us
    pallas_call x1, Pallas kernels, local(): pl.pallas_call(pack_kernel, out_shape=(sds(16, 2, 16, 128), sds(2, 16, 8,...  3.82 us
    unnamed x11, local copies, waits for them, and re-layouts  3.71 us
    pallas_call x1, Pallas kernels, local(): pl.pallas_call(coarse_kernel, out_shape=sds(5, 16, 8, 128), in_specs=[vm(...  2.11 us

profile of v2, /device:TPU:0, one launch (start us, length us, event | category | flops | bytes accessed | tf_op | source)
XLA Modules:
  0.0 69.4 jit_solution(7264388325458376023)
XLA Ops:
  0.6 0.8 %copy.6.cols = s32[32,2]{1,0:T(8,128)S(1)} copy(s32[32,2]{0,1:T(2,128)} %param.6) | data formatting | bytes 512 | tf_op args[2]
  1.4 0.0 copy-start
  1.4 1.3 %copy-done = f32[5,2,32,1024]{3,2,1,0:T(8,128)S(1)} copy-done((f32[5,2,32,1024]{3,2,1,0:T(8,128)S(1)}, f32[5,2,32,1024]{3,2,1,0:T(8,128)}, u32[]{:S(2)}) %copy-start) | copy-done | bytes 1310744
  2.7 0.0 copy-start.2
  2.7 1.0 %copy-done.2 = f32[5,16,8,128]{3,2,1,0:T(8,128)S(1)} copy-done((f32[5,16,8,128]{3,2,1,0:T(8,128)S(1)}, f32[5,16,8,128]{3,2,1,0:T(8,128)}, u32[]{:S(2)}) %copy-start.2) | copy-done | bytes 327704
  3.7 0.0 copy-start.4
  3.7 0.7 copy-done.4
  4.3 0.0 copy-start.1
  4.3 3.8 %pack.1 = (f32[16,2,16,128]{3,2,1,0:T(8,128)S(1)}, f32[2,16,8,128]{3,2,1,0:T(8,128)S(1)}, f32[2,5,16,128]{3,2,1,0:T(8,128)S(1)}, f32[2,5,8,128]{3,2,1,0:T(8,128)...) custom-call(f32[5,2,32,1024]{3,2,1,0:T(8,128)S(1)} %copy-done, f32[5,16,8,128]{3,2,1,0:T(8,128)S(1)} %copy-done.2, ...), custom_call_target="tpu_custom_call" | custom-call | tf_op jit(solution)/shard_map/pack/pallas_call | solution.py:511
  8.2 0.0 copy-start.3
  8.2 29.4 %ghosts.1 = (f32[16,2,16,128]{3,2,1,0:T(8,128)S(1)}, f32[2,5,16,128]{3,2,1,0:T(8,128)S(1)}, f32[2,5,8,128]{3,2,1,0:T(8,128)S(1)}) custom-call(f32[16,2,16,128]{3,2,1,0:T(8,128)S(1)} %get-tuple-element.13.a1, f32[2,16,8,128]{3,2,1,0:T(8,128)S(1)} %get-tuple-element.14.x1, f32[2,5,16,128]{3,2,1,0:T(8,128)S(1)} %get-tuple-element.15.rz, ...), custom_call_target="tpu_custom_call" | custom-call | tf_op jit(solution)/shard_map/ghosts/pallas_call | solution.py:524
  37.6 0.0 copy-done.1
  37.6 10.2 %fine_step.1 = (f32[5,2,32,1024]{3,2,1,0:T(8,128)}, f32[16,2,2,8,128]{4,3,2,1,0:T(8,128)S(1)}) custom-call(f32[5,2,32,1024]{3,2,1,0:T(8,128)S(1)} %copy-done.1, f32[16,2,16,128]{3,2,1,0:T(8,128)S(1)} %get-tuple-element.18.og), custom_call_target="tpu_custom_call" | custom-call | tf_op jit(solution)/shard_map/fine_step/pallas_call | solution.py:541
  47.8 19.4 %owners.1.oe = f32[16,5,8,128]{3,2,1,0:T(8,128)S(1)} custom-call(f32[16,2,2,8,128]{4,3,2,1,0:T(8,128)S(1)} %get-tuple-element.19.av, s32[1,96]{1,0:T(1,128)S(1)} %get-tuple-element.20.grid), custom_call_target="tpu_custom_call" | custom-call | tf_op jit(solution)/shard_map/owners/pallas_call | solution.py:557
  67.3 0.0 copy-done.3
  67.3 2.1 %coarse_step.1 = f32[5,16,8,128]{3,2,1,0:T(8,128)} custom-call(f32[5,16,8,128]{3,2,1,0:T(8,128)S(1)} %copy-done.3, f32[16,5,8,128]{3,2,1,0:T(8,128)S(1)} %owners.1.oe, f32[2,5,16,128]{3,2,1,0:T(8,128)S(1)} %get-tuple-element.21.oz, f32[2,5,8,128]{3,2,1,0:T(8,128)S(1)} %get-tuple-element.22.ocx, s32[1,96]{1,0:T(1,128)S(1)} %get-tuple-element.20.grid), custom_call_target="tpu_custom_call" | custom-call | tf_op jit(solution)/shard_map/coarse_step/pallas_call | solution.py:572
Async XLA Ops:
  1.4 1.3 %copy-start = (f32[5,2,32,1024]{3,2,1,0:T(8,128)S(1)}, f32[5,2,32,1024]{3,2,1,0:T(8,128)}, u32[]{:S(2)}) copy-start(f32[5,2,32,1024]{3,2,1,0:T(8,128)} %fine.3) | copy-start | bytes 3932164
  2.7 1.0 %copy-start.2 = (f32[5,16,8,128]{3,2,1,0:T(8,128)S(1)}, f32[5,16,8,128]{3,2,1,0:T(8,128)}, u32[]{:S(2)}) copy-start(f32[5,16,8,128]{3,2,1,0:T(8,128)} %coarse.3) | copy-start | bytes 983044
  3.7 0.7 copy-start.4
  4.3 33.3 %copy-start.1 = (f32[5,2,32,1024]{3,2,1,0:T(8,128)S(1)}, f32[5,2,32,1024]{3,2,1,0:T(8,128)}, u32[]{:S(2)}) copy-start(f32[5,2,32,1024]{3,2,1,0:T(8,128)} %fine.3) | copy-start | bytes 3932164
  8.2 59.1 %copy-start.3 = (f32[5,16,8,128]{3,2,1,0:T(8,128)S(1)}, f32[5,16,8,128]{3,2,1,0:T(8,128)}, u32[]{:S(2)}) copy-start(f32[5,16,8,128]{3,2,1,0:T(8,128)} %coarse.3) | copy-start | bytes 983044

commit v3 on v2

v3 whole, which is shorter than its diff:
```python
import jax
import jax.numpy as jnp
from jax import lax
from jax.experimental import pallas as pl
from jax.experimental.pallas import tpu as pltpu
from jax.sharding import PartitionSpec as P

F32 = jnp.float32
BF16 = jnp.bfloat16
I32 = jnp.int32
MESH = pl.DeviceIdType.MESH
NS = 8
NP = 16
GOFF = 16


def iota(shape, dim):
    return lax.broadcasted_iota(I32, shape, dim)


def dot3(x, m):
    hi = x.astype(BF16)
    r = x - hi.astype(F32)
    mid = r.astype(BF16)
    lo = (r - mid.astype(F32)).astype(BF16)
    d = lambda a: jnp.dot(a, m, preferred_element_type=F32)
    return d(hi) + (d(mid) + d(lo))


def moved(x, k):
    return pltpu.roll(x, k % 128, 1) if k % 128 else x


def ones_where(c):
    return jnp.where(c, 1.0, 0.0).astype(BF16)


def state(q):
    r = 1.0 / q[0]
    p = 0.4 * (q[4] - 0.5 * ((q[1] * q[1] + q[2] * q[2] + q[3] * q[3]) * r))
    c = jnp.sqrt(1.4 * p * r)
    return r, p, c


def flux(q, s, d):
    r, p, c = s
    u = q[1 + d] * r
    f = [q[1 + d], q[1] * u, q[2] * u, q[3] * u, (q[4] + p) * u]
    f[1 + d] = f[1 + d] + p
    return f, jnp.abs(u) + c


def rusanov(ql, fl, al, qr, fr, ar):
    a = 0.5 * jnp.maximum(al, ar)
    return [0.5 * (fl[v] + fr[v]) - a * (qr[v] - ql[v]) for v in range(5)]


N1 = NP - 1
S_X = N1
S_H = S_X + 2 * NP
S_G = S_H + 4
S_A = S_G + N1
S_E = S_A + N1
N_SEM = S_E + N1


def step_kernel(
    fine, coarse, ids, cols, fo, oe, oz, ocx, grid,
    nbr, fb, cb, a1, x1, rz, ct, pk, ba, bx, tb, dd, og, gh, bf, xg, xo, avs, av, bb, ee, big, chg, ss, rs, ls,
):
    s = lax.axis_index("slab")
    me = lax.axis_index("patch")
    half = lax.rem(me, 2)
    up = lax.rem(s + 1, NS)
    down = lax.rem(s + NS - 1, NS)
    peer = [lax.rem(me + d, NP) for d in range(NP)]
    loads = [pltpu.make_async_copy(fine.at[v], fb.at[v], ls.at[v]) for v in range(5)]
    loads.append(pltpu.make_async_copy(coarse, cb, ls.at[5]))
    barrier = pltpu.get_barrier_semaphore()
    for c in loads:
        c.start()
    for d in range(NP):
        if d:
            pl.semaphore_signal(barrier, inc=1, device_id=(s, peer[d]), device_id_type=MESH)
        pl.semaphore_signal(barrier, inc=1, device_id=(up, peer[d]), device_id_type=MESH)
        pl.semaphore_signal(barrier, inc=1, device_id=(down, peer[d]), device_id_type=MESH)

    def copy(k, src, dst, dev):
        return pltpu.make_async_remote_copy(
            src_ref=src, dst_ref=dst, send_sem=ss.at[k], recv_sem=rs.at[k],
            device_id=dev, device_id_type=MESH,
        )

    def place(t, _):
        n = ids[0, t]
        gy = cols[0, n]
        gz = cols[1, n]
        nbr[4, t] = gy
        nbr[5, t] = gz
        nbr[6, t] = gy + 8 * gz + GOFF
        return 0

    lax.fori_loop(0, 32, place, 0)
    for i in range(GOFF):
        grid[0, i] = jnp.int32(-1)

    def find(k, _):
        q = jnp.int32(-1)
        for t in range(32):
            q = jnp.where(nbr[6, t] == k, t, q)
        grid[0, k] = q
        return 0

    lax.fori_loop(GOFF, GOFF + 48, find, 0)
    for i in range(GOFF + 48, 96):
        grid[0, i] = jnp.int32(-1)

    def look(t, _):
        for g, step in enumerate((-1, 1, -8, 8)):
            nbr[g, t] = grid[0, nbr[6, t] + step]
        return 0

    lax.fori_loop(0, 32, look, 0)

    k = iota((1024, 128), 0)
    c = iota((1024, 128), 1)
    g = c // 32
    i = lax.rem(c, 32)
    want = jnp.where(g == 0, 32 * i + 31, jnp.where(g == 1, 32 * i, jnp.where(g == 2, 992 + i, i)))
    sel = ones_where(k == want)
    for v in range(5):
        loads[v].wait()
        for p in range(2):
            pk[p, v] = dot3(fb[v, p], sel)
            for xr in range(2):
                a1[:, p, 5 * xr + v, :] = pk[p, v, pl.ds(xr, 16, 2), :]
    lane = iota((5, 128), 1)
    tag = jnp.where(iota((3, 128), 1) < 64, ids[0, 2 * me], ids[0, 2 * me + 1]).astype(F32)
    for d, row in ((0, 0), (1, 31)):
        for j in range(8):
            t0 = fb[:, 0, row, 128 * j : 128 * j + 128]
            t1 = fb[:, 1, row, 128 * j : 128 * j + 128]
            xo[:, d, 128 * j : 128 * j + 128] = t0
            xo[:, 2 + d, 128 * j : 128 * j + 128] = t1
            x1[d, 2 * j, 0:5, :] = jnp.where(lane < 64, t0, pltpu.roll(t1, 64, 1))
            x1[d, 2 * j + 1, 0:5, :] = jnp.where(lane < 64, pltpu.roll(t0, 64, 1), t1)
            x1[d, 2 * j, 5:8, :] = tag
            x1[d, 2 * j + 1, 5:8, :] = tag
    loads[5].wait()
    for v in range(5):
        for z in range(8):
            ct[z, 16 * v : 16 * v + 16, :] = cb[v, :, z, :]
    y = iota((128, 128), 0)
    k = iota((128, 128), 1) // 8
    plane = jnp.where(k < 6, 16 * (k + 1) - 1, jnp.where(k < 12, 16 * (k - 4), -1))
    sel = ones_where(y == plane)
    lane8 = lax.rem(iota((80, 128), 1), 8)
    acc = jnp.zeros((80, 128), F32)
    for z in range(8):
        acc = jnp.where(lane8 == z, dot3(ct[z], sel), acc)
    first = ct[0]
    last = ct[7]
    own = jnp.where(half == 0, first, last)
    for v in range(5):
        cut = slice(16 * v, 16 * v + 16)
        a1[:, 0, 10 + v, :] = acc[cut]
        a1[:, 1, 10 + v, :] = own[cut]
        rz[0, v] = first[cut]
        rz[1, v] = last[cut]
    a1[:, 0, 15, :] = jnp.zeros((16, 128), F32)
    a1[:, 1, 15, :] = jnp.zeros((16, 128), F32)

    pl.semaphore_wait(barrier, 3 * NP - 1)
    one = []
    two = []
    for d in range(NP):
        j = peer[d]
        if d:
            one.append(copy(d - 1, a1.at[j], ba.at[pl.ds(2 * me, 2)], (s, j)))
            one[-1].start()
        for c in (
            copy(S_X + 2 * d, x1.at[0, j], bx.at[1, me], (down, j)),
            copy(S_X + 2 * d + 1, x1.at[1, j], bx.at[0, me], (up, j)),
        ):
            c.start()
            one.append(c)
    two = [
        copy(S_H, cb.at[:, 0], ocx.at[1], (down, me)),
        copy(S_H + 1, cb.at[:, 15], ocx.at[0], (up, me)),
        copy(S_H + 2, rz.at[1], oz.at[0], (s, peer[1])),
        copy(S_H + 3, rz.at[0], oz.at[1], (s, peer[N1])),
    ]
    for c in two:
        c.start()
    own = pltpu.make_async_copy(a1.at[me], ba.at[pl.ds(2 * me, 2)], ls.at[6])
    own.start()

    src = iota((1024, 256), 0)
    dst = iota((1024, 256), 1)
    zz = 8 * (dst // 128) + 7 - lax.rem(dst, 128) // 16
    pair = ones_where((src // 64 == zz) & (lax.rem(src, 32) // 2 == lax.rem(dst, 16)))

    def interior(p):
        def along_x(j, _):
            cut = pl.ds(pl.multiple_of(128 * j, 128), 128)
            q = [fb[v, p, :, cut] for v in range(5)]
            f, a = flux(q, state(q), 0)
            nxt = lambda t: pltpu.roll(t, 31, 0)
            hi = rusanov(q, f, a, [nxt(t) for t in q], [nxt(t) for t in f], nxt(a))
            inner = iota((32, 128), 0) < 31
            for v in range(5):
                t = jnp.where(inner, hi[v], 0.0)
                chg[v, :, cut] = t - pltpu.roll(t, 1, 0)
            return 0

        lax.fori_loop(0, 8, along_x, 0)

        def rows(c, _):
            cut = pl.ds(pl.multiple_of(8 * c, 8), 8)
            q = [fb[v, p, cut, :] for v in range(5)]
            st = state(q)
            l8 = iota((8, 1024), 1)
            change = [chg[v, cut, :] for v in range(5)]
            for way, shift, inner in ((2, 32, l8 < 992), (1, 1, (l8 & 31) < 31)):
                f, a = flux(q, st, way)
                nxt = lambda t: pltpu.roll(t, 1024 - shift, 1)
                hi = rusanov(q, f, a, [nxt(t) for t in q], [nxt(t) for t in f], nxt(a))
                for v in range(5):
                    t = jnp.where(inner, hi[v], 0.0)
                    change[v] = change[v] + (t - pltpu.roll(t, shift, 1))
            for v in range(5):
                fo[v, p, cut, :] = q[v] - 0.1 * change[v]
            return 0

        lax.fori_loop(0, 4, rows, 0)
        for v in range(5):
            m = dot3(fo[v, p], pair)
            for h in range(2):
                big[h, 0:32, :] = m[:, 128 * h : 128 * h + 128]
                avs[p, v, h] = 0.125 * (big[h, pl.ds(0, 16, 2), :] + big[h, pl.ds(1, 16, 2), :])

    interior(0)
    src = iota((128, 128), 0)
    dst = iota((128, 128), 1)
    g = dst // 32
    i = lax.rem(dst, 32) // 2
    base = jnp.where(g == 0, 0, jnp.where(g == 1, 48, jnp.where(g == 2, 64, 80)))
    spread = ones_where(src == base + i)
    own.wait()
    for c in one:
        c.wait()

    def tags(i, _):
        for way in range(2):
            t = bx[way, i]
            tb[way, 2 * i] = t
            tb[way, 2 * i + 1] = pltpu.roll(t, 64, 1)
        return 0

    lax.fori_loop(0, NP, tags, 0)
    lane = iota((8, 128), 1)
    group = iota((10, 128), 1) // 32

    def select(j):
        nn = jnp.where(iota((1, 128), 1) < 64, ids[0, 2 * j], ids[0, 2 * j + 1]).astype(F32)
        for p in range(2):
            slot = 2 * j + p
            gy = nbr[4, slot]
            gz = nbr[5, slot]
            a = 4 * (gz + 1)
            r0 = pltpu.roll(ba[a, 8:16, :], (128 - 8 * gy) & 127, 1)
            r1 = pltpu.roll(ba[a + 2, 8:16, :], (136 - 8 * gy) & 127, 1)
            r2 = pltpu.roll(ba[4 * gz + 3, 8:16, :], (176 - 16 * gy) & 127, 1)
            r3 = pltpu.roll(ba[4 * gz + 9, 8:16, :], (192 - 16 * gy) & 127, 1)
            c = jnp.where(lane < 64, jnp.where((lane & 8) == 0, r0, r1), jnp.where(lane < 80, r2, r3))
            c = dot3(c, spread)[2:7]
            val = jnp.concatenate([c, c], axis=0)
            for g in range(4):
                q = nbr[g, slot]
                val = jnp.where((group == g) & (q >= 0), ba[jnp.maximum(q, 0), 0:10, :], val)
            dd[j, p, 0:10, :] = val
            acc = jnp.zeros((5, 128), F32)
            for i in range(2 * NP):
                acc = jnp.where(tb[p, i, 5:6, :] == nn, tb[p, i, 0:5, :], acc)
            dd[j, p, 10:15, :] = acc
            dd[j, p, 15:16, :] = jnp.zeros((1, 128), F32)

    def selected(d):
        j = lax.rem(me + d, NP)
        return copy(S_G + d - 1, dd.at[j], og.at[me], (s, j))

    def select_send(d, _):
        select(lax.rem(me + d, NP))
        selected(d).start()
        return 0

    lax.fori_loop(1, NP, select_send, 0)
    select(me)
    own = pltpu.make_async_copy(dd.at[me], og.at[me], ls.at[6])
    own.start()
    interior(1)

    src = iota((128, 256), 0)
    dst = iota((128, 256), 1)
    g = src // 32
    i = lax.rem(src, 32) // 2
    zz = 8 * (dst // 128) + 7 - lax.rem(dst, 128) // 16
    yy = lax.rem(dst, 16)
    far = 15 * (g & 1)
    hit = (zz == jnp.where(g < 2, i, far)) & (yy == jnp.where(g < 2, far, i))
    sign = jnp.where((g & 1) == 0, -1.0, 1.0)
    mean_of = jnp.where(hit, sign, 0.0).astype(BF16)
    src = iota((128, 128), 0)
    dst = iota((128, 128), 1)
    g = src // 32
    i = lax.rem(src, 32) // 2
    z_at = 64 * (i // 8) + 7 - lax.rem(i, 8)
    at = jnp.where(g == 0, z_at, jnp.where(g == 1, z_at + 17, jnp.where(g == 2, 96 + i, 32 + i)))
    reflux = ones_where(dst == at)
    l1 = iota((1, 128), 1)
    low = ((l1 & 63) < 8) | (l1 >= 96)
    coef = jnp.where(low, -0.05, 0.05).astype(F32) * 0.25
    src = iota((128, 1024), 0)
    dst = iota((128, 1024), 1)
    g = src // 32
    i = lax.rem(src, 32)
    at = jnp.where(g == 0, 32 * i, jnp.where(g == 1, 32 * i + 31, jnp.where(g == 2, i, 992 + i)))
    sign = jnp.where((g & 1) == 0, -1.0, 1.0)
    expand = jnp.where(dst == at, sign, 0.0).astype(BF16)
    own.wait()
    for d in range(1, NP):
        two.append(selected(d))
    for c in two:
        c.wait()

    g1 = iota((32, 128), 1)
    low = ((g1 // 32) & 1) == 0
    isy = g1 < 64

    def face_flux(q):
        r, pr, c = state(q)
        mn = jnp.where(isy, q[2], q[3])
        u = mn * r
        py = jnp.where(isy, pr, 0.0)
        f = [mn, q[1] * u, q[2] * u + py, q[3] * u + (pr - py), (q[4] + pr) * u]
        return f, jnp.abs(u) + c

    for p in range(2):
        for v in range(5):
            for xr in range(2):
                gh[v, pl.ds(xr, 16, 2), :] = og[:, p, 5 * xr + v, :]
        theirs = [gh[v] for v in range(5)]
        mine = [jnp.where(low, pltpu.roll(pk[p, v], 96, 1), pltpu.roll(pk[p, v], 32, 1)) for v in range(5)]
        ql = [jnp.where(low, theirs[v], mine[v]) for v in range(5)]
        qr = [jnp.where(low, mine[v], theirs[v]) for v in range(5)]
        fl, al = face_flux(ql)
        fr, ar = face_flux(qr)
        f = rusanov(ql, fl, al, qr, fr, ar)
        for v in range(5):
            bf[160 * p + 32 * v : 160 * p + 32 * v + 32, :] = f[v]
    l5 = iota((5, 128), 1)
    for way in range(2):
        for j in range(8):
            e = og[2 * j, way, 10:15, :]
            o = og[2 * j + 1, way, 10:15, :]
            cut = slice(128 * j, 128 * j + 128)
            xg[:, way, cut] = jnp.where(l5 < 64, e, pltpu.roll(o, 64, 1))
            xg[:, 2 + way, cut] = jnp.where(l5 < 64, pltpu.roll(e, 64, 1), o)
    row = iota((4, 1024), 0)
    low = (row & 1) == 0
    edge = (row & 1) == jnp.where(s == 0, 0, jnp.where(s == NS - 1, 1, 2))
    mine = [xo[v] for v in range(5)]
    theirs = [jnp.where(edge, mine[v], xg[v]) for v in range(5)]
    ql = [jnp.where(low, theirs[v], mine[v]) for v in range(5)]
    qr = [jnp.where(low, mine[v], theirs[v]) for v in range(5)]
    fl, al = flux(ql, state(ql), 0)
    fr, ar = flux(qr, state(qr), 0)
    f = rusanov(ql, fl, al, qr, fr, ar)
    for v in range(5):
        xg[v] = jnp.where(low, -f[v], f[v])
    fluxes = bf[...]
    m = dot3(fluxes, mean_of)
    big[0] = m[:, 0:128]
    big[1] = m[:, 128:256]
    big[2] = dot3(fluxes, reflux)
    l16 = iota((16, 128), 1)
    for p in range(2):
        yr = [jnp.zeros((16, 128), F32)] * 2
        zr = [jnp.zeros((16, 128), F32)] * 2
        for v in range(5):
            a = 160 * p + 32 * v
            t = [big[h, pl.ds(a, 16, 2), :] + big[h, pl.ds(a + 1, 16, 2), :] for h in range(3)]
            xm = dot3(xg[v, 2 * p : 2 * p + 2, :], pair)
            sub = iota((16, 128), 0)
            w = t[2] * coef
            for h in range(2):
                xh = xm[:, 128 * h : 128 * h + 128]
                fix = t[h] + jnp.where(sub == 0, xh[0:1], jnp.where(sub == 15, xh[1:2], 0.0))
                av[:, h, p, v, :] = avs[p, v, h] - 0.0125 * fix
                yr[h] = jnp.where((l16 >= 25 * v) & (l16 < 25 * v + 25), moved(w, 25 * v - 64 * h), yr[h])
                zr[h] = jnp.where(l16 // 16 == v, moved(w, 16 * v - 64 * h - 32), zr[h])
        for h in range(2):
            av[:, h, p, 5, :] = yr[h]
            av[:, h, p, 6, :] = zr[h]
            av[:, h, p, 7, :] = jnp.zeros((16, 128), F32)
    one = []
    for d in range(1, NP):
        one.append(copy(S_A + d - 1, av.at[peer[d]], bb.at[me], (s, peer[d])))
        one[-1].start()
    own = pltpu.make_async_copy(av.at[me], bb.at[me], ls.at[6])
    own.start()
    for p in range(2):
        for v in range(5):
            a = 160 * p + 32 * v
            fo[v, p] = fo[v, p] - 0.1 * dot3(bf[a : a + 32, :], expand)
            for way, x in ((0, 0), (1, 31)):
                fo[v, p, x : x + 1, :] = fo[v, p, x : x + 1, :] - 0.1 * xg[v, 2 * p + way : 2 * p + way + 1, :]
    lane = iota((8, 128), 1)
    sub = iota((8, 128), 0)
    block = lane // 16
    own.wait()
    for c in one:
        c.wait()

    def expand_to(j):
        h = lax.rem(j, 2)
        r = j // 2
        far = r - 2 + 2 * h
        val = [jnp.zeros((8, 128), F32)] * 5
        add = [jnp.zeros((8, 128), F32)] * 5
        covered = jnp.zeros((8, 128), F32)
        for gy in range(6):
            a = grid[0, gy + 8 * (r - 1) + GOFF]
            b = grid[0, gy + 8 * far + GOFF]
            a0 = jnp.maximum(a, 0)
            b0 = jnp.maximum(b, 0)
            t = bb[a0 // 2, h, a0 & 1]
            zt = bb[b0 // 2, h, b0 & 1, 6:7, :]
            ina = (block == gy + 1) & (a >= 0)
            inb = (block == gy + 1) & (sub == 7 * h) & (b >= 0)
            iny = ((lane == 16 * gy + 15) | (lane == 16 * gy + 32)) & (a >= 0)
            covered = jnp.where(ina, 1.0, covered)
            yt = pltpu.roll(jnp.broadcast_to(t[5:6], (8, 128)), 0, 1, stride=1, stride_axis=0)
            zt = jnp.broadcast_to(zt, (8, 128))
            for v in range(5):
                w = jnp.broadcast_to(t[v : v + 1], (8, 128))
                w = moved(pltpu.roll(w, 0, 1, stride=16, stride_axis=0), 16 * gy + 32)
                val[v] = jnp.where(ina, w, val[v])
                add[v] = jnp.where(iny, add[v] + moved(yt, 16 * gy + 8 - 25 * v), add[v])
                add[v] = jnp.where(inb, add[v] + moved(zt, 16 * gy + 16 - 16 * v), add[v])
        for v in range(5):
            ee[j, v] = jnp.where(covered > 0, val[v], add[v])

    def expanded(d):
        j = lax.rem(me + d, NP)
        return copy(S_E + d - 1, ee.at[j], oe.at[me], (s, j))

    def expand_send(d, _):
        expand_to(lax.rem(me + d, NP))
        expanded(d).start()
        return 0

    lax.fori_loop(1, NP, expand_send, 0)
    expand_to(me)
    own = pltpu.make_async_copy(ee.at[me], oe.at[me], ls.at[6])
    own.start()
    own.wait()
    for d in range(1, NP):
        expanded(d).wait()


def coarse_kernel(coarse, oe, oz, ocx, grid, fo, out, fine_out, sem):
    done = pltpu.make_async_copy(fo, fine_out, sem)
    done.start()
    s = lax.axis_index("slab")
    me = lax.axis_index("patch")
    r = me // 2
    h = lax.rem(me, 2)
    lane = iota((8, 128), 1)
    sub = iota((8, 128), 0)
    blocks = lane // 16

    def cover(row):
        m = jnp.zeros((8, 128), F32)
        for gy in range(6):
            m = jnp.where((blocks == gy + 1) & (grid[0, gy + 8 * (row - 1) + GOFF] >= 0), 1.0, m)
        return m

    mid = cover(r)
    below = jnp.where(h == 0, cover(r - 1), mid)
    above = jnp.where(h == 1, cover(r + 1), mid)
    free = 1.0 - mid
    fup = free * (1.0 - pltpu.roll(mid, 127, 1))
    flo = free * (1.0 - pltpu.roll(mid, 1, 1))
    zlo = free * (1.0 - jnp.where(sub == 0, below, mid))
    zhi = free * (1.0 - jnp.where(sub == 7, above, mid))

    def cells(x):
        q = [coarse[v, x] for v in range(5)]
        st = state(q)
        return q, st, flux(q, st, 0)

    def face(a, b):
        return rusanov(a[0], a[2][0], a[2][1], b[0], b[2][0], b[2][1])

    first = cells(0)
    q = [jnp.where(s == 0, coarse[v, 0], ocx[0, v]) for v in range(5)]
    st = state(q)
    lower = face((q, st, flux(q, st, 0)), first)
    here = first
    for x in range(16):
        if x < 15:
            there = cells(x + 1)
        else:
            q = [jnp.where(s == NS - 1, coarse[v, 15], ocx[1, v]) for v in range(5)]
            st = state(q)
            there = (q, st, flux(q, st, 0))
        upper = face(here, there)
        q, st, _ = here
        change = [(upper[v] - lower[v]) * free for v in range(5)]
        row = slice(x, x + 1)
        zn = [jnp.where(sub == 7, jnp.where(me == NP - 1, q[v], oz[1, v, row, :]), pltpu.roll(q[v], 7, 0)) for v in range(5)]
        zb = [jnp.where(sub == 0, jnp.where(me == 0, q[v], oz[0, v, row, :]), pltpu.roll(q[v], 1, 0)) for v in range(5)]
        f, a = flux(q, st, 2)
        fn, an = flux(zn, state(zn), 2)
        fb, ab = flux(zb, state(zb), 2)
        up = rusanov(q, f, a, zn, fn, an)
        lo = rusanov(zb, fb, ab, q, f, a)
        change = [change[v] + (up[v] * zhi - lo[v] * zlo) for v in range(5)]
        f, a = flux(q, st, 1)
        nxt = lambda t: jnp.where(lane == 127, t, pltpu.roll(t, 127, 1))
        prv = lambda t: jnp.where(lane == 0, t, pltpu.roll(t, 1, 1))
        up = rusanov(q, f, a, [nxt(t) for t in q], [nxt(t) for t in f], nxt(a))
        lo = rusanov([prv(t) for t in q], [prv(t) for t in f], prv(a), q, f, a)
        for v in range(5):
            prov = q[v] - 0.05 * (change[v] + (up[v] * fup - lo[v] * flo))
            e = oe[x, v]
            out[v, x] = jnp.where(mid > 0, e, prov + e)
        here = there
        lower = upper
    done.wait()


def vm():
    return pl.BlockSpec(memory_space=pltpu.VMEM)


def sm():
    return pl.BlockSpec(memory_space=pltpu.SMEM)


def hb():
    return pl.BlockSpec(memory_space=pltpu.HBM)


def sds(*shape, dtype=F32):
    return jax.ShapeDtypeStruct(shape, dtype)


def buf(*shape):
    return pltpu.VMEM(shape, F32)


LIMIT = 48 << 20


def local(coarse, fine, columns, patch_ids):
    fo, oe, oz, ocx, grid = pl.pallas_call(
        step_kernel,
        out_shape=(
            sds(5, 2, 32, 1024), sds(16, 5, 8, 128), sds(2, 5, 16, 128), sds(2, 5, 8, 128), sds(1, 96, dtype=I32),
        ),
        in_specs=[hb(), hb(), sm(), sm()],
        out_specs=(vm(), vm(), vm(), vm(), sm()),
        scratch_shapes=[
            pltpu.SMEM((7, 32), I32),
            buf(5, 2, 32, 1024),
            buf(5, 16, 8, 128),
            buf(16, 2, 16, 128),
            buf(2, 16, 8, 128),
            buf(2, 5, 16, 128),
            buf(8, 80, 128),
            buf(2, 5, 32, 128),
            buf(32, 16, 128),
            buf(2, 16, 8, 128),
            buf(2, 32, 8, 128),
            buf(16, 2, 16, 128),
            buf(16, 2, 16, 128),
            buf(5, 32, 128),
            buf(320, 128),
            buf(5, 4, 1024),
            buf(5, 4, 1024),
            buf(2, 5, 2, 16, 128),
            buf(16, 2, 2, 8, 128),
            buf(16, 2, 2, 8, 128),
            buf(16, 5, 8, 128),
            buf(3, 320, 128),
            buf(5, 32, 1024),
            pltpu.SemaphoreType.DMA((N_SEM,)),
            pltpu.SemaphoreType.DMA((N_SEM,)),
            pltpu.SemaphoreType.DMA((7,)),
        ],
        compiler_params=pltpu.CompilerParams(collective_id=0, has_side_effects=True, vmem_limit_bytes=LIMIT),
        name="step",
    )(fine, coarse, patch_ids, columns.T)
    return pl.pallas_call(
        coarse_kernel,
        out_shape=(sds(5, 16, 8, 128), sds(5, 2, 32, 1024)),
        in_specs=[vm(), vm(), vm(), vm(), sm(), pl.BlockSpec(memory_space=pl.ANY)],
        out_specs=(vm(), hb()),
        scratch_shapes=[pltpu.SemaphoreType.DMA],
        compiler_params=pltpu.CompilerParams(vmem_limit_bytes=LIMIT),
        name="coarse_step",
    )(coarse, oe, oz, ocx, grid, fo)


def solution(mesh):
    return jax.shard_map(
        local,
        mesh=mesh,
        in_specs=(
            P(None, "slab", "patch", None),
            P(None, ("slab", "patch"), None, None),
            P(),
            P("slab", None),
        ),
        out_specs=(P(None, "slab", "patch", None), P(None, ("slab", "patch"), None, None)),
        check_vma=False,
    )
```

time: 69.6 us -> 53.6 us (0.77)
  the two profiles are of different devices: /device:TPU:0 before, /device:TPU:2 now
where the time goes in v3:
time: 53.6 us; the launch traced here: 52.6 us
  Pallas kernels  48.4 us (90%)
  local copies, waits for them, and re-layouts  3.61 us (7%)
  between operations  0.65 us (1%)
    pallas_call x1, Pallas kernels, local(): pl.pallas_call(step_kernel, out_shape=(sds(5, 2, 32, 1024), sds(16, 5, 8,...  45.3 us
    unnamed x8, local copies, waits for them, and re-layouts  3.61 us
    pallas_call x1, Pallas kernels, local(): pl.pallas_call(coarse_kernel, out_shape=(sds(5, 16, 8, 128), sds(5, 2, 32...  3.03 us

profile of v3, /device:TPU:2, one launch (start us, length us, event | category | flops | bytes accessed | tf_op | source)
XLA Modules:
  0.0 52.6 jit_solution(13362286730242343619)
XLA Ops:
  0.6 0.0 copy-start
  0.6 1.0 %copy-done = f32[5,16,8,128]{3,2,1,0:T(8,128)S(1)} copy-done((f32[5,16,8,128]{3,2,1,0:T(8,128)S(1)}, f32[5,16,8,128]{3,2,1,0:T(8,128)}, u32[]{:S(2)}) %copy-start) | copy-done | bytes 327704
  1.6 0.0 copy-start.1
  1.6 1.3 %copy-done.1 = f32[5,2,32,1024]{3,2,1,0:T(8,128)S(1)} copy-done((f32[5,2,32,1024]{3,2,1,0:T(8,128)S(1)}, f32[5,2,32,1024]{3,2,1,0:T(8,128)}, u32[]{:S(2)}) %copy-start.1) | copy-done | bytes 1310744
  2.9 0.0 copy-start.2
  2.9 0.7 %copy-done.2 = s32[32,2]{0,1:T(2,128)S(1)} copy-done((s32[32,2]{0,1:T(2,128)S(1)}, s32[32,2]{0,1:T(2,128)}, u32[]{:S(2)}) %copy-start.2) | copy-done | bytes 280
  3.6 0.0 copy-start.3
  3.6 0.7 %copy-done.3 = s32[1,32]{1,0:T(1,128)S(1)} copy-done((s32[1,32]{1,0:T(1,128)S(1)}, s32[1,32]{1,0:T(1,128)}, u32[]{:S(2)}) %copy-start.3) | copy-done | bytes 152
  4.3 45.3 %step.1 = (f32[5,2,32,1024]{3,2,1,0:T(8,128)S(1)}, f32[16,5,8,128]{3,2,1,0:T(8,128)S(1)}, f32[2,5,16,128]{3,2,1,0:T(8,128)S(1)}, f32[2,5,8,128]{3,2,1,0:T(8,128)S(1)}, s32[1,96]{1,0:T(1,128)S(1)}) custom-call(f32[5,2,32,1024]{3,2,1,0:T(8,128)S(1)} %copy-done.1, f32[5,16,8,128]{3,2,1,0:T(8,128)S(1)} %copy-done, s32[1,32]{1,0:T(1,128)S(1)} %copy-done.3, ...), custom_call_target="tpu_custom_call" | custom-call | tf_op jit(solution)/shard_map/step/pallas_call | solution.py:568
  49.6 3.0 %coarse_step.1 = (f32[5,16,8,128]{3,2,1,0:T(8,128)}, f32[5,2,32,1024]{3,2,1,0:T(8,128)}) custom-call(f32[5,16,8,128]{3,2,1,0:T(8,128)S(1)} %copy-done, f32[16,5,8,128]{3,2,1,0:T(8,128)S(1)} %get-tuple-element.7.oe, f32[2,5,16,128]{3,2,1,0:T(8,128)S(1)} %get-tuple-element.8.oz, f32[2,5,8,128]{3,2,1,0:T(8,128)S(1)} %get-tuple-element.9.ocx, ...), custom_call_target="tpu_custom_call" | custom-call | tf_op jit(solution)/shard_map/coarse_step/pallas_call | solution.py:606
Async XLA Ops:
  0.6 1.0 %copy-start = (f32[5,16,8,128]{3,2,1,0:T(8,128)S(1)}, f32[5,16,8,128]{3,2,1,0:T(8,128)}, u32[]{:S(2)}) copy-start(f32[5,16,8,128]{3,2,1,0:T(8,128)} %coarse.3) | copy-start | bytes 983044
  1.6 1.3 %copy-start.1 = (f32[5,2,32,1024]{3,2,1,0:T(8,128)S(1)}, f32[5,2,32,1024]{3,2,1,0:T(8,128)}, u32[]{:S(2)}) copy-start(f32[5,2,32,1024]{3,2,1,0:T(8,128)} %fine.1) | copy-start | bytes 3932164
  2.9 0.7 %copy-start.2 = (s32[32,2]{0,1:T(2,128)S(1)}, s32[32,2]{0,1:T(2,128)}, u32[]{:S(2)}) copy-start(s32[32,2]{0,1:T(2,128)} %param.6) | copy-start | bytes 772
  3.6 0.7 %copy-start.3 = (s32[1,32]{1,0:T(1,128)S(1)}, s32[1,32]{1,0:T(1,128)}, u32[]{:S(2)}) copy-start(s32[1,32]{1,0:T(1,128)} %ids.1) | copy-start | bytes 388

commit v4 on v3

--- a/solution.py
+++ b/solution.py
@@ -27,6 +27,15 @@
     return d(hi) + (d(mid) + d(lo))
 
 
+def dot3_left(m, x):
+    hi = x.astype(BF16)
+    r = x - hi.astype(F32)
+    mid = r.astype(BF16)
+    lo = (r - mid.astype(F32)).astype(BF16)
+    d = lambda a: jnp.dot(m, a, preferred_element_type=F32)
+    return d(hi) + (d(mid) + d(lo))
+
+
 def moved(x, k):
     return pltpu.roll(x, k % 128, 1) if k % 128 else x
 
@@ -53,6 +62,72 @@
 def rusanov(ql, fl, al, qr, fr, ar):
     a = 0.5 * jnp.maximum(al, ar)
     return [0.5 * (fl[v] + fr[v]) - a * (qr[v] - ql[v]) for v in range(5)]
+
+
+def provisional(s, me, coarse, oz, ocx, grid, prov):
+    r = me // 2
+    h = lax.rem(me, 2)
+    lane = iota((8, 128), 1)
+    sub = iota((8, 128), 0)
+    blocks = lane // 16
+
+    def cover(row):
+        m = jnp.zeros((8, 128), F32)
+        for gy in range(6):
+            m = jnp.where((blocks == gy + 1) & (grid[0, gy + 8 * (row - 1) + GOFF] >= 0), 1.0, m)
+        return m
+
+    mid = cover(r)
+    below = jnp.where(h == 0, cover(r - 1), mid)
+    above = jnp.where(h == 1, cover(r + 1), mid)
+    free = 1.0 - mid
+    fup = free * (1.0 - pltpu.roll(mid, 127, 1))
+    flo = free * (1.0 - pltpu.roll(mid, 1, 1))
+    zlo = free * (1.0 - jnp.where(sub == 0, below, mid))
+    zhi = free * (1.0 - jnp.where(sub == 7, above, mid))
+
+    def cells(x):
+        q = [coarse[v, x] for v in range(5)]
+        st = state(q)
+        return q, st, flux(q, st, 0)
+
+    def face(a, b):
+        return rusanov(a[0], a[2][0], a[2][1], b[0], b[2][0], b[2][1])
+
+    first = cells(0)
+    q = [jnp.where(s == 0, coarse[v, 0], ocx[0, v]) for v in range(5)]
+    st = state(q)
+    lower = face((q, st, flux(q, st, 0)), first)
+    here = first
+    for x in range(16):
+        if x < 15:
+            there = cells(x + 1)
+        else:
+            q = [jnp.where(s == NS - 1, coarse[v, 15], ocx[1, v]) for v in range(5)]
+            st = state(q)
+            there = (q, st, flux(q, st, 0))
+        upper = face(here, there)
+        q, st, _ = here
+        change = [(upper[v] - lower[v]) * free for v in range(5)]
+        row = slice(x, x + 1)
+        zn = [jnp.where(sub == 7, jnp.where(me == NP - 1, q[v], oz[1, v, row, :]), pltpu.roll(q[v], 7, 0)) for v in range(5)]
+        zb = [jnp.where(sub == 0, jnp.where(me == 0, q[v], oz[0, v, row, :]), pltpu.roll(q[v], 1, 0)) for v in range(5)]
+        f, a = flux(q, st, 2)
+        fn, an = flux(zn, state(zn), 2)
+        fb, ab = flux(zb, state(zb), 2)
+        up = rusanov(q, f, a, zn, fn, an)
+        lo = rusanov(zb, fb, ab, q, f, a)
+        change = [change[v] + (up[v] * zhi - lo[v] * zlo) for v in range(5)]
+        f, a = flux(q, st, 1)
+        nxt = lambda t: jnp.where(lane == 127, t, pltpu.roll(t, 127, 1))
+        prv = lambda t: jnp.where(lane == 0, t, pltpu.roll(t, 1, 1))
+        up = rusanov(q, f, a, [nxt(t) for t in q], [nxt(t) for t in f], nxt(a))
+        lo = rusanov([prv(t) for t in q], [prv(t) for t in f], prv(a), q, f, a)
+        for v in range(5):
+            prov[v, x] = q[v] - 0.05 * (change[v] + (up[v] * fup - lo[v] * flo))
+        here = there
+        lower = upper
+    return mid
 
 
 N1 = NP - 1
@@ -65,8 +140,9 @@
 
 
 def step_kernel(
-    fine, coarse, ids, cols, fo, oe, oz, ocx, grid,
-    nbr, fb, cb, a1, x1, rz, ct, pk, ba, bx, tb, dd, og, gh, bf, xg, xo, avs, av, bb, ee, big, chg, ss, rs, ls,
+    fine, coarse, ids, cols, fo, co,
+    nbr, grid, fb, cb, fs, a1, x1, rz, ct, pk, ba, bx, cg, dd, og, oz, ocx,
+    gh, bf, xg, xo, avs, av, bb, ee, oe, big, chg, prov, ss, rs, ls,
 ):
     s = lax.axis_index("slab")
     me = lax.axis_index("patch")
@@ -90,37 +166,6 @@
             src_ref=src, dst_ref=dst, send_sem=ss.at[k], recv_sem=rs.at[k],
             device_id=dev, device_id_type=MESH,
         )
-
-    def place(t, _):
-        n = ids[0, t]
-        gy = cols[0, n]
-        gz = cols[1, n]
-        nbr[4, t] = gy
-        nbr[5, t] = gz
-        nbr[6, t] = gy + 8 * gz + GOFF
-        return 0
-
-    lax.fori_loop(0, 32, place, 0)
-    for i in range(GOFF):
-        grid[0, i] = jnp.int32(-1)
-
-    def find(k, _):
-        q = jnp.int32(-1)
-        for t in range(32):
-            q = jnp.where(nbr[6, t] == k, t, q)
-        grid[0, k] = q
-        return 0
-
-    lax.fori_loop(GOFF, GOFF + 48, find, 0)
-    for i in range(GOFF + 48, 96):
-        grid[0, i] = jnp.int32(-1)
-
-    def look(t, _):
-        for g, step in enumerate((-1, 1, -8, 8)):
-            nbr[g, t] = grid[0, nbr[6, t] + step]
-        return 0
-
-    lax.fori_loop(0, 32, look, 0)
 
     k = iota((1024, 128), 0)
     c = iota((1024, 128), 1)
@@ -195,6 +240,37 @@
     own = pltpu.make_async_copy(a1.at[me], ba.at[pl.ds(2 * me, 2)], ls.at[6])
     own.start()
 
+    def place(t, _):
+        n = ids[0, t]
+        gy = cols[0, n]
+        gz = cols[1, n]
+        nbr[4, t] = gy
+        nbr[5, t] = gz
+        nbr[6, t] = gy + 8 * gz + GOFF
+        return 0
+
+    lax.fori_loop(0, 32, place, 0)
+    for i in range(GOFF):
+        grid[0, i] = jnp.int32(-1)
+
+    def find(k, _):
+        q = jnp.int32(-1)
+        for t in range(32):
+            q = jnp.where(nbr[6, t] == k, t, q)
+        grid[0, k] = q
+        return 0
+
+    lax.fori_loop(GOFF, GOFF + 48, find, 0)
+    for i in range(GOFF + 48, 96):
+        grid[0, i] = jnp.int32(-1)
+
+    def look(t, _):
+        for g, step in enumerate((-1, 1, -8, 8)):
+            nbr[g, t] = grid[0, nbr[6, t] + step]
+        return 0
+
+    lax.fori_loop(0, 32, look, 0)
+
     src = iota((1024, 256), 0)
     dst = iota((1024, 256), 1)
     zz = 8 * (dst // 128) + 7 - lax.rem(dst, 128) // 16
@@ -229,12 +305,12 @@
                     t = jnp.where(inner, hi[v], 0.0)
                     change[v] = change[v] + (t - pltpu.roll(t, shift, 1))
             for v in range(5):
-                fo[v, p, cut, :] = q[v] - 0.1 * change[v]
+                fs[v, p, cut, :] = q[v] - 0.1 * change[v]
             return 0
 
         lax.fori_loop(0, 4, rows, 0)
         for v in range(5):
-            m = dot3(fo[v, p], pair)
+            m = dot3(fs[v, p], pair)
             for h in range(2):
                 big[h, 0:32, :] = m[:, 128 * h : 128 * h + 128]
                 avs[p, v, h] = 0.125 * (big[h, pl.ds(0, 16, 2), :] + big[h, pl.ds(1, 16, 2), :])
@@ -250,19 +326,9 @@
     for c in one:
         c.wait()
 
-    def tags(i, _):
-        for way in range(2):
-            t = bx[way, i]
-            tb[way, 2 * i] = t
-            tb[way, 2 * i + 1] = pltpu.roll(t, 64, 1)
-        return 0
-
-    lax.fori_loop(0, NP, tags, 0)
     lane = iota((8, 128), 1)
-    group = iota((10, 128), 1) // 32
-
-    def select(j):
-        nn = jnp.where(iota((1, 128), 1) < 64, ids[0, 2 * j], ids[0, 2 * j + 1]).astype(F32)
+
+    def place_coarse(j, _):
         for p in range(2):
             slot = 2 * j + p
             gy = nbr[4, slot]
@@ -272,18 +338,45 @@
             r1 = pltpu.roll(ba[a + 2, 8:16, :], (136 - 8 * gy) & 127, 1)
             r2 = pltpu.roll(ba[4 * gz + 3, 8:16, :], (176 - 16 * gy) & 127, 1)
             r3 = pltpu.roll(ba[4 * gz + 9, 8:16, :], (192 - 16 * gy) & 127, 1)
-            c = jnp.where(lane < 64, jnp.where((lane & 8) == 0, r0, r1), jnp.where(lane < 80, r2, r3))
-            c = dot3(c, spread)[2:7]
+            cg[slot] = jnp.where(lane < 64, jnp.where((lane & 8) == 0, r0, r1), jnp.where(lane < 80, r2, r3))
+        return 0
+
+    lax.fori_loop(0, NP, place_coarse, 0, unroll=2)
+    cg[...] = dot3(cg[...].reshape(256, 128), spread).reshape(32, 8, 128)
+    sub = iota((32, 128), 0)
+    want = jnp.zeros((32, 128), I32)
+    for j in range(NP):
+        for p in range(2):
+            want = jnp.where(sub == NP * p + j, ids[0, 2 * j + p], want)
+    want = want.astype(F32)
+    l16 = iota((16, 128), 1)
+    diagonal = l16 == iota((16, 128), 0)
+    for way in range(2):
+        tag = bx[way, :, 5, :]
+        data = jnp.concatenate([bx[way, :, v, :] for v in range(5)], axis=1)
+        got = []
+        for t in range(2):
+            tt = pltpu.roll(tag, 64, 1) if t else tag
+            row = jnp.sum(jnp.where(diagonal, tt, 0.0), axis=0, keepdims=True)
+            got.append(dot3_left(ones_where(want == row)[:, 0:16], data))
+        for v in range(5):
+            g0 = got[0][:, 128 * v : 128 * v + 128]
+            g1 = got[1][:, 128 * v : 128 * v + 128]
+            lo = g0[0:16] + pltpu.roll(g1[0:16], 64, 1)
+            hi = pltpu.roll(g0[16:32], 64, 1) + g1[16:32]
+            dd[:, way, 10 + v, :] = jnp.where(l16 < 64, lo, hi)
+        dd[:, way, 15, :] = jnp.zeros((16, 128), F32)
+    group = iota((10, 128), 1) // 32
+
+    def select(j):
+        for p in range(2):
+            slot = 2 * j + p
+            c = cg[slot, 2:7, :]
             val = jnp.concatenate([c, c], axis=0)
             for g in range(4):
                 q = nbr[g, slot]
                 val = jnp.where((group == g) & (q >= 0), ba[jnp.maximum(q, 0), 0:10, :], val)
             dd[j, p, 0:10, :] = val
-            acc = jnp.zeros((5, 128), F32)
-            for i in range(2 * NP):
-                acc = jnp.where(tb[p, i, 5:6, :] == nn, tb[p, i, 0:5, :], acc)
-            dd[j, p, 10:15, :] = acc
-            dd[j, p, 15:16, :] = jnp.zeros((1, 128), F32)
 
     def selected(d):
         j = lax.rem(me + d, NP)
@@ -385,6 +478,10 @@
     big[2] = dot3(fluxes, reflux)
     l16 = iota((16, 128), 1)
     for p in range(2):
+        gy = nbr[4, 2 * me + p]
+        turn_a = (16 * gy + 32) & 127
+        turn_y = 16 * gy
+        turn_z = (16 * gy + 80) & 127
         yr = [jnp.zeros((16, 128), F32)] * 2
         zr = [jnp.zeros((16, 128), F32)] * 2
         for v in range(5):
@@ -396,12 +493,12 @@
             for h in range(2):
                 xh = xm[:, 128 * h : 128 * h + 128]
                 fix = t[h] + jnp.where(sub == 0, xh[0:1], jnp.where(sub == 15, xh[1:2], 0.0))
-                av[:, h, p, v, :] = avs[p, v, h] - 0.0125 * fix
+                av[:, h, p, v, :] = pltpu.roll(avs[p, v, h] - 0.0125 * fix, turn_a, 1)
                 yr[h] = jnp.where((l16 >= 25 * v) & (l16 < 25 * v + 25), moved(w, 25 * v - 64 * h), yr[h])
-                zr[h] = jnp.where(l16 // 16 == v, moved(w, 16 * v - 64 * h - 32), zr[h])
+                zr[h] = jnp.where(l16 // 16 == 4 - v, moved(w, 16 * (4 - v) - 64 * h - 32), zr[h])
         for h in range(2):
-            av[:, h, p, 5, :] = yr[h]
-            av[:, h, p, 6, :] = zr[h]
+            av[:, h, p, 5, :] = pltpu.roll(yr[h], turn_y, 1)
+            av[:, h, p, 6, :] = pltpu.roll(zr[h], turn_z, 1)
             av[:, h, p, 7, :] = jnp.zeros((16, 128), F32)
     one = []
     for d in range(1, NP):
@@ -412,12 +509,17 @@
     for p in range(2):
         for v in range(5):
             a = 160 * p + 32 * v
-            fo[v, p] = fo[v, p] - 0.1 * dot3(bf[a : a + 32, :], expand)
+            fs[v, p] = fs[v, p] - 0.1 * dot3(bf[a : a + 32, :], expand)
             for way, x in ((0, 0), (1, 31)):
-                fo[v, p, x : x + 1, :] = fo[v, p, x : x + 1, :] - 0.1 * xg[v, 2 * p + way : 2 * p + way + 1, :]
+                fs[v, p, x : x + 1, :] = fs[v, p, x : x + 1, :] - 0.1 * xg[v, 2 * p + way : 2 * p + way + 1, :]
+    stores = [pltpu.make_async_copy(fs.at[v], fo.at[v], ls.at[v]) for v in range(5)]
+    for c in stores:
+        c.start()
     lane = iota((8, 128), 1)
     sub = iota((8, 128), 0)
     block = lane // 16
+    ring = (block + sub) & 7
+    slope = lane + sub - 7
     own.wait()
     for c in one:
         c.wait()
@@ -426,8 +528,9 @@
         h = lax.rem(j, 2)
         r = j // 2
         far = r - 2 + 2 * h
-        val = [jnp.zeros((8, 128), F32)] * 5
-        add = [jnp.zeros((8, 128), F32)] * 5
+        acc = [jnp.zeros((8, 128), F32)] * 5
+        accy = [jnp.zeros((8, 128), F32)] * 5
+        accz = jnp.zeros((8, 128), F32)
         covered = jnp.zeros((8, 128), F32)
         for gy in range(6):
             a = grid[0, gy + 8 * (r - 1) + GOFF]
@@ -436,20 +539,19 @@
             b0 = jnp.maximum(b, 0)
             t = bb[a0 // 2, h, a0 & 1]
             zt = bb[b0 // 2, h, b0 & 1, 6:7, :]
-            ina = (block == gy + 1) & (a >= 0)
-            inb = (block == gy + 1) & (sub == 7 * h) & (b >= 0)
-            iny = ((lane == 16 * gy + 15) | (lane == 16 * gy + 32)) & (a >= 0)
-            covered = jnp.where(ina, 1.0, covered)
-            yt = pltpu.roll(jnp.broadcast_to(t[5:6], (8, 128)), 0, 1, stride=1, stride_axis=0)
-            zt = jnp.broadcast_to(zt, (8, 128))
+            covered = jnp.where((block == gy + 1) & (a >= 0), 1.0, covered)
+            ina = (ring == gy + 1) & (a >= 0)
+            accz = jnp.where((ring == gy + 1) & (b >= 0), zt, accz)
             for v in range(5):
-                w = jnp.broadcast_to(t[v : v + 1], (8, 128))
-                w = moved(pltpu.roll(w, 0, 1, stride=16, stride_axis=0), 16 * gy + 32)
-                val[v] = jnp.where(ina, w, val[v])
-                add[v] = jnp.where(iny, add[v] + moved(yt, 16 * gy + 8 - 25 * v), add[v])
-                add[v] = jnp.where(inb, add[v] + moved(zt, 16 * gy + 16 - 16 * v), add[v])
-        for v in range(5):
-            ee[j, v] = jnp.where(covered > 0, val[v], add[v])
+                acc[v] = jnp.where(ina, t[v : v + 1], acc[v])
+                off = (slope - 16 * gy - 25 * v) & 127
+                accy[v] = jnp.where(((off == 0) | (off == 17)) & (a >= 0), t[5:6], accy[v])
+        accz = pltpu.roll(accz, 0, 1, stride=16, stride_axis=0)
+        for v in range(5):
+            val = pltpu.roll(acc[v], 0, 1, stride=16, stride_axis=0)
+            add = moved(pltpu.roll(accy[v], 0, 1, stride=1, stride_axis=0), 8 - 25 * v)
+            add = add + jnp.where(sub == 7 * h, accz[v : v + 1], 0.0)
+            ee[j, v] = jnp.where(covered > 0, val, add)
 
     def expanded(d):
         j = lax.rem(me + d, NP)
@@ -464,85 +566,32 @@
     expand_to(me)
     own = pltpu.make_async_copy(ee.at[me], oe.at[me], ls.at[6])
     own.start()
+    mid = provisional(s, me, cb, oz, ocx, grid, prov)
     own.wait()
     for d in range(1, NP):
         expanded(d).wait()
-
-
-def coarse_kernel(coarse, oe, oz, ocx, grid, fo, out, fine_out, sem):
-    done = pltpu.make_async_copy(fo, fine_out, sem)
+    for x in range(16):
+        for v in range(5):
+            e = oe[x, v]
+            prov[v, x] = jnp.where(mid > 0, e, prov[v, x] + e)
+    done = pltpu.make_async_copy(prov, co, ls.at[5])
     done.start()
-    s = lax.axis_index("slab")
-    me = lax.axis_index("patch")
-    r = me // 2
-    h = lax.rem(me, 2)
-    lane = iota((8, 128), 1)
-    sub = iota((8, 128), 0)
-    blocks = lane // 16
-
-    def cover(row):
-        m = jnp.zeros((8, 128), F32)
-        for gy in range(6):
-            m = jnp.where((blocks == gy + 1) & (grid[0, gy + 8 * (row - 1) + GOFF] >= 0), 1.0, m)
-        return m
-
-    mid = cover(r)
-    below = jnp.where(h == 0, cover(r - 1), mid)
-    above = jnp.where(h == 1, cover(r + 1), mid)
-    free = 1.0 - mid
-    fup = free * (1.0 - pltpu.roll(mid, 127, 1))
-    flo = free * (1.0 - pltpu.roll(mid, 1, 1))
-    zlo = free * (1.0 - jnp.where(sub == 0, below, mid))
-    zhi = free * (1.0 - jnp.where(sub == 7, above, mid))
-
-    def cells(x):
-        q = [coarse[v, x] for v in range(5)]
-        st = state(q)
-        return q, st, flux(q, st, 0)
-
-    def face(a, b):
-        return rusanov(a[0], a[2][0], a[2][1], b[0], b[2][0], b[2][1])
-
-    first = cells(0)
-    q = [jnp.where(s == 0, coarse[v, 0], ocx[0, v]) for v in range(5)]
-    st = state(q)
-    lower = face((q, st, flux(q, st, 0)), first)
-    here = first
-    for x in range(16):
-        if x < 15:
-            there = cells(x + 1)
-        else:
-            q = [jnp.where(s == NS - 1, coarse[v, 15], ocx[1, v]) for v in range(5)]
-            st = state(q)
-            there = (q, st, flux(q, st, 0))
-        upper = face(here, there)
-        q, st, _ = here
-        change = [(upper[v] - lower[v]) * free for v in range(5)]
-        row = slice(x, x + 1)
-        zn = [jnp.where(sub == 7, jnp.where(me == NP - 1, q[v], oz[1, v, row, :]), pltpu.roll(q[v], 7, 0)) for v in range(5)]
-        zb = [jnp.where(sub == 0, jnp.where(me == 0, q[v], oz[0, v, row, :]), pltpu.roll(q[v], 1, 0)) for v in range(5)]
-        f, a = flux(q, st, 2)
-        fn, an = flux(zn, state(zn), 2)
-        fb, ab = flux(zb, state(zb), 2)
-        up = rusanov(q, f, a, zn, fn, an)
-        lo = rusanov(zb, fb, ab, q, f, a)
-        change = [change[v] + (up[v] * zhi - lo[v] * zlo) for v in range(5)]
-        f, a = flux(q, st, 1)
-        nxt = lambda t: jnp.where(lane == 127, t, pltpu.roll(t, 127, 1))
-        prv = lambda t: jnp.where(lane == 0, t, pltpu.roll(t, 1, 1))
-        up = rusanov(q, f, a, [nxt(t) for t in q], [nxt(t) for t in f], nxt(a))
-        lo = rusanov([prv(t) for t in q], [prv(t) for t in f], prv(a), q, f, a)
-        for v in range(5):
-            prov = q[v] - 0.05 * (change[v] + (up[v] * fup - lo[v] * flo))
-            e = oe[x, v]
-            out[v, x] = jnp.where(mid > 0, e, prov + e)
-        here = there
-        lower = upper
+    for c in stores:
+        c.wait()
     done.wait()
 
 
-def vm():
-    return pl.BlockSpec(memory_space=pltpu.VMEM)
+def copy_kernel(a, b, a_out, b_out, sems):
+    n = a.shape[0]
+    copies = []
+    for v in range(n):
+        copies.append(pltpu.make_async_copy(b.at[v, 0], b_out.at[v, 0], sems.at[n + v]))
+        copies.append(pltpu.make_async_copy(b.at[v, 1], b_out.at[v, 1], sems.at[2 * n + v]))
+        copies.append(pltpu.make_async_copy(a.at[v], a_out.at[v], sems.at[v]))
+    for c in copies:
+        c.start()
+    for c in copies:
+        c.wait()
 
 
 def sm():
@@ -561,21 +610,21 @@
     return pltpu.VMEM(shape, F32)
 
 
-LIMIT = 48 << 20
+LIMIT = 60 << 20
 
 
 def local(coarse, fine, columns, patch_ids):
-    fo, oe, oz, ocx, grid = pl.pallas_call(
+    fo, co = pl.pallas_call(
         step_kernel,
-        out_shape=(
-            sds(5, 2, 32, 1024), sds(16, 5, 8, 128), sds(2, 5, 16, 128), sds(2, 5, 8, 128), sds(1, 96, dtype=I32),
-        ),
+        out_shape=(sds(5, 2, 32, 1024), sds(5, 16, 8, 128)),
         in_specs=[hb(), hb(), sm(), sm()],
-        out_specs=(vm(), vm(), vm(), vm(), sm()),
+        out_specs=(hb(), hb()),
         scratch_shapes=[
             pltpu.SMEM((7, 32), I32),
+            pltpu.SMEM((1, 96), I32),
             buf(5, 2, 32, 1024),
             buf(5, 16, 8, 128),
+            buf(5, 2, 32, 1024),
             buf(16, 2, 16, 128),
             buf(2, 16, 8, 128),
             buf(2, 5, 16, 128),
@@ -583,9 +632,11 @@
             buf(2, 5, 32, 128),
             buf(32, 16, 128),
             buf(2, 16, 8, 128),
-            buf(2, 32, 8, 128),
+            buf(32, 8, 128),
             buf(16, 2, 16, 128),
             buf(16, 2, 16, 128),
+            buf(2, 5, 16, 128),
+            buf(2, 5, 8, 128),
             buf(5, 32, 128),
             buf(320, 128),
             buf(5, 4, 1024),
@@ -594,8 +645,10 @@
             buf(16, 2, 2, 8, 128),
             buf(16, 2, 2, 8, 128),
             buf(16, 5, 8, 128),
+            buf(16, 5, 8, 128),
             buf(3, 320, 128),
             buf(5, 32, 1024),
+            buf(5, 16, 8, 128),
             pltpu.SemaphoreType.DMA((N_SEM,)),
             pltpu.SemaphoreType.DMA((N_SEM,)),
             pltpu.SemaphoreType.DMA((7,)),
@@ -604,14 +657,14 @@
         name="step",
     )(fine, coarse, patch_ids, columns.T)
     return pl.pallas_call(
-        coarse_kernel,
+        copy_kernel,
         out_shape=(sds(5, 16, 8, 128), sds(5, 2, 32, 1024)),
-        in_specs=[vm(), vm(), vm(), vm(), sm(), pl.BlockSpec(memory_space=pl.ANY)],
-        out_specs=(vm(), hb()),
-        scratch_shapes=[pltpu.SemaphoreType.DMA],
+        in_specs=[hb(), hb()],
+        out_specs=(hb(), hb()),
+        scratch_shapes=[pltpu.SemaphoreType.DMA((15,))],
         compiler_params=pltpu.CompilerParams(vmem_limit_bytes=LIMIT),
-        name="coarse_step",
-    )(coarse, oe, oz, ocx, grid, fo)
+        name="copy_out",
+    )(co, fo)
 
 
 def solution(mesh):

time: 53.6 us -> 94.3 us (1.76)
  Pallas kernels: 48.4 us -> 92.5 us
  local copies, waits for them, and re-layouts: 3.61 us -> 0 us
    pallas_call x2, Pallas kernels: 48.4 us -> 92.5 us  [the longest x1 50.9 us: local(): pl.pallas_call(copy_kernel, out_shape=(sds(5, 16, 8, 128), sds(5, 2, 32,...]
    unnamed x8 -> x0, local copies, waits for them, and re-layouts: 3.61 us -> none
where the time goes in v4:
time: 94.3 us; the launch traced here: 93.1 us
  Pallas kernels  92.5 us (98%)
    pallas_call x1, Pallas kernels, local(): pl.pallas_call(copy_kernel, out_shape=(sds(5, 16, 8, 128), sds(5, 2, 32,...  50.9 us
    pallas_call x1, Pallas kernels, local(): pl.pallas_call(step_kernel, out_shape=(sds(5, 2, 32, 1024), sds(5, 16, 8,...  41.6 us

profile of v4, /device:TPU:2, one launch (start us, length us, event | category | flops | bytes accessed | tf_op | source)
XLA Modules:
  0.0 93.1 jit_solution(14863182040415381097)
XLA Ops:
  0.6 41.6 %step.1 = (f32[5,2,32,1024]{3,2,1,0:T(8,128)}, f32[5,16,8,128]{3,2,1,0:T(8,128)}) custom-call(f32[5,2,32,1024]{3,2,1,0:T(8,128)} %fine.1, f32[5,16,8,128]{3,2,1,0:T(8,128)} %coarse.1, s32[1,32]{1,0:T(1,128)} %ids.1, s32[2,32]{1,0:T(2,128)} %bitcast.1), custom_call_target="tpu_custom_call" | custom-call | tf_op jit(solution)/shard_map/step/pallas_call | solution.py:617
  42.2 50.9 %copy_out.1 = (f32[5,16,8,128]{3,2,1,0:T(8,128)}, f32[5,2,32,1024]{3,2,1,0:T(8,128)}) custom-call(f32[5,16,8,128]{3,2,1,0:T(8,128)} %get-tuple-element.4.a, f32[5,2,32,1024]{3,2,1,0:T(8,128)} %get-tuple-element.5.b), custom_call_target="tpu_custom_call" | custom-call | tf_op jit(solution)/shard_map/copy_out/pallas_call | solution.py:659

commit v5 on v4

--- a/solution.py
+++ b/solution.py
@@ -140,9 +140,9 @@
 
 
 def step_kernel(
-    fine, coarse, ids, cols, fo, co,
-    nbr, grid, fb, cb, fs, a1, x1, rz, ct, pk, ba, bx, cg, dd, og, oz, ocx,
-    gh, bf, xg, xo, avs, av, bb, ee, oe, big, chg, prov, ss, rs, ls,
+    fine, coarse, ids_in, cols_in, fs, prov,
+    ids, cols, nbr, grid, fb, cb, a1, x1, rz, ct, pk, ba, bx, cg, dd, og, oz, ocx,
+    gh, bf, xg, xo, avs, av, bb, ee, oe, big, chg, ss, rs, ls,
 ):
     s = lax.axis_index("slab")
     me = lax.axis_index("patch")
@@ -152,6 +152,8 @@
     peer = [lax.rem(me + d, NP) for d in range(NP)]
     loads = [pltpu.make_async_copy(fine.at[v], fb.at[v], ls.at[v]) for v in range(5)]
     loads.append(pltpu.make_async_copy(coarse, cb, ls.at[5]))
+    loads.append(pltpu.make_async_copy(ids_in, ids, ls.at[6]))
+    loads.append(pltpu.make_async_copy(cols_in, cols, ls.at[7]))
     barrier = pltpu.get_barrier_semaphore()
     for c in loads:
         c.start()
@@ -179,6 +181,8 @@
             pk[p, v] = dot3(fb[v, p], sel)
             for xr in range(2):
                 a1[:, p, 5 * xr + v, :] = pk[p, v, pl.ds(xr, 16, 2), :]
+    loads[6].wait()
+    loads[7].wait()
     lane = iota((5, 128), 1)
     tag = jnp.where(iota((3, 128), 1) < 64, ids[0, 2 * me], ids[0, 2 * me + 1]).astype(F32)
     for d, row in ((0, 0), (1, 31)):
@@ -512,9 +516,6 @@
             fs[v, p] = fs[v, p] - 0.1 * dot3(bf[a : a + 32, :], expand)
             for way, x in ((0, 0), (1, 31)):
                 fs[v, p, x : x + 1, :] = fs[v, p, x : x + 1, :] - 0.1 * xg[v, 2 * p + way : 2 * p + way + 1, :]
-    stores = [pltpu.make_async_copy(fs.at[v], fo.at[v], ls.at[v]) for v in range(5)]
-    for c in stores:
-        c.start()
     lane = iota((8, 128), 1)
     sub = iota((8, 128), 0)
     block = lane // 16
@@ -574,11 +575,6 @@
         for v in range(5):
             e = oe[x, v]
             prov[v, x] = jnp.where(mid > 0, e, prov[v, x] + e)
-    done = pltpu.make_async_copy(prov, co, ls.at[5])
-    done.start()
-    for c in stores:
-        c.wait()
-    done.wait()
 
 
 def copy_kernel(a, b, a_out, b_out, sems):
@@ -594,8 +590,8 @@
         c.wait()
 
 
-def sm():
-    return pl.BlockSpec(memory_space=pltpu.SMEM)
+def vm():
+    return pl.BlockSpec(memory_space=pltpu.VMEM)
 
 
 def hb():
@@ -610,21 +606,26 @@
     return pltpu.VMEM(shape, F32)
 
 
-LIMIT = 60 << 20
+LIMIT = 48 << 20
+
+
+def pin(x):
+    return pltpu.with_memory_space_constraint(x, pltpu.HBM)
 
 
 def local(coarse, fine, columns, patch_ids):
     fo, co = pl.pallas_call(
         step_kernel,
         out_shape=(sds(5, 2, 32, 1024), sds(5, 16, 8, 128)),
-        in_specs=[hb(), hb(), sm(), sm()],
-        out_specs=(hb(), hb()),
+        in_specs=[hb()] * 4,
+        out_specs=(vm(), vm()),
         scratch_shapes=[
+            pltpu.SMEM((1, 32), I32),
+            pltpu.SMEM((2, 32), I32),
             pltpu.SMEM((7, 32), I32),
             pltpu.SMEM((1, 96), I32),
             buf(5, 2, 32, 1024),
             buf(5, 16, 8, 128),
-            buf(5, 2, 32, 1024),
             buf(16, 2, 16, 128),
             buf(2, 16, 8, 128),
             buf(2, 5, 16, 128),
@@ -648,18 +649,17 @@
             buf(16, 5, 8, 128),
             buf(3, 320, 128),
             buf(5, 32, 1024),
-            buf(5, 16, 8, 128),
             pltpu.SemaphoreType.DMA((N_SEM,)),
             pltpu.SemaphoreType.DMA((N_SEM,)),
-            pltpu.SemaphoreType.DMA((7,)),
+            pltpu.SemaphoreType.DMA((8,)),
         ],
         compiler_params=pltpu.CompilerParams(collective_id=0, has_side_effects=True, vmem_limit_bytes=LIMIT),
         name="step",
-    )(fine, coarse, patch_ids, columns.T)
+    )(pin(fine), pin(coarse), pin(patch_ids), pin(columns.T))
     return pl.pallas_call(
         copy_kernel,
         out_shape=(sds(5, 16, 8, 128), sds(5, 2, 32, 1024)),
-        in_specs=[hb(), hb()],
+        in_specs=[pl.BlockSpec(memory_space=pl.ANY)] * 2,
         out_specs=(hb(), hb()),
         scratch_shapes=[pltpu.SemaphoreType.DMA((15,))],
         compiler_params=pltpu.CompilerParams(vmem_limit_bytes=LIMIT),

time: 94.3 us -> 43.2 us (0.46)
  the two profiles are of different devices: /device:TPU:2 before, /device:TPU:16 now
where the time goes in v5:
time: 43.2 us; the launch traced here: 43.1 us
  Pallas kernels  42.5 us (98%)
  between operations  0.64 us (1%)
    pallas_call x1, Pallas kernels, local(): pl.pallas_call(step_kernel, out_shape=(sds(5, 2, 32, 1024), sds(5, 16, 8,...  41.2 us
    pallas_call x1, Pallas kernels, local(): pl.pallas_call(copy_kernel, out_shape=(sds(5, 16, 8, 128), sds(5, 2, 32,...  1.28 us

profile of v5, /device:TPU:16, one launch (start us, length us, event | category | flops | bytes accessed | tf_op | source)
XLA Modules:
  0.0 43.1 jit_solution(9467029370191085641)
XLA Ops:
  0.6 41.2 %step.1 = (f32[5,2,32,1024]{3,2,1,0:T(8,128)S(1)}, f32[5,16,8,128]{3,2,1,0:T(8,128)S(1)}) custom-call(f32[5,2,32,1024]{3,2,1,0:T(8,128)} %fine.1, f32[5,16,8,128]{3,2,1,0:T(8,128)} %coarse.1, s32[1,32]{1,0:T(1,128)} %ids_in.1, s32[2,32]{1,0:T(2,128)} %bitcast.1), custom_call_target="tpu_custom_call" | custom-call | tf_op jit(solution)/shard_map/step/pallas_call | solution.py:617
  41.8 1.3 %copy_out.1 = (f32[5,16,8,128]{3,2,1,0:T(8,128)}, f32[5,2,32,1024]{3,2,1,0:T(8,128)}) custom-call(f32[5,16,8,128]{3,2,1,0:T(8,128)S(1)} %get-tuple-element.4.a, f32[5,2,32,1024]{3,2,1,0:T(8,128)S(1)} %get-tuple-element.5.b), custom_call_target="tpu_custom_call" | custom-call | tf_op jit(solution)/shard_map/copy_out/pallas_call | solution.py:659

commit v6 on v5

--- a/solution.py
+++ b/solution.py
@@ -142,7 +142,7 @@
 def step_kernel(
     fine, coarse, ids_in, cols_in, fs, prov,
     ids, cols, nbr, grid, fb, cb, a1, x1, rz, ct, pk, ba, bx, cg, dd, og, oz, ocx,
-    gh, bf, xg, xo, avs, av, bb, ee, oe, big, chg, ss, rs, ls,
+    bf, xg, av, bb, cc, xt, tt, ee, oe, big, chg, ss, rs, ls,
 ):
     s = lax.axis_index("slab")
     me = lax.axis_index("patch")
@@ -178,9 +178,9 @@
     for v in range(5):
         loads[v].wait()
         for p in range(2):
-            pk[p, v] = dot3(fb[v, p], sel)
+            pk[...] = dot3(fb[v, p], sel)
             for xr in range(2):
-                a1[:, p, 5 * xr + v, :] = pk[p, v, pl.ds(xr, 16, 2), :]
+                a1[:, p, 5 * xr + v, :] = pk[pl.ds(xr, 16, 2), :]
     loads[6].wait()
     loads[7].wait()
     lane = iota((5, 128), 1)
@@ -189,10 +189,12 @@
         for j in range(8):
             t0 = fb[:, 0, row, 128 * j : 128 * j + 128]
             t1 = fb[:, 1, row, 128 * j : 128 * j + 128]
-            xo[:, d, 128 * j : 128 * j + 128] = t0
-            xo[:, 2 + d, 128 * j : 128 * j + 128] = t1
-            x1[d, 2 * j, 0:5, :] = jnp.where(lane < 64, t0, pltpu.roll(t1, 64, 1))
-            x1[d, 2 * j + 1, 0:5, :] = jnp.where(lane < 64, pltpu.roll(t0, 64, 1), t1)
+            for o, t in (
+                (0, jnp.where(lane < 64, t0, pltpu.roll(t1, 64, 1))),
+                (1, jnp.where(lane < 64, pltpu.roll(t0, 64, 1), t1)),
+            ):
+                x1[d, 2 * j + o, 0:5, :] = t
+                a1[2 * j + o, 2, 8 * d : 8 * d + 5, :] = t
             x1[d, 2 * j, 5:8, :] = tag
             x1[d, 2 * j + 1, 5:8, :] = tag
     loads[5].wait()
@@ -225,7 +227,7 @@
     for d in range(NP):
         j = peer[d]
         if d:
-            one.append(copy(d - 1, a1.at[j], ba.at[pl.ds(2 * me, 2)], (s, j)))
+            one.append(copy(d - 1, a1.at[j], ba.at[me], (s, j)))
             one[-1].start()
         for c in (
             copy(S_X + 2 * d, x1.at[0, j], bx.at[1, me], (down, j)),
@@ -241,7 +243,7 @@
     ]
     for c in two:
         c.start()
-    own = pltpu.make_async_copy(a1.at[me], ba.at[pl.ds(2 * me, 2)], ls.at[6])
+    own = pltpu.make_async_copy(a1.at[me], ba.at[me], ls.at[6])
     own.start()
 
     def place(t, _):
@@ -254,27 +256,6 @@
         return 0
 
     lax.fori_loop(0, 32, place, 0)
-    for i in range(GOFF):
-        grid[0, i] = jnp.int32(-1)
-
-    def find(k, _):
-        q = jnp.int32(-1)
-        for t in range(32):
-            q = jnp.where(nbr[6, t] == k, t, q)
-        grid[0, k] = q
-        return 0
-
-    lax.fori_loop(GOFF, GOFF + 48, find, 0)
-    for i in range(GOFF + 48, 96):
-        grid[0, i] = jnp.int32(-1)
-
-    def look(t, _):
-        for g, step in enumerate((-1, 1, -8, 8)):
-            nbr[g, t] = grid[0, nbr[6, t] + step]
-        return 0
-
-    lax.fori_loop(0, 32, look, 0)
-
     src = iota((1024, 256), 0)
     dst = iota((1024, 256), 1)
     zz = 8 * (dst // 128) + 7 - lax.rem(dst, 128) // 16
@@ -317,15 +298,51 @@
             m = dot3(fs[v, p], pair)
             for h in range(2):
                 big[h, 0:32, :] = m[:, 128 * h : 128 * h + 128]
-                avs[p, v, h] = 0.125 * (big[h, pl.ds(0, 16, 2), :] + big[h, pl.ds(1, 16, 2), :])
+                av[:, p, h, v, :] = 0.125 * (big[h, pl.ds(0, 16, 2), :] + big[h, pl.ds(1, 16, 2), :])
+        for h in range(2):
+            for v in range(5, 8):
+                av[:, p, h, v, :] = jnp.zeros((16, 128), F32)
 
     interior(0)
+    interior(1)
+    early = []
+    for d in range(1, NP):
+        early.append(copy(S_A + d - 1, av.at[peer[d]], bb.at[me], (s, peer[d])))
+        early[-1].start()
+    own_av = pltpu.make_async_copy(av.at[me], bb.at[me], ls.at[7])
+    own_av.start()
+    for i in range(GOFF):
+        grid[0, i] = jnp.int32(-1)
+
+    def find(k, _):
+        q = jnp.int32(-1)
+        for t in range(32):
+            q = jnp.where(nbr[6, t] == k, t, q)
+        grid[0, k] = q
+        return 0
+
+    lax.fori_loop(GOFF, GOFF + 48, find, 0)
+    for i in range(GOFF + 48, 96):
+        grid[0, i] = jnp.int32(-1)
+
     src = iota((128, 128), 0)
     dst = iota((128, 128), 1)
     g = dst // 32
     i = lax.rem(dst, 32) // 2
     base = jnp.where(g == 0, 0, jnp.where(g == 1, 48, jnp.where(g == 2, 64, 80)))
     spread = ones_where(src == base + i)
+    sub = iota((32, 128), 0)
+    l1 = iota((1, 128), 1)
+    want = jnp.zeros((32, 128), I32)
+    code = jnp.zeros((32, 128), I32)
+    codes = jnp.full((1, 128), -99, I32)
+    for i in range(NP):
+        for p in range(2):
+            k = NP * p + i
+            want = jnp.where(sub == k, ids[0, 2 * i + p], want)
+            code = jnp.where(sub == k, nbr[6, 2 * i + p], code)
+            codes = jnp.where(l1 == k, nbr[6, 2 * i + p], codes)
+    want = want.astype(F32)
     own.wait()
     for c in one:
         c.wait()
@@ -334,68 +351,107 @@
 
     def place_coarse(j, _):
         for p in range(2):
-            slot = 2 * j + p
-            gy = nbr[4, slot]
-            gz = nbr[5, slot]
-            a = 4 * (gz + 1)
-            r0 = pltpu.roll(ba[a, 8:16, :], (128 - 8 * gy) & 127, 1)
-            r1 = pltpu.roll(ba[a + 2, 8:16, :], (136 - 8 * gy) & 127, 1)
-            r2 = pltpu.roll(ba[4 * gz + 3, 8:16, :], (176 - 16 * gy) & 127, 1)
-            r3 = pltpu.roll(ba[4 * gz + 9, 8:16, :], (192 - 16 * gy) & 127, 1)
-            cg[slot] = jnp.where(lane < 64, jnp.where((lane & 8) == 0, r0, r1), jnp.where(lane < 80, r2, r3))
+            gy = nbr[4, 2 * j + p]
+            gz = nbr[5, 2 * j + p]
+            a = 2 * (gz + 1)
+            r0 = pltpu.roll(ba[a, 0, 8:16, :], (128 - 8 * gy) & 127, 1)
+            r1 = pltpu.roll(ba[a + 1, 0, 8:16, :], (136 - 8 * gy) & 127, 1)
+            r2 = pltpu.roll(ba[2 * gz + 1, 1, 8:16, :], (176 - 16 * gy) & 127, 1)
+            r3 = pltpu.roll(ba[2 * gz + 4, 1, 8:16, :], (192 - 16 * gy) & 127, 1)
+            cg[NP * p + j] = jnp.where(lane < 64, jnp.where((lane & 8) == 0, r0, r1), jnp.where(lane < 80, r2, r3))
         return 0
 
     lax.fori_loop(0, NP, place_coarse, 0, unroll=2)
     cg[...] = dot3(cg[...].reshape(256, 128), spread).reshape(32, 8, 128)
-    sub = iota((32, 128), 0)
-    want = jnp.zeros((32, 128), I32)
-    for j in range(NP):
+    packs = [
+        jnp.concatenate([ba[:, 0, k, :], ba[:, 1, k, :]], axis=0) for k in range(10)
+    ]
+    data = jnp.concatenate(packs, axis=1)
+    group = iota((32, 128), 1) // 32
+    near = []
+    absent = jnp.zeros((32, 128), F32)
+    for g, step in enumerate((-1, 1, -8, 8)):
+        hit = codes == code + step
+        near.append(dot3_left(ones_where(hit)[:, 0:32], data))
+        some = jnp.sum(jnp.where(hit, 1.0, 0.0), axis=1, keepdims=True)
+        absent = jnp.where(group == g, 1.0 - some, absent)
+    theirs = []
+    mine = []
+    low = (group & 1) == 0
+    for v in range(5):
+        both = []
+        for xr in range(2):
+            k = 128 * (5 * xr + v)
+            n = [t[:, k : k + 128] for t in near]
+            n = jnp.where(group == 0, n[0], jnp.where(group == 1, n[1], jnp.where(group == 2, n[2], n[3])))
+            both.append(jnp.where(absent > 0.5, cg[:, 2 + v, :], n))
+        theirs.append(jnp.concatenate(both, axis=0))
+        both = [jnp.where(low, pltpu.roll(packs[5 * xr + v], 96, 1), pltpu.roll(packs[5 * xr + v], 32, 1)) for xr in range(2)]
+        mine.append(jnp.concatenate(both, axis=0))
+    g1 = iota((64, 128), 1)
+    low = ((g1 // 32) & 1) == 0
+    isy = g1 < 64
+
+    def face_flux(q):
+        r, pr, c = state(q)
+        mn = jnp.where(isy, q[2], q[3])
+        u = mn * r
+        py = jnp.where(isy, pr, 0.0)
+        f = [mn, q[1] * u, q[2] * u + py, q[3] * u + (pr - py), (q[4] + pr) * u]
+        return f, jnp.abs(u) + c
+
+    ql = [jnp.where(low, theirs[v], mine[v]) for v in range(5)]
+    qr = [jnp.where(low, mine[v], theirs[v]) for v in range(5)]
+    fl, al = face_flux(ql)
+    fr, ar = face_flux(qr)
+    f = rusanov(ql, fl, al, qr, fr, ar)
+    for v in range(5):
         for p in range(2):
-            want = jnp.where(sub == NP * p + j, ids[0, 2 * j + p], want)
-    want = want.astype(F32)
+            for xr in range(2):
+                a = 32 * xr + 16 * p
+                dd[:, p, 5 * xr + v, :] = f[v][a : a + 16]
+    sums = jnp.concatenate([f[v][0:32] + f[v][32:64] for v in range(5)], axis=0)
     l16 = iota((16, 128), 1)
     diagonal = l16 == iota((16, 128), 0)
+    sides = []
     for way in range(2):
         tag = bx[way, :, 5, :]
         data = jnp.concatenate([bx[way, :, v, :] for v in range(5)], axis=1)
         got = []
         for t in range(2):
-            tt = pltpu.roll(tag, 64, 1) if t else tag
-            row = jnp.sum(jnp.where(diagonal, tt, 0.0), axis=0, keepdims=True)
+            tt_ = pltpu.roll(tag, 64, 1) if t else tag
+            row = jnp.sum(jnp.where(diagonal, tt_, 0.0), axis=0, keepdims=True)
             got.append(dot3_left(ones_where(want == row)[:, 0:16], data))
+        theirs = []
         for v in range(5):
             g0 = got[0][:, 128 * v : 128 * v + 128]
             g1 = got[1][:, 128 * v : 128 * v + 128]
-            lo = g0[0:16] + pltpu.roll(g1[0:16], 64, 1)
-            hi = pltpu.roll(g0[16:32], 64, 1) + g1[16:32]
-            dd[:, way, 10 + v, :] = jnp.where(l16 < 64, lo, hi)
-        dd[:, way, 15, :] = jnp.zeros((16, 128), F32)
-    group = iota((10, 128), 1) // 32
-
-    def select(j):
-        for p in range(2):
-            slot = 2 * j + p
-            c = cg[slot, 2:7, :]
-            val = jnp.concatenate([c, c], axis=0)
-            for g in range(4):
-                q = nbr[g, slot]
-                val = jnp.where((group == g) & (q >= 0), ba[jnp.maximum(q, 0), 0:10, :], val)
-            dd[j, p, 0:10, :] = val
-
-    def selected(d):
-        j = lax.rem(me + d, NP)
-        return copy(S_G + d - 1, dd.at[j], og.at[me], (s, j))
-
-    def select_send(d, _):
-        select(lax.rem(me + d, NP))
-        selected(d).start()
-        return 0
-
-    lax.fori_loop(1, NP, select_send, 0)
-    select(me)
+            a = g0[0:16] + pltpu.roll(g1[0:16], 64, 1)
+            b = pltpu.roll(g0[16:32], 64, 1) + g1[16:32]
+            t = jnp.where(l16 < 64, a, b)
+            theirs.append(jnp.where(s == (0 if way == 0 else NS - 1), ba[:, 2, 8 * way + v, :], t))
+        sides.append(theirs)
+    mine = [jnp.concatenate([ba[:, 2, v, :], ba[:, 2, 8 + v, :]], axis=0) for v in range(5)]
+    theirs = [jnp.concatenate([sides[0][v], sides[1][v]], axis=0) for v in range(5)]
+    low = iota((32, 128), 0) < 16
+    ql = [jnp.where(low, theirs[v], mine[v]) for v in range(5)]
+    qr = [jnp.where(low, mine[v], theirs[v]) for v in range(5)]
+    fl, al = flux(ql, state(ql), 0)
+    fr, ar = flux(qr, state(qr), 0)
+    f = rusanov(ql, fl, al, qr, fr, ar)
+    fx = [jnp.where(low, -t, t) for t in f]
+    for v in range(5):
+        for way in range(2):
+            dd[:, way, 10 + v, :] = fx[v][16 * way : 16 * way + 16]
+    dd[:, 0, 15, :] = jnp.zeros((16, 128), F32)
+    dd[:, 1, 15, :] = jnp.zeros((16, 128), F32)
+
+    late = []
+    for d in range(1, NP):
+        late.append(copy(S_G + d - 1, dd.at[peer[d]], og.at[me], (s, peer[d])))
+        late[-1].start()
     own = pltpu.make_async_copy(dd.at[me], og.at[me], ls.at[6])
     own.start()
-    interior(1)
 
     src = iota((128, 256), 0)
     dst = iota((128, 256), 1)
@@ -414,117 +470,52 @@
     z_at = 64 * (i // 8) + 7 - lax.rem(i, 8)
     at = jnp.where(g == 0, z_at, jnp.where(g == 1, z_at + 17, jnp.where(g == 2, 96 + i, 32 + i)))
     reflux = ones_where(dst == at)
-    l1 = iota((1, 128), 1)
     low = ((l1 & 63) < 8) | (l1 >= 96)
     coef = jnp.where(low, -0.05, 0.05).astype(F32) * 0.25
-    src = iota((128, 1024), 0)
-    dst = iota((128, 1024), 1)
-    g = src // 32
-    i = lax.rem(src, 32)
-    at = jnp.where(g == 0, 32 * i, jnp.where(g == 1, 32 * i + 31, jnp.where(g == 2, i, 992 + i)))
-    sign = jnp.where((g & 1) == 0, -1.0, 1.0)
-    expand = jnp.where(dst == at, sign, 0.0).astype(BF16)
-    own.wait()
-    for d in range(1, NP):
-        two.append(selected(d))
+    fix = dot3(sums, mean_of) * -0.0125
+    refl = dot3(sums, reflux) * coef
+    l32 = iota((32, 128), 1)
+    yr = [jnp.zeros((32, 128), F32)] * 2
+    zr = [jnp.zeros((32, 128), F32)] * 2
+    for v in range(5):
+        w = refl[32 * v : 32 * v + 32]
+        for h in range(2):
+            cc[:, h, v, :] = fix[32 * v : 32 * v + 32, 128 * h : 128 * h + 128]
+            yr[h] = jnp.where((l32 >= 25 * v) & (l32 < 25 * v + 25), moved(w, 25 * v - 64 * h), yr[h])
+            zr[h] = jnp.where(l32 // 16 == 4 - v, moved(w, 16 * (4 - v) - 64 * h - 32), zr[h])
+    for h in range(2):
+        cc[:, h, 5, :] = moved(yr[h], -32)
+        cc[:, h, 6, :] = moved(zr[h], 48)
+        cc[:, h, 7, :] = jnp.zeros((32, 128), F32)
+    src = iota((128, 128), 0)
+    dst = iota((128, 128), 1)
+    sums = jnp.concatenate(fx, axis=0)
+    for p in range(2):
+        m = dot3(sums, ones_where((src // 64 == p) & ((src & 31) // 2 == (dst & 15)))) * -0.0125
+        for v in range(5):
+            xt[:, p, v, :] = m[32 * v : 32 * v + 32]
+        for v in range(5, 8):
+            xt[:, p, v, :] = jnp.zeros((32, 128), F32)
     for c in two:
         c.wait()
-
-    g1 = iota((32, 128), 1)
-    low = ((g1 // 32) & 1) == 0
-    isy = g1 < 64
-
-    def face_flux(q):
-        r, pr, c = state(q)
-        mn = jnp.where(isy, q[2], q[3])
-        u = mn * r
-        py = jnp.where(isy, pr, 0.0)
-        f = [mn, q[1] * u, q[2] * u + py, q[3] * u + (pr - py), (q[4] + pr) * u]
-        return f, jnp.abs(u) + c
-
-    for p in range(2):
-        for v in range(5):
-            for xr in range(2):
-                gh[v, pl.ds(xr, 16, 2), :] = og[:, p, 5 * xr + v, :]
-        theirs = [gh[v] for v in range(5)]
-        mine = [jnp.where(low, pltpu.roll(pk[p, v], 96, 1), pltpu.roll(pk[p, v], 32, 1)) for v in range(5)]
-        ql = [jnp.where(low, theirs[v], mine[v]) for v in range(5)]
-        qr = [jnp.where(low, mine[v], theirs[v]) for v in range(5)]
-        fl, al = face_flux(ql)
-        fr, ar = face_flux(qr)
-        f = rusanov(ql, fl, al, qr, fr, ar)
-        for v in range(5):
-            bf[160 * p + 32 * v : 160 * p + 32 * v + 32, :] = f[v]
-    l5 = iota((5, 128), 1)
-    for way in range(2):
-        for j in range(8):
-            e = og[2 * j, way, 10:15, :]
-            o = og[2 * j + 1, way, 10:15, :]
-            cut = slice(128 * j, 128 * j + 128)
-            xg[:, way, cut] = jnp.where(l5 < 64, e, pltpu.roll(o, 64, 1))
-            xg[:, 2 + way, cut] = jnp.where(l5 < 64, pltpu.roll(e, 64, 1), o)
-    row = iota((4, 1024), 0)
-    low = (row & 1) == 0
-    edge = (row & 1) == jnp.where(s == 0, 0, jnp.where(s == NS - 1, 1, 2))
-    mine = [xo[v] for v in range(5)]
-    theirs = [jnp.where(edge, mine[v], xg[v]) for v in range(5)]
-    ql = [jnp.where(low, theirs[v], mine[v]) for v in range(5)]
-    qr = [jnp.where(low, mine[v], theirs[v]) for v in range(5)]
-    fl, al = flux(ql, state(ql), 0)
-    fr, ar = flux(qr, state(qr), 0)
-    f = rusanov(ql, fl, al, qr, fr, ar)
-    for v in range(5):
-        xg[v] = jnp.where(low, -f[v], f[v])
-    fluxes = bf[...]
-    m = dot3(fluxes, mean_of)
-    big[0] = m[:, 0:128]
-    big[1] = m[:, 128:256]
-    big[2] = dot3(fluxes, reflux)
-    l16 = iota((16, 128), 1)
-    for p in range(2):
-        gy = nbr[4, 2 * me + p]
-        turn_a = (16 * gy + 32) & 127
-        turn_y = 16 * gy
-        turn_z = (16 * gy + 80) & 127
-        yr = [jnp.zeros((16, 128), F32)] * 2
-        zr = [jnp.zeros((16, 128), F32)] * 2
-        for v in range(5):
-            a = 160 * p + 32 * v
-            t = [big[h, pl.ds(a, 16, 2), :] + big[h, pl.ds(a + 1, 16, 2), :] for h in range(3)]
-            xm = dot3(xg[v, 2 * p : 2 * p + 2, :], pair)
-            sub = iota((16, 128), 0)
-            w = t[2] * coef
+    mid = provisional(s, me, cb, oz, ocx, grid, prov)
+    own_av.wait()
+    for c in early:
+        c.wait()
+
+    def turn(i, _):
+        for p in range(2):
+            gy = nbr[4, 2 * i + p]
             for h in range(2):
-                xh = xm[:, 128 * h : 128 * h + 128]
-                fix = t[h] + jnp.where(sub == 0, xh[0:1], jnp.where(sub == 15, xh[1:2], 0.0))
-                av[:, h, p, v, :] = pltpu.roll(avs[p, v, h] - 0.0125 * fix, turn_a, 1)
-                yr[h] = jnp.where((l16 >= 25 * v) & (l16 < 25 * v + 25), moved(w, 25 * v - 64 * h), yr[h])
-                zr[h] = jnp.where(l16 // 16 == 4 - v, moved(w, 16 * (4 - v) - 64 * h - 32), zr[h])
-        for h in range(2):
-            av[:, h, p, 5, :] = pltpu.roll(yr[h], turn_y, 1)
-            av[:, h, p, 6, :] = pltpu.roll(zr[h], turn_z, 1)
-            av[:, h, p, 7, :] = jnp.zeros((16, 128), F32)
-    one = []
-    for d in range(1, NP):
-        one.append(copy(S_A + d - 1, av.at[peer[d]], bb.at[me], (s, peer[d])))
-        one[-1].start()
-    own = pltpu.make_async_copy(av.at[me], bb.at[me], ls.at[6])
-    own.start()
-    for p in range(2):
-        for v in range(5):
-            a = 160 * p + 32 * v
-            fs[v, p] = fs[v, p] - 0.1 * dot3(bf[a : a + 32, :], expand)
-            for way, x in ((0, 0), (1, 31)):
-                fs[v, p, x : x + 1, :] = fs[v, p, x : x + 1, :] - 0.1 * xg[v, 2 * p + way : 2 * p + way + 1, :]
+                tt[i, p, h] = pltpu.roll(bb[i, p, h] + cc[NP * p + i, h], (16 * gy + 32) & 127, 1)
+        return 0
+
+    lax.fori_loop(0, NP, turn, 0, unroll=2)
     lane = iota((8, 128), 1)
     sub = iota((8, 128), 0)
     block = lane // 16
     ring = (block + sub) & 7
     slope = lane + sub - 7
-    own.wait()
-    for c in one:
-        c.wait()
-
     def expand_to(j):
         h = lax.rem(j, 2)
         r = j // 2
@@ -533,13 +524,16 @@
         accy = [jnp.zeros((8, 128), F32)] * 5
         accz = jnp.zeros((8, 128), F32)
         covered = jnp.zeros((8, 128), F32)
+        side = [jnp.zeros((8, 128), F32)] * 2
         for gy in range(6):
             a = grid[0, gy + 8 * (r - 1) + GOFF]
             b = grid[0, gy + 8 * far + GOFF]
             a0 = jnp.maximum(a, 0)
             b0 = jnp.maximum(b, 0)
-            t = bb[a0 // 2, h, a0 & 1]
-            zt = bb[b0 // 2, h, b0 & 1, 6:7, :]
+            t = tt[a0 // 2, a0 & 1, h]
+            zt = tt[b0 // 2, b0 & 1, h, 6:7, :]
+            for way in range(2):
+                side[way] = jnp.where((block == gy + 1) & (a >= 0), xt[NP * way + a0 // 2, a0 & 1], side[way])
             covered = jnp.where((block == gy + 1) & (a >= 0), 1.0, covered)
             ina = (ring == gy + 1) & (a >= 0)
             accz = jnp.where((ring == gy + 1) & (b >= 0), zt, accz)
@@ -553,6 +547,8 @@
             add = moved(pltpu.roll(accy[v], 0, 1, stride=1, stride_axis=0), 8 - 25 * v)
             add = add + jnp.where(sub == 7 * h, accz[v : v + 1], 0.0)
             ee[j, v] = jnp.where(covered > 0, val, add)
+        ee[j, 5] = side[0]
+        ee[j, 6] = side[1]
 
     def expanded(d):
         j = lax.rem(me + d, NP)
@@ -565,15 +561,42 @@
 
     lax.fori_loop(1, NP, expand_send, 0)
     expand_to(me)
-    own = pltpu.make_async_copy(ee.at[me], oe.at[me], ls.at[6])
-    own.start()
-    mid = provisional(s, me, cb, oz, ocx, grid, prov)
+    own_ee = pltpu.make_async_copy(ee.at[me], oe.at[me], ls.at[7])
+    own_ee.start()
+
+    src = iota((128, 1024), 0)
+    dst = iota((128, 1024), 1)
+    g = src // 32
+    i = lax.rem(src, 32)
+    at = jnp.where(g == 0, 32 * i, jnp.where(g == 1, 32 * i + 31, jnp.where(g == 2, i, 992 + i)))
+    sign = jnp.where((g & 1) == 0, -1.0, 1.0)
+    expand = jnp.where(dst == at, sign, 0.0).astype(BF16)
     own.wait()
+    for c in late:
+        c.wait()
+    l5 = iota((5, 128), 1)
+    for way in range(2):
+        for j in range(8):
+            e = og[2 * j, way, 10:15, :]
+            o = og[2 * j + 1, way, 10:15, :]
+            cut = slice(128 * j, 128 * j + 128)
+            xg[:, way, cut] = jnp.where(l5 < 64, e, pltpu.roll(o, 64, 1))
+            xg[:, 2 + way, cut] = jnp.where(l5 < 64, pltpu.roll(e, 64, 1), o)
+    for p in range(2):
+        for v in range(5):
+            for xr in range(2):
+                bf[pl.ds(xr, 16, 2), :] = og[:, p, 5 * xr + v, :]
+            fs[v, p] = fs[v, p] - 0.1 * dot3(bf[...], expand)
+            for way, x in ((0, 0), (1, 31)):
+                fs[v, p, x : x + 1, :] = fs[v, p, x : x + 1, :] - 0.1 * xg[v, 2 * p + way : 2 * p + way + 1, :]
+    own_ee.wait()
     for d in range(1, NP):
         expanded(d).wait()
     for x in range(16):
         for v in range(5):
             e = oe[x, v]
+            if x in (0, 15):
+                e = e + oe[pl.ds(8 * half, 8), 5 + x // 15, v, :]
             prov[v, x] = jnp.where(mid > 0, e, prov[v, x] + e)
 
 
@@ -626,28 +649,28 @@
             pltpu.SMEM((1, 96), I32),
             buf(5, 2, 32, 1024),
             buf(5, 16, 8, 128),
-            buf(16, 2, 16, 128),
+            buf(16, 3, 16, 128),
             buf(2, 16, 8, 128),
             buf(2, 5, 16, 128),
             buf(8, 80, 128),
-            buf(2, 5, 32, 128),
-            buf(32, 16, 128),
+            buf(32, 128),
+            buf(16, 3, 16, 128),
             buf(2, 16, 8, 128),
             buf(32, 8, 128),
             buf(16, 2, 16, 128),
             buf(16, 2, 16, 128),
             buf(2, 5, 16, 128),
             buf(2, 5, 8, 128),
-            buf(5, 32, 128),
-            buf(320, 128),
+            buf(32, 128),
             buf(5, 4, 1024),
-            buf(5, 4, 1024),
-            buf(2, 5, 2, 16, 128),
             buf(16, 2, 2, 8, 128),
             buf(16, 2, 2, 8, 128),
-            buf(16, 5, 8, 128),
-            buf(16, 5, 8, 128),
-            buf(3, 320, 128),
+            buf(32, 2, 8, 128),
+            buf(32, 2, 8, 128),
+            buf(16, 2, 2, 8, 128),
+            buf(16, 7, 8, 128),
+            buf(16, 7, 8, 128),
+            buf(2, 32, 128),
             buf(5, 32, 1024),
             pltpu.SemaphoreType.DMA((N_SEM,)),
             pltpu.SemaphoreType.DMA((N_SEM,)),

time: 43.2 us -> 36.2 us (0.84)
  the two profiles are of different devices: /device:TPU:16 before, /device:TPU:9 now
where the time goes in v6:
time: 36.2 us; the launch traced here: 36.1 us
  Pallas kernels  35.4 us (98%)
  between operations  0.64 us (2%)
    pallas_call x1, Pallas kernels, local(): pl.pallas_call(step_kernel, out_shape=(sds(5, 2, 32, 1024), sds(5, 16, 8,...  34.1 us
    pallas_call x1, Pallas kernels, local(): pl.pallas_call(copy_kernel, out_shape=(sds(5, 16, 8, 128), sds(5, 2, 32,...  1.28 us

profile of v6, /device:TPU:9, one launch (start us, length us, event | category | flops | bytes accessed | tf_op | source)
XLA Modules:
  0.0 36.1 jit_solution(12442796797536761803)
XLA Ops:
  0.6 34.1 %step.1 = (f32[5,2,32,1024]{3,2,1,0:T(8,128)S(1)}, f32[5,16,8,128]{3,2,1,0:T(8,128)S(1)}) custom-call(f32[5,2,32,1024]{3,2,1,0:T(8,128)} %fine.1, f32[5,16,8,128]{3,2,1,0:T(8,128)} %coarse.1, s32[1,32]{1,0:T(1,128)} %ids_in.1, s32[2,32]{1,0:T(2,128)} %bitcast.1), custom_call_target="tpu_custom_call" | custom-call | tf_op jit(solution)/shard_map/step/pallas_call | solution.py:640
  34.8 1.3 %copy_out.1 = (f32[5,16,8,128]{3,2,1,0:T(8,128)}, f32[5,2,32,1024]{3,2,1,0:T(8,128)}) custom-call(f32[5,16,8,128]{3,2,1,0:T(8,128)S(1)} %get-tuple-element.4.a, f32[5,2,32,1024]{3,2,1,0:T(8,128)S(1)} %get-tuple-element.5.b), custom_call_target="tpu_custom_call" | custom-call | tf_op jit(solution)/shard_map/copy_out/pallas_call | solution.py:682

commit v7 on v6

--- a/solution.py
+++ b/solution.py
@@ -136,13 +136,14 @@
 S_G = S_H + 4
 S_A = S_G + N1
 S_E = S_A + N1
-N_SEM = S_E + N1
+S_S = S_E + N1
+N_SEM = S_S + N1
 
 
 def step_kernel(
     fine, coarse, ids_in, cols_in, fs, prov,
     ids, cols, nbr, grid, fb, cb, a1, x1, rz, ct, pk, ba, bx, cg, dd, og, oz, ocx,
-    bf, xg, av, bb, cc, xt, tt, ee, oe, big, chg, ss, rs, ls,
+    bf, xg, av, bb, cc, xt, tt, ee, oe, se, so, big, chg, ss, rs, ls,
 ):
     s = lax.axis_index("slab")
     me = lax.axis_index("patch")
@@ -180,7 +181,7 @@
         for p in range(2):
             pk[...] = dot3(fb[v, p], sel)
             for xr in range(2):
-                a1[:, p, 5 * xr + v, :] = pk[pl.ds(xr, 16, 2), :]
+                a1[:, 16 * p + 5 * xr + v, :] = pk[pl.ds(xr, 16, 2), :]
     loads[6].wait()
     loads[7].wait()
     lane = iota((5, 128), 1)
@@ -194,7 +195,12 @@
                 (1, jnp.where(lane < 64, pltpu.roll(t0, 64, 1), t1)),
             ):
                 x1[d, 2 * j + o, 0:5, :] = t
-                a1[2 * j + o, 2, 8 * d : 8 * d + 5, :] = t
+                if d == 0:
+                    a1[2 * j + o, 32:37, :] = t
+                else:
+                    a1[2 * j + o, 37:40, :] = t[0:3]
+                    a1[2 * j + o, 15:16, :] = t[3:4]
+                    a1[2 * j + o, 31:32, :] = t[4:5]
             x1[d, 2 * j, 5:8, :] = tag
             x1[d, 2 * j + 1, 5:8, :] = tag
     loads[5].wait()
@@ -214,12 +220,10 @@
     own = jnp.where(half == 0, first, last)
     for v in range(5):
         cut = slice(16 * v, 16 * v + 16)
-        a1[:, 0, 10 + v, :] = acc[cut]
-        a1[:, 1, 10 + v, :] = own[cut]
+        a1[:, 10 + v, :] = acc[cut]
+        a1[:, 26 + v, :] = own[cut]
         rz[0, v] = first[cut]
         rz[1, v] = last[cut]
-    a1[:, 0, 15, :] = jnp.zeros((16, 128), F32)
-    a1[:, 1, 15, :] = jnp.zeros((16, 128), F32)
 
     pl.semaphore_wait(barrier, 3 * NP - 1)
     one = []
@@ -298,10 +302,9 @@
             m = dot3(fs[v, p], pair)
             for h in range(2):
                 big[h, 0:32, :] = m[:, 128 * h : 128 * h + 128]
-                av[:, p, h, v, :] = 0.125 * (big[h, pl.ds(0, 16, 2), :] + big[h, pl.ds(1, 16, 2), :])
-        for h in range(2):
-            for v in range(5, 8):
-                av[:, p, h, v, :] = jnp.zeros((16, 128), F32)
+                av[:, 10 * p + 5 * h + v, :] = 0.125 * (big[h, pl.ds(0, 16, 2), :] + big[h, pl.ds(1, 16, 2), :])
+        for k in range(2):
+            av[:, 20 + 2 * p + k, :] = jnp.zeros((16, 128), F32)
 
     interior(0)
     interior(1)
@@ -354,17 +357,17 @@
             gy = nbr[4, 2 * j + p]
             gz = nbr[5, 2 * j + p]
             a = 2 * (gz + 1)
-            r0 = pltpu.roll(ba[a, 0, 8:16, :], (128 - 8 * gy) & 127, 1)
-            r1 = pltpu.roll(ba[a + 1, 0, 8:16, :], (136 - 8 * gy) & 127, 1)
-            r2 = pltpu.roll(ba[2 * gz + 1, 1, 8:16, :], (176 - 16 * gy) & 127, 1)
-            r3 = pltpu.roll(ba[2 * gz + 4, 1, 8:16, :], (192 - 16 * gy) & 127, 1)
+            r0 = pltpu.roll(ba[a, 8:16, :], (128 - 8 * gy) & 127, 1)
+            r1 = pltpu.roll(ba[a + 1, 8:16, :], (136 - 8 * gy) & 127, 1)
+            r2 = pltpu.roll(ba[2 * gz + 1, 24:32, :], (176 - 16 * gy) & 127, 1)
+            r3 = pltpu.roll(ba[2 * gz + 4, 24:32, :], (192 - 16 * gy) & 127, 1)
             cg[NP * p + j] = jnp.where(lane < 64, jnp.where((lane & 8) == 0, r0, r1), jnp.where(lane < 80, r2, r3))
         return 0
 
     lax.fori_loop(0, NP, place_coarse, 0, unroll=2)
     cg[...] = dot3(cg[...].reshape(256, 128), spread).reshape(32, 8, 128)
     packs = [
-        jnp.concatenate([ba[:, 0, k, :], ba[:, 1, k, :]], axis=0) for k in range(10)
+        jnp.concatenate([ba[:, k, :], ba[:, 16 + k, :]], axis=0) for k in range(10)
     ]
     data = jnp.concatenate(packs, axis=1)
     group = iota((32, 128), 1) // 32
@@ -413,6 +416,7 @@
     sums = jnp.concatenate([f[v][0:32] + f[v][32:64] for v in range(5)], axis=0)
     l16 = iota((16, 128), 1)
     diagonal = l16 == iota((16, 128), 0)
+    own_x = [32 + k for k in range(8)] + [15, 31]
     sides = []
     for way in range(2):
         tag = bx[way, :, 5, :]
@@ -429,9 +433,9 @@
             a = g0[0:16] + pltpu.roll(g1[0:16], 64, 1)
             b = pltpu.roll(g0[16:32], 64, 1) + g1[16:32]
             t = jnp.where(l16 < 64, a, b)
-            theirs.append(jnp.where(s == (0 if way == 0 else NS - 1), ba[:, 2, 8 * way + v, :], t))
+            theirs.append(jnp.where(s == (0 if way == 0 else NS - 1), ba[:, own_x[5 * way + v], :], t))
         sides.append(theirs)
-    mine = [jnp.concatenate([ba[:, 2, v, :], ba[:, 2, 8 + v, :]], axis=0) for v in range(5)]
+    mine = [jnp.concatenate([ba[:, own_x[v], :], ba[:, own_x[5 + v], :]], axis=0) for v in range(5)]
     theirs = [jnp.concatenate([sides[0][v], sides[1][v]], axis=0) for v in range(5)]
     low = iota((32, 128), 0) < 16
     ql = [jnp.where(low, theirs[v], mine[v]) for v in range(5)]
@@ -507,7 +511,9 @@
         for p in range(2):
             gy = nbr[4, 2 * i + p]
             for h in range(2):
-                tt[i, p, h] = pltpu.roll(bb[i, p, h] + cc[NP * p + i, h], (16 * gy + 32) & 127, 1)
+                k = 10 * p + 5 * h
+                t = jnp.concatenate([bb[i, k : k + 5, :], jnp.zeros((3, 128), F32)], axis=0)
+                tt[i, p, h] = pltpu.roll(t + cc[NP * p + i, h], (16 * gy + 32) & 127, 1)
         return 0
 
     lax.fori_loop(0, NP, turn, 0, unroll=2)
@@ -547,22 +553,57 @@
             add = moved(pltpu.roll(accy[v], 0, 1, stride=1, stride_axis=0), 8 - 25 * v)
             add = add + jnp.where(sub == 7 * h, accz[v : v + 1], 0.0)
             ee[j, v] = jnp.where(covered > 0, val, add)
-        ee[j, 5] = side[0]
-        ee[j, 6] = side[1]
+        se[j, 0] = side[0]
+        se[j, 1] = side[1]
 
     def expanded(d):
         j = lax.rem(me + d, NP)
         return copy(S_E + d - 1, ee.at[j], oe.at[me], (s, j))
 
+    def sided(d):
+        j = lax.rem(me + d, NP)
+        return copy(S_S + d - 1, se.at[j], so.at[lax.rem(me, 8)], (s, j))
+
+    def takes(j):
+        return (j > 0) & (j < NP - 1)
+
+    def takes_side(j, m):
+        return (j > 1) & (j < NP - 2) & (lax.rem(j, 2) == m // 8)
+
     def expand_send(d, _):
-        expand_to(lax.rem(me + d, NP))
-        expanded(d).start()
+        j = lax.rem(me + d, NP)
+        expand_to(j)
+
+        @pl.when(takes(j))
+        def _():
+            expanded(d).start()
+
+        @pl.when(takes_side(j, me))
+        def _():
+            sided(d).start()
+
         return 0
 
     lax.fori_loop(1, NP, expand_send, 0)
     expand_to(me)
     own_ee = pltpu.make_async_copy(ee.at[me], oe.at[me], ls.at[7])
-    own_ee.start()
+    own_se = pltpu.make_async_copy(se.at[me], so.at[lax.rem(me, 8)], ls.at[0])
+
+    @pl.when(takes(me))
+    def _():
+        own_ee.start()
+
+    @pl.when(takes_side(me, me))
+    def _():
+        own_se.start()
+
+    @pl.when(jnp.logical_not(takes(me)))
+    def _():
+        oe[...] = jnp.zeros((16, 5, 8, 128), F32)
+
+    @pl.when((me < 2) | (me >= NP - 2))
+    def _():
+        so[...] = jnp.zeros((8, 2, 8, 128), F32)
 
     src = iota((128, 1024), 0)
     dst = iota((128, 1024), 1)
@@ -589,14 +630,35 @@
             fs[v, p] = fs[v, p] - 0.1 * dot3(bf[...], expand)
             for way, x in ((0, 0), (1, 31)):
                 fs[v, p, x : x + 1, :] = fs[v, p, x : x + 1, :] - 0.1 * xg[v, 2 * p + way : 2 * p + way + 1, :]
-    own_ee.wait()
+
+    @pl.when(takes(me))
+    def _():
+        own_ee.wait()
+        for d in range(1, NP):
+            expanded(d).wait_recv()
+
+    @pl.when(takes_side(me, me))
+    def _():
+        own_se.wait()
+
     for d in range(1, NP):
-        expanded(d).wait()
+        @pl.when(takes(peer[d]))
+        def _():
+            expanded(d).wait_send()
+
+        @pl.when(takes_side(peer[d], me))
+        def _():
+            sided(d).wait_send()
+
+        @pl.when(takes_side(me, peer[NP - d]))
+        def _():
+            sided(d).wait_recv()
+
     for x in range(16):
         for v in range(5):
             e = oe[x, v]
             if x in (0, 15):
-                e = e + oe[pl.ds(8 * half, 8), 5 + x // 15, v, :]
+                e = e + so[:, x // 15, v, :]
             prov[v, x] = jnp.where(mid > 0, e, prov[v, x] + e)
 
 
@@ -649,12 +711,12 @@
             pltpu.SMEM((1, 96), I32),
             buf(5, 2, 32, 1024),
             buf(5, 16, 8, 128),
-            buf(16, 3, 16, 128),
+            buf(16, 40, 128),
             buf(2, 16, 8, 128),
             buf(2, 5, 16, 128),
             buf(8, 80, 128),
             buf(32, 128),
-            buf(16, 3, 16, 128),
+            buf(16, 40, 128),
             buf(2, 16, 8, 128),
             buf(32, 8, 128),
             buf(16, 2, 16, 128),
@@ -663,13 +725,15 @@
             buf(2, 5, 8, 128),
             buf(32, 128),
             buf(5, 4, 1024),
-            buf(16, 2, 2, 8, 128),
-            buf(16, 2, 2, 8, 128),
+            buf(16, 24, 128),
+            buf(16, 24, 128),
             buf(32, 2, 8, 128),
             buf(32, 2, 8, 128),
             buf(16, 2, 2, 8, 128),
-            buf(16, 7, 8, 128),
-            buf(16, 7, 8, 128),
+            buf(16, 5, 8, 128),
+            buf(16, 5, 8, 128),
+            buf(16, 2, 8, 128),
+            buf(8, 2, 8, 128),
             buf(2, 32, 128),
             buf(5, 32, 1024),
             pltpu.SemaphoreType.DMA((N_SEM,)),

time: 36.2 us -> 34 us (0.939)
  the two profiles are of different devices: /device:TPU:9 before, /device:TPU:2 now
where the time goes in v7:
time: 34 us; the launch traced here: 33.8 us
  Pallas kernels  33.2 us (98%)
  between operations  0.64 us (2%)
    pallas_call x1, Pallas kernels, local(): pl.pallas_call(step_kernel, out_shape=(sds(5, 2, 32, 1024), sds(5, 16, 8,...  31.9 us
    pallas_call x1, Pallas kernels, local(): pl.pallas_call(copy_kernel, out_shape=(sds(5, 16, 8, 128), sds(5, 2, 32,...  1.28 us

profile of v7, /device:TPU:2, one launch (start us, length us, event | category | flops | bytes accessed | tf_op | source)
XLA Modules:
  0.0 33.8 jit_solution(8039329638428308532)
XLA Ops:
  0.6 31.9 %step.1 = (f32[5,2,32,1024]{3,2,1,0:T(8,128)S(1)}, f32[5,16,8,128]{3,2,1,0:T(8,128)S(1)}) custom-call(f32[5,2,32,1024]{3,2,1,0:T(8,128)} %fine.1, f32[5,16,8,128]{3,2,1,0:T(8,128)} %coarse.1, s32[1,32]{1,0:T(1,128)} %ids_in.1, s32[2,32]{1,0:T(2,128)} %bitcast.1), custom_call_target="tpu_custom_call" | custom-call | tf_op jit(solution)/shard_map/step/pallas_call | solution.py:702
  32.5 1.3 %copy_out.1 = (f32[5,16,8,128]{3,2,1,0:T(8,128)}, f32[5,2,32,1024]{3,2,1,0:T(8,128)}) custom-call(f32[5,16,8,128]{3,2,1,0:T(8,128)S(1)} %get-tuple-element.4.a, f32[5,2,32,1024]{3,2,1,0:T(8,128)S(1)} %get-tuple-element.5.b), custom_call_target="tpu_custom_call" | custom-call | tf_op jit(solution)/shard_map/copy_out/pallas_call | solution.py:746

commit v8 on v7

--- a/solution.py
+++ b/solution.py
@@ -131,6 +131,10 @@
 
 
 N1 = NP - 1
+OFFSETS = sorted(
+    ((dx, dz) for dx in range(4) for dz in range(4)),
+    key=lambda o: (o != (0, 0), -(min(o[0], 4 - o[0]) + min(o[1], 4 - o[1]))),
+)
 S_X = N1
 S_H = S_X + 2 * NP
 S_G = S_H + 4
@@ -150,7 +154,9 @@
     half = lax.rem(me, 2)
     up = lax.rem(s + 1, NS)
     down = lax.rem(s + NS - 1, NS)
-    peer = [lax.rem(me + d, NP) for d in range(NP)]
+    x, z = me // 4, lax.rem(me, 4)
+    peer = [lax.rem(x + dx, 4) * 4 + lax.rem(z + dz, 4) for dx, dz in OFFSETS]
+    source = [lax.rem(x + 4 - dx, 4) * 4 + lax.rem(z + 4 - dz, 4) for dx, dz in OFFSETS]
     loads = [pltpu.make_async_copy(fine.at[v], fb.at[v], ls.at[v]) for v in range(5)]
     loads.append(pltpu.make_async_copy(coarse, cb, ls.at[5]))
     loads.append(pltpu.make_async_copy(ids_in, ids, ls.at[6]))
@@ -228,7 +234,7 @@
     pl.semaphore_wait(barrier, 3 * NP - 1)
     one = []
     two = []
-    for d in range(NP):
+    for d in [*range(1, NP), 0]:
         j = peer[d]
         if d:
             one.append(copy(d - 1, a1.at[j], ba.at[me], (s, j)))
@@ -242,24 +248,14 @@
     two = [
         copy(S_H, cb.at[:, 0], ocx.at[1], (down, me)),
         copy(S_H + 1, cb.at[:, 15], ocx.at[0], (up, me)),
-        copy(S_H + 2, rz.at[1], oz.at[0], (s, peer[1])),
-        copy(S_H + 3, rz.at[0], oz.at[1], (s, peer[N1])),
+        copy(S_H + 2, rz.at[1], oz.at[0], (s, lax.rem(me + 1, NP))),
+        copy(S_H + 3, rz.at[0], oz.at[1], (s, lax.rem(me + N1, NP))),
     ]
     for c in two:
         c.start()
     own = pltpu.make_async_copy(a1.at[me], ba.at[me], ls.at[6])
     own.start()
 
-    def place(t, _):
-        n = ids[0, t]
-        gy = cols[0, n]
-        gz = cols[1, n]
-        nbr[4, t] = gy
-        nbr[5, t] = gz
-        nbr[6, t] = gy + 8 * gz + GOFF
-        return 0
-
-    lax.fori_loop(0, 32, place, 0)
     src = iota((1024, 256), 0)
     dst = iota((1024, 256), 1)
     zz = 8 * (dst // 128) + 7 - lax.rem(dst, 128) // 16
@@ -314,6 +310,16 @@
         early[-1].start()
     own_av = pltpu.make_async_copy(av.at[me], bb.at[me], ls.at[7])
     own_av.start()
+    def place(t, _):
+        n = ids[0, t]
+        gy = cols[0, n]
+        gz = cols[1, n]
+        nbr[4, t] = gy
+        nbr[5, t] = gz
+        nbr[6, t] = gy + 8 * gz + GOFF
+        return 0
+
+    lax.fori_loop(0, 32, place, 0)
     for i in range(GOFF):
         grid[0, i] = jnp.int32(-1)
 
@@ -364,7 +370,7 @@
             cg[NP * p + j] = jnp.where(lane < 64, jnp.where((lane & 8) == 0, r0, r1), jnp.where(lane < 80, r2, r3))
         return 0
 
-    lax.fori_loop(0, NP, place_coarse, 0, unroll=2)
+    lax.fori_loop(0, NP, place_coarse, 0, unroll=4)
     cg[...] = dot3(cg[...].reshape(256, 128), spread).reshape(32, 8, 128)
     packs = [
         jnp.concatenate([ba[:, k, :], ba[:, 16 + k, :]], axis=0) for k in range(10)
@@ -516,7 +522,7 @@
                 tt[i, p, h] = pltpu.roll(t + cc[NP * p + i, h], (16 * gy + 32) & 127, 1)
         return 0
 
-    lax.fori_loop(0, NP, turn, 0, unroll=2)
+    lax.fori_loop(0, NP, turn, 0, unroll=4)
     lane = iota((8, 128), 1)
     sub = iota((8, 128), 0)
     block = lane // 16
@@ -557,12 +563,10 @@
         se[j, 1] = side[1]
 
     def expanded(d):
-        j = lax.rem(me + d, NP)
-        return copy(S_E + d - 1, ee.at[j], oe.at[me], (s, j))
+        return copy(S_E + d - 1, ee.at[peer[d]], oe.at[me], (s, peer[d]))
 
     def sided(d):
-        j = lax.rem(me + d, NP)
-        return copy(S_S + d - 1, se.at[j], so.at[lax.rem(me, 8)], (s, j))
+        return copy(S_S + d - 1, se.at[peer[d]], so.at[lax.rem(me, 8)], (s, peer[d]))
 
     def takes(j):
         return (j > 0) & (j < NP - 1)
@@ -570,22 +574,22 @@
     def takes_side(j, m):
         return (j > 1) & (j < NP - 2) & (lax.rem(j, 2) == m // 8)
 
-    def expand_send(d, _):
-        j = lax.rem(me + d, NP)
-        expand_to(j)
-
-        @pl.when(takes(j))
-        def _():
-            expanded(d).start()
-
-        @pl.when(takes_side(j, me))
-        def _():
-            sided(d).start()
-
-        return 0
-
-    lax.fori_loop(1, NP, expand_send, 0)
-    expand_to(me)
+    order = [*range(1, NP), 0]
+    for b in range(0, NP, 4):
+        for d in order[b : b + 4]:
+            expand_to(peer[d])
+        for d in order[b : b + 4]:
+            if d == 0:
+                continue
+
+            @pl.when(takes(peer[d]))
+            def _():
+                expanded(d).start()
+
+            @pl.when(takes_side(peer[d], me))
+            def _():
+                sided(d).start()
+
     own_ee = pltpu.make_async_copy(ee.at[me], oe.at[me], ls.at[7])
     own_se = pltpu.make_async_copy(se.at[me], so.at[lax.rem(me, 8)], ls.at[0])
 
@@ -650,7 +654,7 @@
         def _():
             sided(d).wait_send()
 
-        @pl.when(takes_side(me, peer[NP - d]))
+        @pl.when(takes_side(me, source[d]))
         def _():
             sided(d).wait_recv()
 

time: 34 us -> 32.5 us (0.956)
  Pallas kernels: 33.2 us -> 31.6 us
    pallas_call x1, Pallas kernels: 31.9 us -> 30.4 us  [local(): pl.pallas_call(step_kernel, out_shape=(sds(5, 2, 32, 1024), sds(5, 16, 8,...]
where the time goes in v8:
time: 32.5 us; the launch traced here: 32.3 us
  Pallas kernels  31.6 us (97%)
  between operations  0.64 us (2%)
    pallas_call x1, Pallas kernels, local(): pl.pallas_call(step_kernel, out_shape=(sds(5, 2, 32, 1024), sds(5, 16, 8,...  30.4 us
    pallas_call x1, Pallas kernels, local(): pl.pallas_call(copy_kernel, out_shape=(sds(5, 16, 8, 128), sds(5, 2, 32,...  1.28 us

profile of v8, /device:TPU:2, one launch (start us, length us, event | category | flops | bytes accessed | tf_op | source)
XLA Modules:
  0.0 32.3 jit_solution(17564169951757026013)
XLA Ops:
  0.6 30.4 %step.1 = (f32[5,2,32,1024]{3,2,1,0:T(8,128)S(1)}, f32[5,16,8,128]{3,2,1,0:T(8,128)S(1)}) custom-call(f32[5,2,32,1024]{3,2,1,0:T(8,128)} %fine.1, f32[5,16,8,128]{3,2,1,0:T(8,128)} %coarse.1, s32[1,32]{1,0:T(1,128)} %ids_in.1, s32[2,32]{1,0:T(2,128)} %bitcast.1), custom_call_target="tpu_custom_call" | custom-call | tf_op jit(solution)/shard_map/step/pallas_call | solution.py:706
  31.0 1.3 %copy_out.1 = (f32[5,16,8,128]{3,2,1,0:T(8,128)}, f32[5,2,32,1024]{3,2,1,0:T(8,128)}) custom-call(f32[5,16,8,128]{3,2,1,0:T(8,128)S(1)} %get-tuple-element.4.a, f32[5,2,32,1024]{3,2,1,0:T(8,128)S(1)} %get-tuple-element.5.b), custom_call_target="tpu_custom_call" | custom-call | tf_op jit(solution)/shard_map/copy_out/pallas_call | solution.py:750

commit v9 on v8

--- a/solution.py
+++ b/solution.py
@@ -23,8 +23,9 @@
     r = x - hi.astype(F32)
     mid = r.astype(BF16)
     lo = (r - mid.astype(F32)).astype(BF16)
-    d = lambda a: jnp.dot(a, m, preferred_element_type=F32)
-    return d(hi) + (d(mid) + d(lo))
+    n = x.shape[0]
+    y = jnp.dot(jnp.concatenate([hi, mid, lo], axis=0), m, preferred_element_type=F32)
+    return y[0:n] + (y[n : 2 * n] + y[2 * n : 3 * n])
 
 
 def dot3_left(m, x):
@@ -184,10 +185,11 @@
     sel = ones_where(k == want)
     for v in range(5):
         loads[v].wait()
+    pk[...] = dot3(fb[...].reshape(320, 1024), sel)
+    for v in range(5):
         for p in range(2):
-            pk[...] = dot3(fb[v, p], sel)
             for xr in range(2):
-                a1[:, 16 * p + 5 * xr + v, :] = pk[pl.ds(xr, 16, 2), :]
+                a1[:, 16 * p + 5 * xr + v, :] = pk[pl.ds(64 * v + 32 * p + xr, 16, 2), :]
     loads[6].wait()
     loads[7].wait()
     lane = iota((5, 128), 1)
@@ -219,8 +221,9 @@
     sel = ones_where(y == plane)
     lane8 = lax.rem(iota((80, 128), 1), 8)
     acc = jnp.zeros((80, 128), F32)
+    planes = dot3(ct[...].reshape(640, 128), sel)
     for z in range(8):
-        acc = jnp.where(lane8 == z, dot3(ct[z], sel), acc)
+        acc = jnp.where(lane8 == z, planes[80 * z : 80 * z + 80], acc)
     first = ct[0]
     last = ct[7]
     own = jnp.where(half == 0, first, last)
@@ -294,11 +297,12 @@
             return 0
 
         lax.fori_loop(0, 4, rows, 0)
-        for v in range(5):
-            m = dot3(fs[v, p], pair)
-            for h in range(2):
-                big[h, 0:32, :] = m[:, 128 * h : 128 * h + 128]
-                av[:, 10 * p + 5 * h + v, :] = 0.125 * (big[h, pl.ds(0, 16, 2), :] + big[h, pl.ds(1, 16, 2), :])
+        m = dot3(fs[:, p].reshape(160, 1024), pair)
+        for h in range(2):
+            big[h] = m[:, 128 * h : 128 * h + 128]
+            for v in range(5):
+                a = 32 * v
+                av[:, 10 * p + 5 * h + v, :] = 0.125 * (big[h, pl.ds(a, 16, 2), :] + big[h, pl.ds(a + 1, 16, 2), :])
         for k in range(2):
             av[:, 20 + 2 * p + k, :] = jnp.zeros((16, 128), F32)
 
@@ -381,9 +385,10 @@
     absent = jnp.zeros((32, 128), F32)
     for g, step in enumerate((-1, 1, -8, 8)):
         hit = codes == code + step
-        near.append(dot3_left(ones_where(hit)[:, 0:32], data))
+        near.append(ones_where(hit)[:, 0:32])
         some = jnp.sum(jnp.where(hit, 1.0, 0.0), axis=1, keepdims=True)
         absent = jnp.where(group == g, 1.0 - some, absent)
+    near = dot3_left(jnp.concatenate(near, axis=0), data)
     theirs = []
     mine = []
     low = (group & 1) == 0
@@ -391,7 +396,7 @@
         both = []
         for xr in range(2):
             k = 128 * (5 * xr + v)
-            n = [t[:, k : k + 128] for t in near]
+            n = [near[32 * g : 32 * g + 32, k : k + 128] for g in range(4)]
             n = jnp.where(group == 0, n[0], jnp.where(group == 1, n[1], jnp.where(group == 2, n[2], n[3])))
             both.append(jnp.where(absent > 0.5, cg[:, 2 + v, :], n))
         theirs.append(jnp.concatenate(both, axis=0))
@@ -431,11 +436,12 @@
         for t in range(2):
             tt_ = pltpu.roll(tag, 64, 1) if t else tag
             row = jnp.sum(jnp.where(diagonal, tt_, 0.0), axis=0, keepdims=True)
-            got.append(dot3_left(ones_where(want == row)[:, 0:16], data))
+            got.append(ones_where(want == row)[:, 0:16])
+        got = dot3_left(jnp.concatenate(got, axis=0), data)
         theirs = []
         for v in range(5):
-            g0 = got[0][:, 128 * v : 128 * v + 128]
-            g1 = got[1][:, 128 * v : 128 * v + 128]
+            g0 = got[0:32, 128 * v : 128 * v + 128]
+            g1 = got[32:64, 128 * v : 128 * v + 128]
             a = g0[0:16] + pltpu.roll(g1[0:16], 64, 1)
             b = pltpu.roll(g0[16:32], 64, 1) + g1[16:32]
             t = jnp.where(l16 < 64, a, b)
@@ -630,8 +636,10 @@
     for p in range(2):
         for v in range(5):
             for xr in range(2):
-                bf[pl.ds(xr, 16, 2), :] = og[:, p, 5 * xr + v, :]
-            fs[v, p] = fs[v, p] - 0.1 * dot3(bf[...], expand)
+                bf[pl.ds(32 * v + xr, 16, 2), :] = og[:, p, 5 * xr + v, :]
+        m = dot3(bf[...], expand)
+        for v in range(5):
+            fs[v, p] = fs[v, p] - 0.1 * m[32 * v : 32 * v + 32]
             for way, x in ((0, 0), (1, 31)):
                 fs[v, p, x : x + 1, :] = fs[v, p, x : x + 1, :] - 0.1 * xg[v, 2 * p + way : 2 * p + way + 1, :]
 
@@ -719,7 +727,7 @@
             buf(2, 16, 8, 128),
             buf(2, 5, 16, 128),
             buf(8, 80, 128),
-            buf(32, 128),
+            buf(320, 128),
             buf(16, 40, 128),
             buf(2, 16, 8, 128),
             buf(32, 8, 128),
@@ -727,7 +735,7 @@
             buf(16, 2, 16, 128),
             buf(2, 5, 16, 128),
             buf(2, 5, 8, 128),
-            buf(32, 128),
+            buf(160, 128),
             buf(5, 4, 1024),
             buf(16, 24, 128),
             buf(16, 24, 128),
@@ -738,7 +746,7 @@
             buf(16, 5, 8, 128),
             buf(16, 2, 8, 128),
             buf(8, 2, 8, 128),
-            buf(2, 32, 128),
+            buf(2, 160, 128),
             buf(5, 32, 1024),
             pltpu.SemaphoreType.DMA((N_SEM,)),
             pltpu.SemaphoreType.DMA((N_SEM,)),

time: 32.5 us -> 31.2 us (0.960)
  Pallas kernels: 31.6 us -> 30.3 us
    pallas_call x1, Pallas kernels: 30.4 us -> 29 us  [local(): pl.pallas_call(step_kernel, out_shape=(sds(5, 2, 32, 1024), sds(5, 16, 8,...]
where the time goes in v9:
time: 31.2 us; the launch traced here: 31 us
  Pallas kernels  30.3 us (97%)
  between operations  0.64 us (2%)
    pallas_call x1, Pallas kernels, local(): pl.pallas_call(step_kernel, out_shape=(sds(5, 2, 32, 1024), sds(5, 16, 8,...  29 us
    pallas_call x1, Pallas kernels, local(): pl.pallas_call(copy_kernel, out_shape=(sds(5, 16, 8, 128), sds(5, 2, 32,...  1.28 us

profile of v9, /device:TPU:2, one launch (start us, length us, event | category | flops | bytes accessed | tf_op | source)
XLA Modules:
  0.0 31.0 jit_solution(993735548750533278)
XLA Ops:
  0.6 29.0 %step.1 = (f32[5,2,32,1024]{3,2,1,0:T(8,128)S(1)}, f32[5,16,8,128]{3,2,1,0:T(8,128)S(1)}) custom-call(f32[5,2,32,1024]{3,2,1,0:T(8,128)} %fine.1, f32[5,16,8,128]{3,2,1,0:T(8,128)} %coarse.1, s32[1,32]{1,0:T(1,128)} %ids_in.1, s32[2,32]{1,0:T(2,128)} %bitcast.1), custom_call_target="tpu_custom_call" | custom-call | tf_op jit(solution)/shard_map/step/pallas_call | solution.py:714
  29.7 1.3 %copy_out.1 = (f32[5,16,8,128]{3,2,1,0:T(8,128)}, f32[5,2,32,1024]{3,2,1,0:T(8,128)}) custom-call(f32[5,16,8,128]{3,2,1,0:T(8,128)S(1)} %get-tuple-element.4.a, f32[5,2,32,1024]{3,2,1,0:T(8,128)S(1)} %get-tuple-element.5.b), custom_call_target="tpu_custom_call" | custom-call | tf_op jit(solution)/shard_map/copy_out/pallas_call | solution.py:758

commit v10 on v9

--- a/solution.py
+++ b/solution.py
@@ -277,7 +277,7 @@
                 chg[v, :, cut] = t - pltpu.roll(t, 1, 0)
             return 0
 
-        lax.fori_loop(0, 8, along_x, 0)
+        lax.fori_loop(0, 8, along_x, 0, unroll=2)
 
         def rows(c, _):
             cut = pl.ds(pl.multiple_of(8 * c, 8), 8)

time: 31.2 us -> 31.2 us (level)
  no operation moved by 1% of the time
where the time goes in v10:
time: 31.2 us; the launch traced here: 31 us
  Pallas kernels  30.3 us (97%)
  between operations  0.64 us (2%)
    pallas_call x1, Pallas kernels, local(): pl.pallas_call(step_kernel, out_shape=(sds(5, 2, 32, 1024), sds(5, 16, 8,...  29.1 us
    pallas_call x1, Pallas kernels, local(): pl.pallas_call(copy_kernel, out_shape=(sds(5, 16, 8, 128), sds(5, 2, 32,...  1.28 us

profile of v10, /device:TPU:2, one launch (start us, length us, event | category | flops | bytes accessed | tf_op | source)
XLA Modules:
  0.0 31.0 jit_solution(18308216124933424385)
XLA Ops:
  0.6 29.1 %step.1 = (f32[5,2,32,1024]{3,2,1,0:T(8,128)S(1)}, f32[5,16,8,128]{3,2,1,0:T(8,128)S(1)}) custom-call(f32[5,2,32,1024]{3,2,1,0:T(8,128)} %fine.1, f32[5,16,8,128]{3,2,1,0:T(8,128)} %coarse.1, s32[1,32]{1,0:T(1,128)} %ids_in.1, s32[2,32]{1,0:T(2,128)} %bitcast.1), custom_call_target="tpu_custom_call" | custom-call | tf_op jit(solution)/shard_map/step/pallas_call | solution.py:714
  29.7 1.3 %copy_out.1 = (f32[5,16,8,128]{3,2,1,0:T(8,128)}, f32[5,2,32,1024]{3,2,1,0:T(8,128)}) custom-call(f32[5,16,8,128]{3,2,1,0:T(8,128)S(1)} %get-tuple-element.4.a, f32[5,2,32,1024]{3,2,1,0:T(8,128)S(1)} %get-tuple-element.5.b), custom_call_target="tpu_custom_call" | custom-call | tf_op jit(solution)/shard_map/copy_out/pallas_call | solution.py:758

commit v11 on v9

--- a/solution.py
+++ b/solution.py
@@ -512,9 +512,6 @@
             xt[:, p, v, :] = m[32 * v : 32 * v + 32]
         for v in range(5, 8):
             xt[:, p, v, :] = jnp.zeros((32, 128), F32)
-    for c in two:
-        c.wait()
-    mid = provisional(s, me, cb, oz, ocx, grid, prov)
     own_av.wait()
     for c in early:
         c.wait()
@@ -615,6 +612,9 @@
     def _():
         so[...] = jnp.zeros((8, 2, 8, 128), F32)
 
+    for c in two:
+        c.wait()
+    mid = provisional(s, me, cb, oz, ocx, grid, prov)
     src = iota((128, 1024), 0)
     dst = iota((128, 1024), 1)
     g = src // 32

time: 31.2 us -> 31.2 us (level); the launches traced: 31 us -> 30.6 us
  Pallas kernels: 30.3 us -> 29.9 us
    pallas_call x1, Pallas kernels: 29 us -> 28.7 us  [local(): pl.pallas_call(step_kernel, out_shape=(sds(5, 2, 32, 1024), sds(5, 16, 8,...]
where the time goes in v11:
time: 31.2 us; the launch traced here: 30.6 us
  Pallas kernels  29.9 us (96%)
  between operations  0.64 us (2%)
    pallas_call x1, Pallas kernels, local(): pl.pallas_call(step_kernel, out_shape=(sds(5, 2, 32, 1024), sds(5, 16, 8,...  28.7 us
    pallas_call x1, Pallas kernels, local(): pl.pallas_call(copy_kernel, out_shape=(sds(5, 16, 8, 128), sds(5, 2, 32,...  1.28 us

profile of v11, /device:TPU:2, one launch (start us, length us, event | category | flops | bytes accessed | tf_op | source)
XLA Modules:
  0.0 30.6 jit_solution(14590732574970385588)
XLA Ops:
  0.6 28.7 %step.1 = (f32[5,2,32,1024]{3,2,1,0:T(8,128)S(1)}, f32[5,16,8,128]{3,2,1,0:T(8,128)S(1)}) custom-call(f32[5,2,32,1024]{3,2,1,0:T(8,128)} %fine.1, f32[5,16,8,128]{3,2,1,0:T(8,128)} %coarse.1, s32[1,32]{1,0:T(1,128)} %ids_in.1, s32[2,32]{1,0:T(2,128)} %bitcast.1), custom_call_target="tpu_custom_call" | custom-call | tf_op jit(solution)/shard_map/step/pallas_call | solution.py:714
  29.3 1.3 %copy_out.1 = (f32[5,16,8,128]{3,2,1,0:T(8,128)}, f32[5,2,32,1024]{3,2,1,0:T(8,128)}) custom-call(f32[5,16,8,128]{3,2,1,0:T(8,128)S(1)} %get-tuple-element.4.a, f32[5,2,32,1024]{3,2,1,0:T(8,128)S(1)} %get-tuple-element.5.b), custom_call_target="tpu_custom_call" | custom-call | tf_op jit(solution)/shard_map/copy_out/pallas_call | solution.py:758

commit v12 on v11

--- a/solution.py
+++ b/solution.py
@@ -324,20 +324,6 @@
         return 0
 
     lax.fori_loop(0, 32, place, 0)
-    for i in range(GOFF):
-        grid[0, i] = jnp.int32(-1)
-
-    def find(k, _):
-        q = jnp.int32(-1)
-        for t in range(32):
-            q = jnp.where(nbr[6, t] == k, t, q)
-        grid[0, k] = q
-        return 0
-
-    lax.fori_loop(GOFF, GOFF + 48, find, 0)
-    for i in range(GOFF + 48, 96):
-        grid[0, i] = jnp.int32(-1)
-
     src = iota((128, 128), 0)
     dst = iota((128, 128), 1)
     g = dst // 32
@@ -468,6 +454,20 @@
         late[-1].start()
     own = pltpu.make_async_copy(dd.at[me], og.at[me], ls.at[6])
     own.start()
+
+    for i in range(GOFF):
+        grid[0, i] = jnp.int32(-1)
+
+    def find(k, _):
+        q = jnp.int32(-1)
+        for t in range(32):
+            q = jnp.where(nbr[6, t] == k, t, q)
+        grid[0, k] = q
+        return 0
+
+    lax.fori_loop(GOFF, GOFF + 48, find, 0)
+    for i in range(GOFF + 48, 96):
+        grid[0, i] = jnp.int32(-1)
 
     src = iota((128, 256), 0)
     dst = iota((128, 256), 1)

time: 31.2 us -> 30.9 us (level); the launches traced: 30.6 us -> 30.8 us
  no operation moved by 1% of the time
where the time goes in v12:
time: 30.9 us; the launch traced here: 30.8 us
  Pallas kernels  30.1 us (97%)
  between operations  0.64 us (2%)
    pallas_call x1, Pallas kernels, local(): pl.pallas_call(step_kernel, out_shape=(sds(5, 2, 32, 1024), sds(5, 16, 8,...  28.9 us
    pallas_call x1, Pallas kernels, local(): pl.pallas_call(copy_kernel, out_shape=(sds(5, 16, 8, 128), sds(5, 2, 32,...  1.28 us

profile of v12, /device:TPU:2, one launch (start us, length us, event | category | flops | bytes accessed | tf_op | source)
XLA Modules:
  0.0 30.8 jit_solution(14882905614600913625)
XLA Ops:
  0.6 28.9 %step.1 = (f32[5,2,32,1024]{3,2,1,0:T(8,128)S(1)}, f32[5,16,8,128]{3,2,1,0:T(8,128)S(1)}) custom-call(f32[5,2,32,1024]{3,2,1,0:T(8,128)} %fine.1, f32[5,16,8,128]{3,2,1,0:T(8,128)} %coarse.1, s32[1,32]{1,0:T(1,128)} %ids_in.1, s32[2,32]{1,0:T(2,128)} %bitcast.1), custom_call_target="tpu_custom_call" | custom-call | tf_op jit(solution)/shard_map/step/pallas_call | solution.py:714
  29.5 1.3 %copy_out.1 = (f32[5,16,8,128]{3,2,1,0:T(8,128)}, f32[5,2,32,1024]{3,2,1,0:T(8,128)}) custom-call(f32[5,16,8,128]{3,2,1,0:T(8,128)S(1)} %get-tuple-element.4.a, f32[5,2,32,1024]{3,2,1,0:T(8,128)S(1)} %get-tuple-element.5.b), custom_call_target="tpu_custom_call" | custom-call | tf_op jit(solution)/shard_map/copy_out/pallas_call | solution.py:758
